TPU v7x, 256 devices: a whole 4x4x8 slice. The times are simulated.
256 devices in a mesh: seq: 32 (over x, y, z_lo), chan: 8 (over z_hi, core).
Axes of the slice: x: 4, y: 4, z: 8 (z_hi: 4, z_lo: 2; z = z_hi * 2 + z_lo), core: 2. Of those that a mesh axis runs over, the one named last changes fastest.
Arguments:
- gate_feat: bfloat16 [8192, 4096], P('seq', 'chan'), may hold values from -30 to 30
- key_feat: bfloat16 [8192, 4096], P('seq', 'chan'), may hold values from -5 to 5
- value_feat: bfloat16 [8192, 4096], P('seq', 'chan'), may hold values from -5 to 5
- filter_taps: bfloat16 [8192, 4096], P('seq', 'chan'), may hold values from -0.0625 to 0.0625
- skip_bias: float32 [4096], P('chan'), may hold values from 0.5 to 1.5
- norm_gain: float32 [4096], P('chan'), may hold values from 0.25 to 1.75
- cotangent: bfloat16 [8192, 4096], P('seq', 'chan'), may hold values from -5 to 5
Outputs:
- normed_out: bfloat16 [8192, 4096], P('seq', 'chan')
- grad_gate: bfloat16 [8192, 4096], P('seq', 'chan')
- grad_key: bfloat16 [8192, 4096], P('seq', 'chan')
- grad_value: bfloat16 [8192, 4096], P('seq', 'chan')
- grad_filter: bfloat16 [8192, 4096], P('seq', 'chan')
- grad_bias: float32 [4096], P('chan')
All inputs are finite; a program needn't handle non-finite values.
Results may differ from a plain program's by a relative error of at most 0.015.
Values may be sent and summed in bfloat16 or wider, within the bound.
No kernel may reach another device: no remote copies, remote signals or barrier semaphores. Data moves between devices by JAX's collectives and lax.ppermute only.
A program may use at most 64 MiB of HBM per device.

v0:
```python
import math

import jax
import jax.numpy as jnp
from jax import lax
from jax.sharding import PartitionSpec as P

D = 4096


epsilon = 1e-05


def angle_table(first_idx, second_idx, full_count):
    product = first_idx[:, None] * second_idx[None, :] % full_count
    return product.astype(jnp.float32) * (2.0 * math.pi / full_count)


def einsum_high(pattern, first_op, second_op):
    return jnp.einsum(
        pattern,
        first_op,
        second_op,
        precision=lax.Precision.HIGHEST,
        preferred_element_type=jnp.float32,
    )


def complex_mix(pattern, first_re, first_im, second_re, second_im):
    real_out = einsum_high(pattern, first_re, second_re) - einsum_high(pattern, first_im, second_im)
    imag_out = einsum_high(pattern, first_re, second_im) + einsum_high(pattern, first_im, second_re)
    return (real_out, imag_out)


def indices(amount):
    return jnp.arange(amount, dtype=jnp.int32)


def token_forward(stacked):
    devices = lax.axis_size("seq")
    my_index = lax.axis_index("seq")
    tokens = stacked.shape[1]
    block_rows = tokens // devices
    freq_span = 2 * devices
    full_count = freq_span * tokens
    outer_angle = angle_table(indices(freq_span), indices(devices), freq_span)
    twist_angle = angle_table(
        indices(freq_span), my_index * block_rows + indices(block_rows), full_count
    )
    inner_angle = angle_table(indices(tokens), indices(tokens), tokens)

    def across(pieces):
        values = pieces.astype(jnp.float32)
        part_re = einsum_high("kd,sdjc->skjc", jnp.cos(outer_angle), values)
        part_im = einsum_high("kd,sdjc->skjc", -jnp.sin(outer_angle), values)
        twist_re = jnp.cos(twist_angle)[None, :, :, None]
        twist_im = -jnp.sin(twist_angle)[None, :, :, None]
        return (part_re * twist_re - part_im * twist_im, part_re * twist_im + part_im * twist_re)

    spread_re, spread_im = across(
        lax.all_to_all(stacked[:, None], "seq", split_axis=2, concat_axis=1, tiled=True)
    )
    pieces = (
        lax.all_to_all(
            spread_re.astype(jnp.bfloat16), "seq", split_axis=1, concat_axis=2, tiled=True
        ).astype(spread_re.dtype),
        lax.all_to_all(
            spread_im.astype(jnp.bfloat16), "seq", split_axis=1, concat_axis=2, tiled=True
        ).astype(spread_im.dtype),
    )
    return complex_mix(
        "qr,sarc->saqc", jnp.cos(inner_angle), -jnp.sin(inner_angle), pieces[0], pieces[1]
    )


def token_inverse(spec_re, spec_im):
    devices = lax.axis_size("seq")
    my_index = lax.axis_index("seq")
    tokens = spec_re.shape[2]
    freq_span = 2 * devices
    full_count = freq_span * tokens
    inner_angle = angle_table(indices(tokens), indices(tokens), tokens)
    back_re, back_im = complex_mix(
        "rq,saqc->sarc", jnp.cos(inner_angle), jnp.sin(inner_angle), spec_re, spec_im
    )
    twist_angle = angle_table(2 * my_index + indices(2), indices(tokens), full_count)
    twist_re = jnp.cos(twist_angle)[None, :, :, None]
    twist_im = jnp.sin(twist_angle)[None, :, :, None]
    turned_re = back_re * twist_re - back_im * twist_im
    turned_im = back_re * twist_im + back_im * twist_re
    outer_angle = angle_table(indices(devices), indices(freq_span), freq_span)

    def across(pieces):
        real_out = einsum_high("dk,skjc->sdjc", jnp.cos(outer_angle), pieces[0])
        real_out = real_out - einsum_high("dk,skjc->sdjc", jnp.sin(outer_angle), pieces[1])
        return (real_out / full_count).astype(jnp.bfloat16)

    gathered = across(
        (
            lax.all_to_all(
                turned_re.astype(jnp.bfloat16), "seq", split_axis=2, concat_axis=1, tiled=True
            ).astype(turned_re.dtype),
            lax.all_to_all(
                turned_im.astype(jnp.bfloat16), "seq", split_axis=2, concat_axis=1, tiled=True
            ).astype(turned_im.dtype),
        )
    )
    returned = lax.all_to_all(gathered, "seq", split_axis=1, concat_axis=2, tiled=True)
    return returned[:, 0]


def on_device(gate_feat, key_feat, value_feat, filter_taps, skip_bias, norm_gain, cotangent):
    mixed = (key_feat.astype(jnp.float32) * value_feat.astype(jnp.float32)).astype(jnp.bfloat16)
    mixed_wide = mixed.astype(jnp.float32)
    spec_re, spec_im = token_forward(jnp.stack([mixed, filter_taps]))
    mixed_re, filter_re = (spec_re[0], spec_re[1])
    mixed_im, filter_im = (spec_im[0], spec_im[1])
    prod_re = mixed_re * filter_re - mixed_im * filter_im
    prod_im = mixed_re * filter_im + mixed_im * filter_re
    conv_out = token_inverse(prod_re[None], prod_im[None])[0]
    full = conv_out.astype(jnp.float32) + skip_bias[None, :] * mixed_wide
    gated = gate_feat.astype(jnp.float32) * full
    scaled_grad = cotangent.astype(jnp.float32) * norm_gain[None, :]
    square_sum, row_inner = lax.psum(
        (jnp.sum(gated * gated, axis=1), jnp.sum(scaled_grad * gated, axis=1)), "chan"
    )
    inv_rms = lax.rsqrt(square_sum / D + epsilon)[:, None]
    normed_out = (gated * inv_rms * norm_gain[None, :]).astype(jnp.bfloat16)
    grad_gated = inv_rms * scaled_grad - gated * inv_rms**3 * row_inner[:, None] / D
    grad_gate = (grad_gated * full).astype(jnp.bfloat16)
    grad_conv = (grad_gated * gate_feat.astype(jnp.float32)).astype(jnp.bfloat16)
    grad_wide = grad_conv.astype(jnp.float32)
    grad_bias = lax.psum(jnp.sum(grad_wide * mixed_wide, axis=0), "seq")
    grad_re, grad_im = token_forward(grad_conv[None])
    grad_re, grad_im = (grad_re[0], grad_im[0])
    first_re = filter_re * grad_re + filter_im * grad_im
    first_im = filter_re * grad_im - filter_im * grad_re
    second_re = mixed_re * grad_re + mixed_im * grad_im
    second_im = mixed_re * grad_im - mixed_im * grad_re
    returned = token_inverse(jnp.stack([first_re, second_re]), jnp.stack([first_im, second_im]))
    grad_mixed_conv, grad_filter = (returned[0], returned[1])
    grad_mixed = grad_mixed_conv.astype(jnp.float32) + skip_bias[None, :] * grad_wide
    grad_key = (grad_mixed * value_feat.astype(jnp.float32)).astype(jnp.bfloat16)
    grad_value = (grad_mixed * key_feat.astype(jnp.float32)).astype(jnp.bfloat16)
    return (normed_out, grad_gate, grad_key, grad_value, grad_filter, grad_bias)


def solution(mesh):
    return jax.shard_map(
        on_device,
        mesh=mesh,
        in_specs=(
            P("seq", "chan"),
            P("seq", "chan"),
            P("seq", "chan"),
            P("seq", "chan"),
            P("chan"),
            P("chan"),
            P("seq", "chan"),
        ),
        out_specs=(
            P("seq", "chan"),
            P("seq", "chan"),
            P("seq", "chan"),
            P("seq", "chan"),
            P("seq", "chan"),
            P("chan"),
        ),
        check_vma=False,
    )
```

profile of v0, /device:TPU:0, one launch (start us, length us, event | category | flops | bytes accessed | tf_op | source)
XLA Modules:
  0.0 352.2 jit_solution(10182194202087817792)
XLA Ops:
  0.6 1.1 fusion.40
  1.7 1.0 maximum_bitcast_fusion
  2.7 1.3 copy.84
  4.1 6.9 %all-to-all-start = ((bf16[2,1,256,512]{3,0,1,2:T(2,128)(2,1)}), bf16[2,1,256,512]{3,0,1,2:T(2,128)(2,1)S(1)}, u32[]{:S(2)}, u32[]{:S(2)}) async-start(bf16[2,1,256,512]{3,0,1,2:T(2,128)(2,1)} %copy.84), calls=%async_computation | async-start | bytes 1048576 | tf_op jit(solution)/shard_map/all_to_all | solution.py:61
  11.2 12.1 %all-to-all-done = bf16[2,1,256,512]{3,0,1,2:T(2,128)(2,1)S(1)} async-done(((bf16[2,1,256,512]{3,0,1,2:T(2,128)(2,1)}), bf16[2,1,256,512]{3,0,1,2:T(2,128)(2,1)S(1)}, u32[]{:S(2)}, u32[]{:S(2)}) %all-to-all-start) | async-done | bytes 524320 | tf_op jit(solution)/shard_map/all_to_all | solution.py:61
  23.4 1.2 fusion.59
  24.6 1.8 fusion.1
  26.4 1.6 copy.92
  28.0 3.9 %all-to-all-start.2 = ((bf16[2,64,8,512]{3,2,0,1:T(8,128)(2,1)}), bf16[2,64,8,512]{3,2,0,1:T(8,128)(2,1)S(1)}, u32[]{:S(2)}, u32[]{:S(2)}) async-start(bf16[2,64,8,512]{3,2,0,1:T(8,128)(2,1)} %copy.92), calls=%async_computation.2 | async-start | bytes 2097152 | tf_op jit(solution)/shard_map/all_to_all | solution.py:67
  31.9 1.6 copy.88
  33.5 15.0 %all-to-all-done.2 = bf16[2,64,8,512]{3,2,0,1:T(8,128)(2,1)S(1)} async-done(((bf16[2,64,8,512]{3,2,0,1:T(8,128)(2,1)}), bf16[2,64,8,512]{3,2,0,1:T(8,128)(2,1)S(1)}, u32[]{:S(2)}, u32[]{:S(2)}) %all-to-all-start.2) | async-done | bytes 1048608 | tf_op jit(solution)/shard_map/all_to_all | solution.py:67
  48.5 4.1 %all-to-all-start.1 = ((bf16[2,64,8,512]{3,2,0,1:T(8,128)(2,1)}), bf16[2,64,8,512]{3,2,0,1:T(8,128)(2,1)S(1)}, u32[]{:S(2)}, u32[]{:S(2)}) async-start(bf16[2,64,8,512]{3,2,0,1:T(8,128)(2,1)} %copy.88), calls=%async_computation.1 | async-start | bytes 2097152 | tf_op jit(solution)/shard_map/all_to_all | solution.py:64
  52.8 3.4 fusion.28
  56.2 11.8 %all-to-all-done.1 = bf16[2,64,8,512]{3,2,0,1:T(8,128)(2,1)S(1)} async-done(((bf16[2,64,8,512]{3,2,0,1:T(8,128)(2,1)}), bf16[2,64,8,512]{3,2,0,1:T(8,128)(2,1)S(1)}, u32[]{:S(2)}, u32[]{:S(2)}) %all-to-all-start.1) | async-done | bytes 1048608 | tf_op jit(solution)/shard_map/all_to_all | solution.py:64
  68.0 2.1 fusion.32
  70.2 2.2 add_bitcast_fusion
  72.5 2.2 subtract_bitcast_fusion
  75.0 2.0 fusion.26
  77.0 2.4 fusion.22
  79.3 2.0 fusion.13
  81.3 2.2 fusion.46
  83.5 1.2 copy.101
  84.7 3.9 %all-to-all-start.4 = ((bf16[1,2,256,512]{3,1,0,2:T(2,128)(2,1)}), bf16[1,2,256,512]{3,1,0,2:T(2,128)(2,1)S(1)}, u32[]{:S(2)}, u32[]{:S(2)}) async-start(bf16[1,2,256,512]{3,1,0,2:T(2,128)(2,1)} %copy.101), calls=%async_computation.4 | async-start | bytes 1048576 | tf_op jit(solution)/shard_map/all_to_all | solution.py:103
  88.6 1.2 copy.98
  89.8 9.7 %all-to-all-done.4 = bf16[1,2,256,512]{3,1,0,2:T(2,128)(2,1)S(1)} async-done(((bf16[1,2,256,512]{3,1,0,2:T(2,128)(2,1)}), bf16[1,2,256,512]{3,1,0,2:T(2,128)(2,1)S(1)}, u32[]{:S(2)}, u32[]{:S(2)}) %all-to-all-start.4) | async-done | bytes 524320 | tf_op jit(solution)/shard_map/all_to_all | solution.py:103
  99.5 3.9 %all-to-all-start.3 = ((bf16[1,2,256,512]{3,1,0,2:T(2,128)(2,1)}), bf16[1,2,256,512]{3,1,0,2:T(2,128)(2,1)S(1)}, u32[]{:S(2)}, u32[]{:S(2)}) async-start(bf16[1,2,256,512]{3,1,0,2:T(2,128)(2,1)} %copy.98), calls=%async_computation.3 | async-start | bytes 1048576 | tf_op jit(solution)/shard_map/all_to_all | solution.py:100
  103.4 1.3 copy.103
  104.8 1.2 reshape.175
  106.0 8.2 %all-to-all-done.3 = bf16[1,2,256,512]{3,1,0,2:T(2,128)(2,1)S(1)} async-done(((bf16[1,2,256,512]{3,1,0,2:T(2,128)(2,1)}), bf16[1,2,256,512]{3,1,0,2:T(2,128)(2,1)S(1)}, u32[]{:S(2)}, u32[]{:S(2)}) %all-to-all-start.3) | async-done | bytes 524320 | tf_op jit(solution)/shard_map/all_to_all | solution.py:100
  114.9 1.0 reshape.174
  115.9 1.5 fusion.121
  118.1 12.7 %all_to_all.171 = bf16[1,32,8,512]{3,2,0,1:T(8,128)(2,1)S(1)} all-to-all(bf16[1,32,8,512]{3,2,0,1:T(8,128)(2,1)S(1)} %copy.104), channel_id=1, replica_groups=mesh['seq'=32,'chan'=8] {'seq'}, dimensions={1} | all-to-all | bytes 524288 | tf_op jit(solution)/shard_map/all_to_all | solution.py:108
  131.2 15.4 %all-reduce = (f32[256]{0:T(256)S(1)}, f32[256]{0:T(256)S(1)}) all-reduce(f32[256]{0:T(256)S(1)} %get-tuple-element.7, f32[256]{0:T(256)S(1)} %get-tuple-element.6), channel_id=1, replica_groups=mesh['seq'=32,'chan'=8] {'chan'}, use_global_device_ids=true, to_apply=%region_1.2 | all-reduce | flops 512 | bytes 4096 | tf_op jit(solution)/shard_map/psum | solution.py:124
  146.6 1.2 fusion.44
  149.4 2.2 reduce
  151.7 13.4 %all_to_all.172 = bf16[32,2,2048]{2,1,0:T(2,128)(2,1)S(1)} all-to-all(bf16[32,2,2048]{2,1,0:T(2,128)(2,1)S(1)} %reshape.195), channel_id=1, replica_groups=mesh['seq'=32,'chan'=8] {'seq'}, dimensions={0} | all-to-all | bytes 524288 | tf_op jit(solution)/shard_map/all_to_all | solution.py:61
  165.4 0.7 convolution_bitcast_fusion.1
  166.2 1.0 add_convert_fusion.1
  167.2 1.1 copy.109
  168.3 3.9 %all-to-all-start.7 = ((bf16[1,64,8,512]{3,2,0,1:T(8,128)(2,1)}), bf16[1,64,8,512]{3,2,0,1:T(8,128)(2,1)S(1)}, u32[]{:S(2)}, u32[]{:S(2)}) async-start(bf16[1,64,8,512]{3,2,0,1:T(8,128)(2,1)} %copy.109), calls=%async_computation.7 | async-start | bytes 1048576 | tf_op jit(solution)/shard_map/all_to_all | solution.py:64
  172.2 1.1 copy.112
  173.3 10.8 %all-to-all-done.7 = bf16[1,64,8,512]{3,2,0,1:T(8,128)(2,1)S(1)} async-done(((bf16[1,64,8,512]{3,2,0,1:T(8,128)(2,1)}), bf16[1,64,8,512]{3,2,0,1:T(8,128)(2,1)S(1)}, u32[]{:S(2)}, u32[]{:S(2)}) %all-to-all-start.7) | async-done | bytes 524320 | tf_op jit(solution)/shard_map/all_to_all | solution.py:64
  184.1 4.1 %all-to-all-start.8 = ((bf16[1,64,8,512]{3,2,0,1:T(8,128)(2,1)}), bf16[1,64,8,512]{3,2,0,1:T(8,128)(2,1)S(1)}, u32[]{:S(2)}, u32[]{:S(2)}) async-start(bf16[1,64,8,512]{3,2,0,1:T(8,128)(2,1)} %copy.112), calls=%async_computation.8 | async-start | bytes 1048576 | tf_op jit(solution)/shard_map/all_to_all | solution.py:67
  188.1 2.6 fusion.51
  190.8 8.1 %all-to-all-done.8 = bf16[1,64,8,512]{3,2,0,1:T(8,128)(2,1)S(1)} async-done(((bf16[1,64,8,512]{3,2,0,1:T(8,128)(2,1)}), bf16[1,64,8,512]{3,2,0,1:T(8,128)(2,1)S(1)}, u32[]{:S(2)}, u32[]{:S(2)}) %all-to-all-start.8) | async-done | bytes 524320 | tf_op jit(solution)/shard_map/all_to_all | solution.py:67
  198.9 1.6 fusion.47
  200.6 1.7 fusion.12
  202.3 2.2 multiply_add_fusion.1
  204.5 2.8 fusion.4
  207.3 3.1 fusion.5
  210.4 2.9 fusion.8
  213.3 3.2 fusion.21
  216.6 2.2 copy.120
  218.7 3.9 %all-to-all-start.10 = ((bf16[2,2,256,512]{3,1,0,2:T(2,128)(2,1)}), bf16[2,2,256,512]{3,1,0,2:T(2,128)(2,1)S(1)}, u32[]{:S(2)}, u32[]{:S(2)}) async-start(bf16[2,2,256,512]{3,1,0,2:T(2,128)(2,1)} %copy.120), calls=%async_computation.10 | async-start | bytes 2097152 | tf_op jit(solution)/shard_map/all_to_all | solution.py:103
  222.7 2.2 copy.117
  224.8 13.3 %all-to-all-done.10 = bf16[2,2,256,512]{3,1,0,2:T(2,128)(2,1)S(1)} async-done(((bf16[2,2,256,512]{3,1,0,2:T(2,128)(2,1)}), bf16[2,2,256,512]{3,1,0,2:T(2,128)(2,1)S(1)}, u32[]{:S(2)}, u32[]{:S(2)}) %all-to-all-start.10) | async-done | bytes 1048608 | tf_op jit(solution)/shard_map/all_to_all | solution.py:103
  238.1 4.2 %all-to-all-start.9 = ((bf16[2,2,256,512]{3,1,0,2:T(2,128)(2,1)}), bf16[2,2,256,512]{3,1,0,2:T(2,128)(2,1)S(1)}, u32[]{:S(2)}, u32[]{:S(2)}) async-start(bf16[2,2,256,512]{3,1,0,2:T(2,128)(2,1)} %copy.117), calls=%async_computation.9 | async-start | bytes 2097152 | tf_op jit(solution)/shard_map/all_to_all | solution.py:100
  242.5 1.1 copy.122
  244.1 14.1 %all-to-all-done.9 = bf16[2,2,256,512]{3,1,0,2:T(2,128)(2,1)S(1)} async-done(((bf16[2,2,256,512]{3,1,0,2:T(2,128)(2,1)}), bf16[2,2,256,512]{3,1,0,2:T(2,128)(2,1)S(1)}, u32[]{:S(2)}, u32[]{:S(2)}) %all-to-all-start.9) | async-done | bytes 1048608 | tf_op jit(solution)/shard_map/all_to_all | solution.py:100
  258.4 1.1 copy.119
  261.4 1.1 copy.123
  262.5 3.9 %all-to-all-start.11 = ((bf16[2,32,8,512]{3,2,0,1:T(8,128)(2,1)}), bf16[2,32,8,512]{3,2,0,1:T(8,128)(2,1)S(1)}, u32[]{:S(2)}, u32[]{:S(2)}) async-start(bf16[2,32,8,512]{3,2,0,1:T(8,128)(2,1)} %copy.123), calls=%async_computation.11 | async-start | bytes 1048576 | tf_op jit(solution)/shard_map/all_to_all | solution.py:108
  266.4 83.9 %psum.23 = f32[512]{0:T(512)} all-reduce(f32[512]{0:T(512)S(1)} %get-tuple-element.10), channel_id=1, replica_groups=mesh['seq'=32,'chan'=8] {'seq'}, use_global_device_ids=true, to_apply=%region_5.6 | all-reduce | flops 512 | bytes 4096 | tf_op jit(solution)/shard_map/psum | solution.py:133
  351.0 1.0 fusion.39
  (54 shorter events, 7.6 us)
Async XLA Ops:
  4.1 19.2 %all-to-all-start = ((bf16[2,1,256,512]{3,0,1,2:T(2,128)(2,1)}), bf16[2,1,256,512]{3,0,1,2:T(2,128)(2,1)S(1)}, u32[]{:S(2)}, u32[]{:S(2)}) async-start(bf16[2,1,256,512]{3,0,1,2:T(2,128)(2,1)} %copy.84), calls=%async_computation | async-start | bytes 1048576 | tf_op jit(solution)/shard_map/all_to_all | solution.py:61
  28.0 20.5 %all-to-all-start.2 = ((bf16[2,64,8,512]{3,2,0,1:T(8,128)(2,1)}), bf16[2,64,8,512]{3,2,0,1:T(8,128)(2,1)S(1)}, u32[]{:S(2)}, u32[]{:S(2)}) async-start(bf16[2,64,8,512]{3,2,0,1:T(8,128)(2,1)} %copy.92), calls=%async_computation.2 | async-start | bytes 2097152 | tf_op jit(solution)/shard_map/all_to_all | solution.py:67
  48.5 19.5 %all-to-all-start.1 = ((bf16[2,64,8,512]{3,2,0,1:T(8,128)(2,1)}), bf16[2,64,8,512]{3,2,0,1:T(8,128)(2,1)S(1)}, u32[]{:S(2)}, u32[]{:S(2)}) async-start(bf16[2,64,8,512]{3,2,0,1:T(8,128)(2,1)} %copy.88), calls=%async_computation.1 | async-start | bytes 2097152 | tf_op jit(solution)/shard_map/all_to_all | solution.py:64
  68.0 2.2 copy-start.2
  72.4 2.3 copy-start
  84.7 14.8 %all-to-all-start.4 = ((bf16[1,2,256,512]{3,1,0,2:T(2,128)(2,1)}), bf16[1,2,256,512]{3,1,0,2:T(2,128)(2,1)S(1)}, u32[]{:S(2)}, u32[]{:S(2)}) async-start(bf16[1,2,256,512]{3,1,0,2:T(2,128)(2,1)} %copy.101), calls=%async_computation.4 | async-start | bytes 1048576 | tf_op jit(solution)/shard_map/all_to_all | solution.py:103
  99.5 14.8 %all-to-all-start.3 = ((bf16[1,2,256,512]{3,1,0,2:T(2,128)(2,1)}), bf16[1,2,256,512]{3,1,0,2:T(2,128)(2,1)S(1)}, u32[]{:S(2)}, u32[]{:S(2)}) async-start(bf16[1,2,256,512]{3,1,0,2:T(2,128)(2,1)} %copy.98), calls=%async_computation.3 | async-start | bytes 1048576 | tf_op jit(solution)/shard_map/all_to_all | solution.py:100
  114.9 16.0 %copy-start.12 = (f32[512]{0:T(512)S(1)}, f32[512]{0:T(512)}, u32[]{:S(2)}) copy-start(f32[512]{0:T(512)} %param.11) | copy-start | bytes 6148
  114.9 16.0 %copy-start.13 = (f32[512]{0:T(512)S(1)}, f32[512]{0:T(512)}, u32[]{:S(2)}) copy-start(f32[512]{0:T(512)} %param.12) | copy-start | bytes 6148
  115.9 14.9 %copy-start.6 = (bf16[256,512]{1,0:T(8,128)(2,1)S(1)}, bf16[256,512]{1,0:T(8,128)(2,1)}, u32[]{:S(2)}) copy-start(bf16[256,512]{1,0:T(8,128)(2,1)} %param.13) | copy-start | bytes 786436
  115.9 14.9 %copy-start.8 = (bf16[256,512]{1,0:T(8,128)(2,1)S(1)}, bf16[256,512]{1,0:T(8,128)(2,1)}, u32[]{:S(2)}) copy-start(bf16[256,512]{1,0:T(8,128)(2,1)} %param.7) | copy-start | bytes 786436
  117.9 28.7 %copy-start.7 = (bf16[256,512]{1,0:T(8,128)(2,1)S(1)}, bf16[256,512]{1,0:T(8,128)(2,1)}, u32[]{:S(2)}) copy-start(bf16[256,512]{1,0:T(8,128)(2,1)} %param.13) | copy-start | bytes 786436
  117.9 28.7 %copy-start.9 = (bf16[256,512]{1,0:T(8,128)(2,1)S(1)}, bf16[256,512]{1,0:T(8,128)(2,1)}, u32[]{:S(2)}) copy-start(bf16[256,512]{1,0:T(8,128)(2,1)} %param.7) | copy-start | bytes 786436
  147.8 0.7 copy-start.3
  168.3 15.8 %all-to-all-start.7 = ((bf16[1,64,8,512]{3,2,0,1:T(8,128)(2,1)}), bf16[1,64,8,512]{3,2,0,1:T(8,128)(2,1)S(1)}, u32[]{:S(2)}, u32[]{:S(2)}) async-start(bf16[1,64,8,512]{3,2,0,1:T(8,128)(2,1)} %copy.109), calls=%async_computation.7 | async-start | bytes 1048576 | tf_op jit(solution)/shard_map/all_to_all | solution.py:64
  184.1 14.8 %all-to-all-start.8 = ((bf16[1,64,8,512]{3,2,0,1:T(8,128)(2,1)}), bf16[1,64,8,512]{3,2,0,1:T(8,128)(2,1)S(1)}, u32[]{:S(2)}, u32[]{:S(2)}) async-start(bf16[1,64,8,512]{3,2,0,1:T(8,128)(2,1)} %copy.112), calls=%async_computation.8 | async-start | bytes 1048576 | tf_op jit(solution)/shard_map/all_to_all | solution.py:67
  198.9 1.7 copy-start.5
  198.9 3.4 copy-start.1
  218.7 19.4 %all-to-all-start.10 = ((bf16[2,2,256,512]{3,1,0,2:T(2,128)(2,1)}), bf16[2,2,256,512]{3,1,0,2:T(2,128)(2,1)S(1)}, u32[]{:S(2)}, u32[]{:S(2)}) async-start(bf16[2,2,256,512]{3,1,0,2:T(2,128)(2,1)} %copy.120), calls=%async_computation.10 | async-start | bytes 2097152 | tf_op jit(solution)/shard_map/all_to_all | solution.py:103
  238.1 20.0 %all-to-all-start.9 = ((bf16[2,2,256,512]{3,1,0,2:T(2,128)(2,1)}), bf16[2,2,256,512]{3,1,0,2:T(2,128)(2,1)S(1)}, u32[]{:S(2)}, u32[]{:S(2)}) async-start(bf16[2,2,256,512]{3,1,0,2:T(2,128)(2,1)} %copy.117), calls=%async_computation.9 | async-start | bytes 2097152 | tf_op jit(solution)/shard_map/all_to_all | solution.py:100
  260.6 90.3 %copy-start.4 = (bf16[256,512]{1,0:T(8,128)(2,1)S(1)}, bf16[256,512]{1,0:T(8,128)(2,1)}, u32[]{:S(2)}) copy-start(bf16[256,512]{1,0:T(8,128)(2,1)} %copy-done.3) | copy-start | bytes 786436
  260.6 90.3 %copy-start.10 = (bf16[256,512]{1,0:T(8,128)(2,1)S(1)}, bf16[256,512]{1,0:T(8,128)(2,1)}, u32[]{:S(2)}) copy-start(bf16[256,512]{1,0:T(8,128)(2,1)} %param.9) | copy-start | bytes 786436
  260.6 90.3 %copy-start.11 = (bf16[256,512]{1,0:T(8,128)(2,1)S(1)}, bf16[256,512]{1,0:T(8,128)(2,1)}, u32[]{:S(2)}) copy-start(bf16[256,512]{1,0:T(8,128)(2,1)} %param.8) | copy-start | bytes 786436
  262.5 87.8 %all-to-all-start.11 = ((bf16[2,32,8,512]{3,2,0,1:T(8,128)(2,1)}), bf16[2,32,8,512]{3,2,0,1:T(8,128)(2,1)S(1)}, u32[]{:S(2)}, u32[]{:S(2)}) async-start(bf16[2,32,8,512]{3,2,0,1:T(8,128)(2,1)} %copy.123), calls=%async_computation.11 | async-start | bytes 1048576 | tf_op jit(solution)/shard_map/all_to_all | solution.py:108
where the time goes:
time: 358 us; the launch traced here: 352 us
  blocking collectives  125 us (35%)
  waiting for transfers between devices  103 us (29%)
  matrix products  46.9 us (13%)
  starting transfers between devices  42.7 us (12%)
  local copies, waits for them, and re-layouts  25.2 us (7%)
  other arithmetic  7.3 us (2%)
    psum x1, blocking collectives, on_device(): grad_bias = lax.psum(jnp.sum(grad_wide * mixed_wide, axis=0), 'seq')  83.9 us
    dot_general x24, matrix products, einsum_high(): jnp.einsum(pattern, first_op, second_op, precision=lax.Precision.HIGHEST,...  46.9 us
    all_to_all x2, waiting for transfers between devices, token_forward(): lax.all_to_all(spread_im.astype(jnp.bfloat16), 'seq', split_axis=1, conca...  23.2 us
    all_to_all x2, waiting for transfers between devices, token_inverse(): lax.all_to_all(turned_im.astype(jnp.bfloat16), 'seq', split_axis=2, conca...  23 us
    all_to_all x2, waiting for transfers between devices, token_forward(): lax.all_to_all(spread_re.astype(jnp.bfloat16), 'seq', split_axis=1, conca...  22.6 us
    all_to_all x2, waiting for transfers between devices, token_inverse(): lax.all_to_all(turned_re.astype(jnp.bfloat16), 'seq', split_axis=2, conca...  22.4 us
    psum x1, blocking collectives, on_device(): lax.psum((jnp.sum(gated * gated, axis=1), jnp.sum(scaled_grad * gated, ax...  15.4 us
    all_to_all x1, blocking collectives, token_forward(): lax.all_to_all(stacked[:, None], 'seq', split_axis=2, concat_axis=1, tile...  13.4 us
  transfers between devices with their start and end apart: 10, of which 9 were waited for; matrix products, arithmetic and copies ran while one was open for 5% of the time, Pallas kernels for 0%

commit v1 on v0

v1 whole, which is shorter than its diff:
```python
import functools

import jax
import jax.numpy as jnp
import numpy as np
from jax import lax
from jax.experimental import pallas as pl
from jax.experimental.pallas import tpu as pltpu
from jax.sharding import PartitionSpec as P

D = 4096
LENGTH = 8192
epsilon = 1e-05

f32, bf16 = jnp.float32, jnp.bfloat16

PARTS = 32
GROUP = 8
BLOCK = LENGTH // PARTS
WIDTH = D // GROUP
PIECE = WIDTH // PARTS
HALF = PIECE // 2
FULL = 2 * LENGTH
SPAN = 2 * PARTS
BINS = PARTS + 1
ROWS = BINS * PIECE
TAIL = 16


def tables():
    low = np.array(list(range(1, PARTS)) + [0, PARTS])
    block, inside = np.arange(PARTS), np.arange(BLOCK)
    outer = 2 * np.pi * (low[:, None] * block[None, :] % SPAN) / SPAN
    cosine, sine = np.cos(outer), np.sin(outer)
    eye = np.eye(HALF)
    enter = np.kron(np.concatenate([cosine, -sine[: PARTS - 1]], 0), eye)
    weight = np.where((low == 0) | (low == PARTS), 1.0, 2.0)[:, None] / 4
    leave = np.kron(np.concatenate([cosine * weight, (sine * weight)[: PARTS - 1]], 0).T, eye)
    turn = 2 * np.pi * (low[:, None] * inside[None, :] % FULL) / FULL
    turn = np.stack([np.repeat(np.cos(turn), HALF, 0), np.repeat(-np.sin(turn), HALF, 0)])
    inner = 2 * np.pi * (inside[:, None] * inside[None, :] % BLOCK) / BLOCK
    cosine, sine = np.cos(inner) / 16, -np.sin(inner) / 16
    inner = np.block([[cosine, sine], [-sine, cosine]])
    return (
        enter.astype(np.float32).astype(bf16),
        leave.astype(np.float32).astype(bf16),
        inner.astype(np.float32).astype(bf16),
        turn.astype(np.float32),
    )


def dot(first, second):
    return jnp.dot(first, second, preferred_element_type=f32)


def rotate(real, imag, turn):
    cosine, sine = turn[0], turn[1]
    own = imag.shape[0]
    turned_re = jnp.concatenate(
        [real[:own] * cosine[:own] - imag * sine[:own], real[own:] * cosine[own:]], 0
    )
    turned_im = jnp.concatenate(
        [real[:own] * sine[:own] + imag * cosine[:own], real[own:] * sine[own:]], 0
    )
    return turned_re, turned_im


def join(halves):
    parts = [half.reshape(BINS, HALF, BLOCK) for half in halves]
    return jnp.concatenate(parts, 1).reshape(ROWS, BLOCK)


def spectrum(signal, enter, inner, turn):
    wide = signal.astype(f32)
    reals, imags = [], []
    for half in range(2):
        rows = wide[:, half * HALF : (half + 1) * HALF].reshape(PARTS * HALF, BLOCK)
        mixed = dot(enter, rows.astype(bf16))
        real, imag = rotate(mixed[: BINS * HALF], mixed[BINS * HALF :], turn)
        reals.append(real)
        imags.append(imag)
    both = jnp.concatenate([join(reals).astype(bf16), join(imags).astype(bf16)], 1)
    return dot(both, inner)


def invert(real, imag, leave, inner, turn):
    back = dot(jnp.concatenate([real.astype(bf16), imag.astype(bf16)], 1), inner)
    back = back.reshape(BINS, PIECE, 2 * BLOCK)
    outs = []
    for half in range(2):
        rows = back[:, half * HALF : (half + 1) * HALF].reshape(BINS * HALF, 2 * BLOCK)
        real, imag = rows[:, :BLOCK], rows[:, BLOCK:]
        own = (BINS - 2) * HALF
        turned_re = real * turn[0] - imag * turn[1]
        turned_im = real[:own] * turn[1][:own] + imag[:own] * turn[0][:own]
        turned = jnp.concatenate([turned_re, turned_im], 0).astype(bf16)
        outs.append(dot(leave, turned).reshape(PARTS, HALF, BLOCK))
    return jnp.concatenate(outs, 1)


def flat(pieces):
    return pieces.reshape(WIDTH, BLOCK)


def cut(rows):
    return rows.reshape(PARTS, PIECE, BLOCK)


def pack_kernel(key_ref, value_ref, taps_ref, out_ref):
    mixed = (key_ref[...].astype(f32) * value_ref[...].astype(f32)).astype(bf16)
    out_ref[:, :PIECE, :] = cut(mixed.T)
    out_ref[:, PIECE:, :] = cut(taps_ref[...].T)


def side_kernel(gate_ref, cot_ref, skip_ref, gain_ref, gate_out, cot_out, skip_out, gain_out):
    gate_out[...] = gate_ref[...].T
    cot_out[...] = cot_ref[...].T
    skip_out[...] = jnp.broadcast_to(skip_ref[...], (128, WIDTH)).T
    gain_out[...] = jnp.broadcast_to(gain_ref[...], (128, WIDTH)).T


def forward_kernel(in_ref, enter_ref, leave_ref, inner_ref, turn_ref, out_ref, spec_ref):
    enter, leave, inner = enter_ref[...], leave_ref[...], inner_ref[...]
    turn = (turn_ref[0], turn_ref[1])
    first = spectrum(in_ref[:, :PIECE, :], enter, inner, turn)
    spec_ref[0] = first.astype(bf16)
    second = spectrum(in_ref[:, PIECE:, :], enter, inner, turn)
    spec_ref[1] = second.astype(bf16)
    first_re, first_im = first[:, :BLOCK], first[:, BLOCK:]
    second_re, second_im = second[:, :BLOCK], second[:, BLOCK:]
    real = first_re * second_re - first_im * second_im
    imag = -(first_re * second_im + first_im * second_re)
    out_ref[...] = invert(real, imag, leave, inner, turn).astype(bf16)


def wide_twice(column):
    return jnp.concatenate([column, column], 1)


def gate_parts(conv_ref, pack_ref, gate_ref, skip_ref):
    mixed = flat(pack_ref[:, :PIECE, :]).astype(f32)
    full = flat(conv_ref[...]).astype(f32) + wide_twice(skip_ref[...]) * mixed
    gate = gate_ref[...].astype(f32)
    return full, gate, gate * full


def sums_kernel(conv_ref, pack_ref, gate_ref, cot_ref, skip_ref, gain_ref, out_ref):
    _, _, gated = gate_parts(conv_ref, pack_ref, gate_ref, skip_ref)
    scaled = cot_ref[...].astype(f32) * wide_twice(gain_ref[...])
    squares = jnp.sum(gated * gated, axis=0, keepdims=True)
    inner = jnp.sum(scaled * gated, axis=0, keepdims=True)
    both = jnp.concatenate([squares, inner], 0)
    out_ref[...] = jnp.broadcast_to(both[None], (GROUP, 2, BLOCK))


def norm_parts(sums_ref):
    sums = jnp.sum(sums_ref[...], axis=0)
    inv_rms = lax.rsqrt(sums[0:1] / D + epsilon)
    return inv_rms, inv_rms * inv_rms * inv_rms * sums[1:2] / D


def grad_kernel(sums_ref, conv_ref, pack_ref, gate_ref, cot_ref, skip_ref, gain_ref, out_ref):
    inv_rms, pull = norm_parts(sums_ref)
    _, gate, gated = gate_parts(conv_ref, pack_ref, gate_ref, skip_ref)
    scaled = cot_ref[...].astype(f32) * wide_twice(gain_ref[...])
    grad_gated = inv_rms * scaled - gated * pull
    out_ref[...] = cut((grad_gated * gate).astype(bf16))


def norm_kernel(
    sums_ref, conv_ref, pack_ref, gate_ref, cot_ref, skip_ref, gain_ref, grad_ref, normed_out, gate_out, grad_out
):
    inv_rms, pull = norm_parts(sums_ref)
    full, _, gated = gate_parts(conv_ref, pack_ref, gate_ref, skip_ref)
    gain = wide_twice(gain_ref[...])
    normed_out[...] = (gated * inv_rms * gain).astype(bf16).T
    grad_gated = inv_rms * (cot_ref[...].astype(f32) * gain) - gated * pull
    gate_out[...] = (grad_gated * full).astype(bf16).T
    grad_out[...] = flat(grad_ref[...]).T


def backward_kernel(in_ref, pack_ref, spec_ref, enter_ref, leave_ref, inner_ref, turn_ref, out_ref):
    enter, leave, inner = enter_ref[...], leave_ref[...], inner_ref[...]
    turn = (turn_ref[0], turn_ref[1])
    grad = in_ref[...]
    bias = jnp.sum(grad.astype(f32) * pack_ref[:, :PIECE, :].astype(f32), axis=0)
    bias = jnp.sum(bias, axis=1, keepdims=True)
    high = bias.astype(bf16).astype(f32)
    lane = lax.broadcasted_iota(jnp.int32, (PIECE, 128), 1)
    bias = jnp.where(lane == 0, high, jnp.where(lane == 1, bias - high, 0.0)).astype(bf16)
    out_ref[:, 4 * PIECE :, :] = jnp.broadcast_to(bias[None], (PARTS, TAIL, 128))
    grad = spectrum(grad, enter, inner, turn)
    grad_re, grad_im = grad[:, :BLOCK], grad[:, BLOCK:]
    for place, other in ((0, 1), (1, 0)):
        real, imag = spec_ref[other, :, :BLOCK].astype(f32), spec_ref[other, :, BLOCK:].astype(f32)
        result = invert(
            real * grad_re + imag * grad_im, imag * grad_re - real * grad_im, leave, inner, turn
        ).astype(bf16)
        out_ref[:, 2 * place * PIECE : (2 * place + 1) * PIECE, :] = result[:, :, :128]
        out_ref[:, (2 * place + 1) * PIECE : (2 * place + 2) * PIECE, :] = result[:, :, 128:]


def last_kernel(in_ref, grad_ref, key_ref, value_ref, skip_ref, key_out, value_out, taps_out, bias_out):
    def whole(place):
        at = 2 * place * PIECE
        left, right = in_ref[:, at : at + PIECE, :], in_ref[:, at + PIECE : at + 2 * PIECE, :]
        return jnp.concatenate([left.reshape(WIDTH, 128).T, right.reshape(WIDTH, 128).T], 0)

    grad_mixed = whole(0).astype(f32) + skip_ref[...] * grad_ref[...].astype(f32)
    key_out[...] = (grad_mixed * value_ref[...].astype(f32)).astype(bf16)
    value_out[...] = (grad_mixed * key_ref[...].astype(f32)).astype(bf16)
    taps_out[...] = whole(1)
    bias = in_ref[:, 4 * PIECE :, :].reshape(WIDTH, 128).astype(f32).T
    bias_out[...] = bias[0:1] + bias[1:2]


def call(kernel, name, outs, *operands):
    return pl.pallas_call(
        kernel,
        name=name,
        out_shape=[jax.ShapeDtypeStruct(shape, kind) for shape, kind in outs],
        compiler_params=pltpu.CompilerParams(vmem_limit_bytes=40 * 1024 * 1024),
    )(*operands)


def on_device(gate_feat, key_feat, value_feat, filter_taps, skip_bias, norm_gain, cotangent):
    enter, leave, inner, turn = (jnp.asarray(table) for table in tables())
    skip_row, gain_row = skip_bias[None, :], norm_gain[None, :]
    natural = ((BLOCK, WIDTH), bf16)
    turned = ((WIDTH, BLOCK), bf16)
    column = ((WIDTH, 128), f32)
    pieces = ((PARTS, PIECE, BLOCK), bf16)

    (packed,) = call(pack_kernel, "pack", [((PARTS, 2 * PIECE, BLOCK), bf16)], key_feat, value_feat, filter_taps)
    arrived = lax.all_to_all(packed, "seq", 0, 0, tiled=True)
    gate_t, cot_t, skip_t, gain_t = call(
        side_kernel, "side", [turned, turned, column, column], gate_feat, cotangent, skip_row, gain_row
    )
    conv, spec = call(
        forward_kernel, "forward", [pieces, ((2, ROWS, 2 * BLOCK), bf16)], arrived, enter, leave, inner, turn
    )
    conv = lax.all_to_all(conv, "seq", 0, 0, tiled=True)
    sides = (conv, packed, gate_t, cot_t, skip_t, gain_t)
    (sums,) = call(sums_kernel, "sums", [((GROUP, 2, BLOCK), f32)], *sides)
    sums = lax.all_to_all(sums, "chan", 0, 0, tiled=True)
    (grad,) = call(grad_kernel, "grad", [pieces], sums, *sides)
    grad_arrived = lax.all_to_all(grad, "seq", 0, 0, tiled=True)
    normed_out, grad_gate, grad_conv = call(norm_kernel, "norm", [natural] * 3, sums, *sides, grad)
    (result,) = call(
        backward_kernel,
        "backward",
        [((PARTS, 4 * PIECE + TAIL, 128), bf16)],
        grad_arrived,
        arrived,
        spec,
        enter,
        leave,
        inner,
        turn,
    )
    result = lax.all_to_all(result, "seq", 0, 0, tiled=True)
    grad_key, grad_value, grad_filter, grad_bias = call(
        last_kernel,
        "last",
        [natural] * 3 + [((1, WIDTH), f32)],
        result,
        grad_conv,
        key_feat,
        value_feat,
        skip_row,
    )
    return normed_out, grad_gate, grad_key, grad_value, grad_filter, grad_bias[0]


def solution(mesh):
    wide, row = P("seq", "chan"), P("chan")
    return jax.shard_map(
        on_device,
        mesh=mesh,
        in_specs=(wide, wide, wide, wide, row, row, wide),
        out_specs=(wide, wide, wide, wide, wide, row),
        check_vma=False,
    )
```

time: 358 us -> 90.6 us (0.25); the launches traced: 352 us -> 89.3 us
  waiting for transfers between devices: 103 us -> 19.5 us
  blocking collectives: 125 us -> 47.2 us
  matrix products: 46.9 us -> 0 us
  starting transfers between devices: 42.7 us -> 7.77 us
  local copies, waits for them, and re-layouts: 25.2 us -> 5.64 us
  Pallas kernels: 0 us -> 8.45 us
  other arithmetic: 7.3 us -> 0 us
    psum x2 -> x0, blocking collectives: 99.3 us -> none  [the longest x1 83.9 us: on_device(): grad_bias = lax.psum(jnp.sum(grad_wide * mixed_wide, axis=0), 'seq')]
    all_to_all x10 -> x2, waiting for transfers between devices: 103 us -> 19.5 us  [the longest x1 11.4 us: on_device(): result = lax.all_to_all(result, 'seq', 0, 0, tiled=True)]
    dot_general x24 -> x0, matrix products: 46.9 us -> none  [einsum_high(): jnp.einsum(pattern, first_op, second_op, precision=lax.Precision.HIGHEST,...]
    all_to_all x10 -> x2, starting transfers between devices: 42.7 us -> 7.77 us  [the longest x1 3.9 us: on_device(): result = lax.all_to_all(result, 'seq', 0, 0, tiled=True)]
    all_to_all x2 -> x3, blocking collectives: 26.1 us -> 47.2 us  [the longest x1 19 us: on_device(): arrived = lax.all_to_all(packed, 'seq', 0, 0, tiled=True)]
    convert_element_type x10 -> x0, local copies, waits for them, and re-layouts: 13.3 us -> none  [the longest x2 3.35 us: token_inverse(): turned_re.astype(jnp.bfloat16)]
    pallas_call x0 -> x8, Pallas kernels: none -> 8.45 us  [call(): pl.pallas_call(kernel, name=name, out_shape=[jax.ShapeDtypeStruct(shape,...]
    all_to_all x11 -> x0, local copies, waits for them, and re-layouts: 5.47 us -> none  [the longest x5 3.1 us: token_inverse(): lax.all_to_all(turned_im.astype(jnp.bfloat16), 'seq', split_axis=2, conca...]
  transfers between devices with their start and end apart: 10 -> 2, of which waited for: 9 -> 2; matrix products, arithmetic and copies ran while one was open for 5% -> 0% of each run, Pallas kernels for 0% -> 2%
where the time goes in v1:
time: 90.6 us; the launch traced here: 89.3 us
  blocking collectives  47.2 us (52%)
  waiting for transfers between devices  19.5 us (22%)
  Pallas kernels  8.45 us (9%)
  starting transfers between devices  7.77 us (9%)
  local copies, waits for them, and re-layouts  5.64 us (6%)
    all_to_all x1, blocking collectives, on_device(): arrived = lax.all_to_all(packed, 'seq', 0, 0, tiled=True)  19 us
    all_to_all x1, blocking collectives, on_device(): sums = lax.all_to_all(sums, 'chan', 0, 0, tiled=True)  15.1 us
    all_to_all x1, blocking collectives, on_device(): grad_arrived = lax.all_to_all(grad, 'seq', 0, 0, tiled=True)  13 us
    all_to_all x1, waiting for transfers between devices, on_device(): result = lax.all_to_all(result, 'seq', 0, 0, tiled=True)  11.4 us
    pallas_call x8, Pallas kernels, call(): pl.pallas_call(kernel, name=name, out_shape=[jax.ShapeDtypeStruct(shape,...  8.45 us
    all_to_all x1, waiting for transfers between devices, on_device(): conv = lax.all_to_all(conv, 'seq', 0, 0, tiled=True)  8.12 us
    unnamed x36, local copies, waits for them, and re-layouts  5.64 us
    all_to_all x1, starting transfers between devices, on_device(): result = lax.all_to_all(result, 'seq', 0, 0, tiled=True)  3.9 us
  transfers between devices with their start and end apart: 2, of which 2 were waited for; matrix products, arithmetic and copies ran while one was open for 0% of the time, Pallas kernels for 2%

profile of v1, /device:TPU:0, one launch (start us, length us, event | category | flops | bytes accessed | tf_op | source)
XLA Modules:
  0.0 89.3 jit_solution(11223350865149539285)
XLA Ops:
  0.6 0.0 copy-start
  0.6 0.0 copy-start.1
  0.7 0.0 copy-start.5
  0.7 1.0 %copy-done.5 = bf16[256,512]{1,0:T(8,128)(2,1)S(1)} copy-done((bf16[256,512]{1,0:T(8,128)(2,1)S(1)}, bf16[256,512]{1,0:T(8,128)(2,1)}, u32[]{:S(2)}) %copy-start.5) | copy-done | bytes 262168
  1.7 0.0 copy-start.7
  1.7 0.9 %copy-done.7 = bf16[256,512]{1,0:T(8,128)(2,1)S(1)} copy-done((bf16[256,512]{1,0:T(8,128)(2,1)S(1)}, bf16[256,512]{1,0:T(8,128)(2,1)}, u32[]{:S(2)}) %copy-start.7) | copy-done | bytes 262168
  2.6 0.0 copy-start.12
  2.6 0.9 %copy-done.12 = bf16[256,512]{1,0:T(8,128)(2,1)S(1)} copy-done((bf16[256,512]{1,0:T(8,128)(2,1)S(1)}, bf16[256,512]{1,0:T(8,128)(2,1)}, u32[]{:S(2)}) %copy-start.12) | copy-done | bytes 262168
  3.6 0.0 copy-start.9
  3.6 0.0 copy-start.10
  3.6 0.2 pack.1.pack_ref
  3.8 19.0 %all_to_all.25.in_ref.pack_ref = bf16[32,32,256]{2,1,0:T(8,128)(2,1)S(1)} all-to-all(bf16[32,32,256]{2,1,0:T(8,128)(2,1)S(1)} %pack.1.pack_ref), channel_id=1, replica_groups=mesh['seq'=32,'chan'=8] {'seq'}, dimensions={0} | all-to-all | bytes 1048576 | tf_op jit(solution)/shard_map/all_to_all | solution.py:235
  22.8 0.0 copy-done
  22.8 0.0 copy-done.1
  22.8 0.0 copy-done.9
  22.8 0.0 copy-done.10
  22.8 0.0 copy-start.13
  22.9 0.0 copy-start.15
  22.9 0.0 copy-start.17
  22.9 2.5 %forward.1 = (bf16[32,16,256]{2,1,0:T(8,128)(2,1)}, bf16[2,528,512]{2,1,0:T(8,128)(2,1)S(1)}) custom-call(bf16[32,32,256]{2,1,0:T(8,128)(2,1)S(1)} %all_to_all.25.in_ref.pack_ref, bf16[512,256]{1,0:T(8,128)(2,1)S(1)} %copy-done.10, bf16[256,512]{1,0:T(8,128)(2,1)S(1)} %copy-done.9, bf16[512,512]{1,0:T(8,128)(2,1)S(1)} %copy-done.1, f32[2,264,256]{2,1,0:T(8,128)S(1)} %copy-done), custom_call_target="tpu_custom_call" | custom-call | tf_op jit(solution)/shard_map/forward/pallas_call | solution.py:218
  25.4 0.0 copy-start.3
  25.4 1.0 %copy-done.3 = bf16[2,528,512]{2,1,0:T(8,128)(2,1)} copy-done((bf16[2,528,512]{2,1,0:T(8,128)(2,1)}, bf16[2,528,512]{2,1,0:T(8,128)(2,1)S(1)}, u32[]{:S(2)}) %copy-start.3) | copy-done | bytes 1081368
  26.4 3.9 %all-to-all-start.1 = ((bf16[32,16,256]{2,1,0:T(8,128)(2,1)}), bf16[32,16,256]{2,1,0:T(8,128)(2,1)S(1)}, u32[]{:S(2)}, u32[]{:S(2)}) async-start(bf16[32,16,256]{2,1,0:T(8,128)(2,1)} %get-tuple-element.19), calls=%async_computation.1 | async-start | bytes 524288 | tf_op jit(solution)/shard_map/all_to_all | solution.py:242
  30.3 0.0 copy-done.13
  30.3 0.0 copy-done.15
  30.3 0.0 copy-done.17
  30.3 0.0 copy-start.14
  30.3 0.9 %copy-done.14 = bf16[256,512]{1,0:T(8,128)(2,1)S(1)} copy-done((bf16[256,512]{1,0:T(8,128)(2,1)S(1)}, bf16[256,512]{1,0:T(8,128)(2,1)}, u32[]{:S(2)}) %copy-start.14) | copy-done | bytes 262168
  31.3 0.3 side.1
  31.6 8.1 %all-to-all-done.1.conv_ref = bf16[32,16,256]{2,1,0:T(8,128)(2,1)S(1)} async-done(((bf16[32,16,256]{2,1,0:T(8,128)(2,1)}), bf16[32,16,256]{2,1,0:T(8,128)(2,1)S(1)}, u32[]{:S(2)}, u32[]{:S(2)}) %all-to-all-start.1) | async-done | bytes 262176 | tf_op jit(solution)/shard_map/all_to_all | solution.py:242
  39.7 0.3 sums.1
  40.0 15.1 %all_to_all.26.sums_ref = f32[8,2,256]{2,1,0:T(2,128)S(1)} all-to-all(f32[8,2,256]{2,1,0:T(2,128)S(1)} %sums.1), channel_id=1, replica_groups=mesh['seq'=32,'chan'=8] {'chan'}, dimensions={0} | all-to-all | bytes 32768 | tf_op jit(solution)/shard_map/all_to_all | solution.py:245
  55.2 0.0 copy-start.2
  55.2 0.0 copy-start.4
  55.2 0.0 copy-start.11
  55.2 0.2 grad.1.grad_ref
  55.4 13.0 %all_to_all.27.in_ref = bf16[32,16,256]{2,1,0:T(8,128)(2,1)S(1)} all-to-all(bf16[32,16,256]{2,1,0:T(8,128)(2,1)S(1)} %grad.1.grad_ref), channel_id=1, replica_groups=mesh['seq'=32,'chan'=8] {'seq'}, dimensions={0} | all-to-all | bytes 524288 | tf_op jit(solution)/shard_map/all_to_all | solution.py:247
  68.4 0.0 copy-done.2
  68.4 0.0 copy-done.4
  68.4 0.0 copy-done.11
  68.4 2.8 %backward.1 = bf16[32,80,128]{2,1,0:T(8,128)(2,1)} custom-call(bf16[32,16,256]{2,1,0:T(8,128)(2,1)S(1)} %all_to_all.27.in_ref, bf16[32,32,256]{2,1,0:T(8,128)(2,1)S(1)} %all_to_all.25.in_ref.pack_ref, bf16[2,528,512]{2,1,0:T(8,128)(2,1)S(1)} %copy-done.4, bf16[512,256]{1,0:T(8,128)(2,1)S(1)} %copy-done.11, bf16[256,512]{1,0:T(8,128)(2,1)S(1)} %copy-done.9, ...), custom_call_target="tpu_custom_call" | custom-call | tf_op jit(solution)/shard_map/backward/pallas_call | solution.py:218
  71.2 3.9 %all-to-all-start.4 = ((bf16[32,80,128]{2,1,0:T(8,128)(2,1)}), bf16[32,80,128]{2,1,0:T(8,128)(2,1)S(1)}, u32[]{:S(2)}, u32[]{:S(2)}) async-start(bf16[32,80,128]{2,1,0:T(8,128)(2,1)} %backward.1), calls=%async_computation.4 | async-start | bytes 1310720 | tf_op jit(solution)/shard_map/all_to_all | solution.py:261
  75.1 0.0 copy-start.6
  75.1 0.0 copy-start.8
  75.1 1.0 %norm.1 = (bf16[256,512]{1,0:T(8,128)(2,1)}, bf16[256,512]{1,0:T(8,128)(2,1)}, bf16[256,512]{1,0:T(8,128)(2,1)S(1)}) custom-call(f32[8,2,256]{2,1,0:T(2,128)S(1)} %all_to_all.26.sums_ref, bf16[32,16,256]{2,1,0:T(8,128)(2,1)S(1)} %all-to-all-done.1.conv_ref, bf16[32,32,256]{2,1,0:T(8,128)(2,1)S(1)} %pack.1.pack_ref, ...), custom_call_target="tpu_custom_call" | custom-call | tf_op jit(solution)/shard_map/norm/pallas_call | solution.py:218
  76.2 11.4 %all-to-all-done.4.in_ref = bf16[32,80,128]{2,1,0:T(8,128)(2,1)S(1)} async-done(((bf16[32,80,128]{2,1,0:T(8,128)(2,1)}), bf16[32,80,128]{2,1,0:T(8,128)(2,1)S(1)}, u32[]{:S(2)}, u32[]{:S(2)}) %all-to-all-start.4) | async-done | bytes 655392 | tf_op jit(solution)/shard_map/all_to_all | solution.py:261
  87.6 0.0 copy-done.6
  87.6 0.0 copy-done.8
  87.6 0.0 copy-start.16
  87.6 0.7 copy-done.16
  88.3 1.1 %last.1 = (bf16[256,512]{1,0:T(8,128)(2,1)}, bf16[256,512]{1,0:T(8,128)(2,1)}, bf16[256,512]{1,0:T(8,128)(2,1)}, f32[1,512]{1,0:T(1,128)}) custom-call(bf16[32,80,128]{2,1,0:T(8,128)(2,1)S(1)} %all-to-all-done.4.in_ref, bf16[256,512]{1,0:T(8,128)(2,1)S(1)} %get-tuple-element.27.grad_ref, bf16[256,512]{1,0:T(8,128)(2,1)S(1)} %copy-done.6, ...), custom_call_target="tpu_custom_call" | custom-call | tf_op jit(solution)/shard_map/last/pallas_call | solution.py:218
Async XLA Ops:
  0.6 22.2 %copy-start = (f32[2,264,256]{2,1,0:T(8,128)S(1)}, f32[2,264,256]{2,1,0:T(8,128)}, u32[]{:S(2)}) copy-start(f32[2,264,256]{2,1,0:T(8,128)} %constant.11.clone.turn_ref) | copy-start | bytes 1622020
  0.6 22.2 %copy-start.1 = (bf16[512,512]{1,0:T(8,128)(2,1)S(1)}, bf16[512,512]{1,0:T(8,128)(2,1)}, u32[]{:S(2)}) copy-start(bf16[512,512]{1,0:T(8,128)(2,1)} %constant.10.clone.inner_ref) | copy-start | bytes 1572868
  0.7 1.0 %copy-start.5 = (bf16[256,512]{1,0:T(8,128)(2,1)S(1)}, bf16[256,512]{1,0:T(8,128)(2,1)}, u32[]{:S(2)}) copy-start(bf16[256,512]{1,0:T(8,128)(2,1)} %key_ref.3) | copy-start | bytes 786436
  1.7 0.9 %copy-start.7 = (bf16[256,512]{1,0:T(8,128)(2,1)S(1)}, bf16[256,512]{1,0:T(8,128)(2,1)}, u32[]{:S(2)}) copy-start(bf16[256,512]{1,0:T(8,128)(2,1)} %value_ref.3) | copy-start | bytes 786436
  2.6 0.9 %copy-start.12 = (bf16[256,512]{1,0:T(8,128)(2,1)S(1)}, bf16[256,512]{1,0:T(8,128)(2,1)}, u32[]{:S(2)}) copy-start(bf16[256,512]{1,0:T(8,128)(2,1)} %taps_ref.1) | copy-start | bytes 786436
  3.6 19.2 %copy-start.9 = (bf16[256,512]{1,0:T(8,128)(2,1)S(1)}, bf16[256,512]{1,0:T(8,128)(2,1)}, u32[]{:S(2)}) copy-start(bf16[256,512]{1,0:T(8,128)(2,1)} %constant.9.clone.leave_ref) | copy-start | bytes 786436
  3.6 19.2 %copy-start.10 = (bf16[512,256]{1,0:T(8,128)(2,1)S(1)}, bf16[512,256]{1,0:T(8,128)(2,1)}, u32[]{:S(2)}) copy-start(bf16[512,256]{1,0:T(8,128)(2,1)} %constant.8.clone.enter_ref) | copy-start | bytes 786436
  22.8 7.5 %copy-start.13 = (bf16[256,512]{1,0:T(8,128)(2,1)S(1)}, bf16[256,512]{1,0:T(8,128)(2,1)}, u32[]{:S(2)}) copy-start(bf16[256,512]{1,0:T(8,128)(2,1)} %gate_ref.1) | copy-start | bytes 786436
  22.9 7.5 %copy-start.15 = (f32[512]{0:T(512)S(1)}, f32[512]{0:T(512)}, u32[]{:S(2)}) copy-start(f32[512]{0:T(512)} %param.15) | copy-start | bytes 6148
  22.9 7.5 %copy-start.17 = (f32[512]{0:T(512)S(1)}, f32[512]{0:T(512)}, u32[]{:S(2)}) copy-start(f32[512]{0:T(512)} %param.16) | copy-start | bytes 6148
  25.4 1.0 %copy-start.3 = (bf16[2,528,512]{2,1,0:T(8,128)(2,1)}, bf16[2,528,512]{2,1,0:T(8,128)(2,1)S(1)}, u32[]{:S(2)}) copy-start(bf16[2,528,512]{2,1,0:T(8,128)(2,1)S(1)} %get-tuple-element.26.spec_ref) | copy-start | bytes 3244036
  26.4 13.3 %all-to-all-start.1 = ((bf16[32,16,256]{2,1,0:T(8,128)(2,1)}), bf16[32,16,256]{2,1,0:T(8,128)(2,1)S(1)}, u32[]{:S(2)}, u32[]{:S(2)}) async-start(bf16[32,16,256]{2,1,0:T(8,128)(2,1)} %get-tuple-element.19), calls=%async_computation.1 | async-start | bytes 524288 | tf_op jit(solution)/shard_map/all_to_all | solution.py:242
  30.3 1.0 %copy-start.14 = (bf16[256,512]{1,0:T(8,128)(2,1)S(1)}, bf16[256,512]{1,0:T(8,128)(2,1)}, u32[]{:S(2)}) copy-start(bf16[256,512]{1,0:T(8,128)(2,1)} %cot_ref.1) | copy-start | bytes 786436
  55.2 13.2 %copy-start.2 = (bf16[512,512]{1,0:T(8,128)(2,1)S(1)}, bf16[512,512]{1,0:T(8,128)(2,1)}, u32[]{:S(2)}) copy-start(bf16[512,512]{1,0:T(8,128)(2,1)} %constant.10.clone.inner_ref) | copy-start | bytes 1572868
  55.2 13.2 %copy-start.4 = (bf16[2,528,512]{2,1,0:T(8,128)(2,1)S(1)}, bf16[2,528,512]{2,1,0:T(8,128)(2,1)}, u32[]{:S(2)}) copy-start(bf16[2,528,512]{2,1,0:T(8,128)(2,1)} %copy-done.3) | copy-start | bytes 3244036
  55.2 13.2 %copy-start.11 = (bf16[512,256]{1,0:T(8,128)(2,1)S(1)}, bf16[512,256]{1,0:T(8,128)(2,1)}, u32[]{:S(2)}) copy-start(bf16[512,256]{1,0:T(8,128)(2,1)} %constant.8.clone.enter_ref) | copy-start | bytes 786436
  71.2 16.4 %all-to-all-start.4 = ((bf16[32,80,128]{2,1,0:T(8,128)(2,1)}), bf16[32,80,128]{2,1,0:T(8,128)(2,1)S(1)}, u32[]{:S(2)}, u32[]{:S(2)}) async-start(bf16[32,80,128]{2,1,0:T(8,128)(2,1)} %backward.1), calls=%async_computation.4 | async-start | bytes 1310720 | tf_op jit(solution)/shard_map/all_to_all | solution.py:261
  75.1 12.5 %copy-start.6 = (bf16[256,512]{1,0:T(8,128)(2,1)S(1)}, bf16[256,512]{1,0:T(8,128)(2,1)}, u32[]{:S(2)}) copy-start(bf16[256,512]{1,0:T(8,128)(2,1)} %key_ref.3) | copy-start | bytes 786436
  75.1 12.5 %copy-start.8 = (bf16[256,512]{1,0:T(8,128)(2,1)S(1)}, bf16[256,512]{1,0:T(8,128)(2,1)}, u32[]{:S(2)}) copy-start(bf16[256,512]{1,0:T(8,128)(2,1)} %value_ref.3) | copy-start | bytes 786436
  87.6 0.7 copy-start.16

commit v2 on v1

--- a/solution.py
+++ b/solution.py
@@ -1,5 +1,3 @@
-import functools
-
 import jax
 import jax.numpy as jnp
 import numpy as np
@@ -24,7 +22,8 @@
 SPAN = 2 * PARTS
 BINS = PARTS + 1
 ROWS = BINS * PIECE
-TAIL = 16
+TAIL = 8
+CHIPS = GROUP // 2
 
 
 def tables():
@@ -106,9 +105,20 @@
     return rows.reshape(PARTS, PIECE, BLOCK)
 
 
-def pack_kernel(key_ref, value_ref, taps_ref, out_ref):
+def pack_kernel(key_hbm, value_hbm, taps_hbm, out_ref, key_ref, value_ref, taps_ref, sems):
+    copies = [
+        pltpu.make_async_copy(source, target, sems.at[place])
+        for place, (source, target) in enumerate(
+            ((key_hbm, key_ref), (value_hbm, value_ref), (taps_hbm, taps_ref))
+        )
+    ]
+    for copy in copies:
+        copy.start()
+    copies[0].wait()
+    copies[1].wait()
     mixed = (key_ref[...].astype(f32) * value_ref[...].astype(f32)).astype(bf16)
     out_ref[:, :PIECE, :] = cut(mixed.T)
+    copies[2].wait()
     out_ref[:, PIECE:, :] = cut(taps_ref[...].T)
 
 
@@ -119,18 +129,23 @@
     gain_out[...] = jnp.broadcast_to(gain_ref[...], (128, WIDTH)).T
 
 
-def forward_kernel(in_ref, enter_ref, leave_ref, inner_ref, turn_ref, out_ref, spec_ref):
+def forward_kernel(in_ref, enter_ref, leave_ref, inner_ref, turn_ref, out_ref, spec_hbm, spec_ref, sems):
     enter, leave, inner = enter_ref[...], leave_ref[...], inner_ref[...]
     turn = (turn_ref[0], turn_ref[1])
-    first = spectrum(in_ref[:, :PIECE, :], enter, inner, turn)
-    spec_ref[0] = first.astype(bf16)
-    second = spectrum(in_ref[:, PIECE:, :], enter, inner, turn)
-    spec_ref[1] = second.astype(bf16)
-    first_re, first_im = first[:, :BLOCK], first[:, BLOCK:]
-    second_re, second_im = second[:, :BLOCK], second[:, BLOCK:]
+    spectra, copies = [], []
+    for place in range(2):
+        signal = in_ref[:, place * PIECE : (place + 1) * PIECE, :]
+        spectra.append(spectrum(signal, enter, inner, turn))
+        spec_ref[place] = spectra[place].astype(bf16)
+        copies.append(pltpu.make_async_copy(spec_ref.at[place], spec_hbm.at[place], sems.at[place]))
+        copies[place].start()
+    first_re, first_im = spectra[0][:, :BLOCK], spectra[0][:, BLOCK:]
+    second_re, second_im = spectra[1][:, :BLOCK], spectra[1][:, BLOCK:]
     real = first_re * second_re - first_im * second_im
     imag = -(first_re * second_im + first_im * second_re)
     out_ref[...] = invert(real, imag, leave, inner, turn).astype(bf16)
+    for copy in copies:
+        copy.wait()
 
 
 def wide_twice(column):
@@ -149,12 +164,11 @@
     scaled = cot_ref[...].astype(f32) * wide_twice(gain_ref[...])
     squares = jnp.sum(gated * gated, axis=0, keepdims=True)
     inner = jnp.sum(scaled * gated, axis=0, keepdims=True)
-    both = jnp.concatenate([squares, inner], 0)
-    out_ref[...] = jnp.broadcast_to(both[None], (GROUP, 2, BLOCK))
+    out_ref[...] = jnp.concatenate([squares, inner], 0)
 
 
 def norm_parts(sums_ref):
-    sums = jnp.sum(sums_ref[...], axis=0)
+    sums = sums_ref[...]
     inv_rms = lax.rsqrt(sums[0:1] / D + epsilon)
     return inv_rms, inv_rms * inv_rms * inv_rms * sums[1:2] / D
 
@@ -168,7 +182,8 @@
 
 
 def norm_kernel(
-    sums_ref, conv_ref, pack_ref, gate_ref, cot_ref, skip_ref, gain_ref, grad_ref, normed_out, gate_out, grad_out
+    sums_ref, conv_ref, pack_ref, gate_ref, cot_ref, skip_ref, gain_ref, grad_ref, row_ref,
+    normed_out, gate_out, grad_out, row_out,
 ):
     inv_rms, pull = norm_parts(sums_ref)
     full, _, gated = gate_parts(conv_ref, pack_ref, gate_ref, skip_ref)
@@ -177,6 +192,7 @@
     grad_gated = inv_rms * (cot_ref[...].astype(f32) * gain) - gated * pull
     gate_out[...] = (grad_gated * full).astype(bf16).T
     grad_out[...] = flat(grad_ref[...]).T
+    row_out[...] = row_ref[...]
 
 
 def backward_kernel(in_ref, pack_ref, spec_ref, enter_ref, leave_ref, inner_ref, turn_ref, out_ref):
@@ -186,9 +202,11 @@
     bias = jnp.sum(grad.astype(f32) * pack_ref[:, :PIECE, :].astype(f32), axis=0)
     bias = jnp.sum(bias, axis=1, keepdims=True)
     high = bias.astype(bf16).astype(f32)
-    lane = lax.broadcasted_iota(jnp.int32, (PIECE, 128), 1)
-    bias = jnp.where(lane == 0, high, jnp.where(lane == 1, bias - high, 0.0)).astype(bf16)
-    out_ref[:, 4 * PIECE :, :] = jnp.broadcast_to(bias[None], (PARTS, TAIL, 128))
+    lane = lax.broadcasted_iota(jnp.int32, (TAIL, 128), 1)
+    tail = jnp.zeros((TAIL, 128), f32)
+    for at, part in enumerate((high[:HALF], (bias - high)[:HALF], high[HALF:], (bias - high)[HALF:])):
+        tail = jnp.where(lane == at, part, tail)
+    out_ref[:, 4 * PIECE :, :] = jnp.broadcast_to(tail.astype(bf16)[None], (PARTS, TAIL, 128))
     grad = spectrum(grad, enter, inner, turn)
     grad_re, grad_im = grad[:, :BLOCK], grad[:, BLOCK:]
     for place, other in ((0, 1), (1, 0)):
@@ -200,27 +218,53 @@
         out_ref[:, (2 * place + 1) * PIECE : (2 * place + 2) * PIECE, :] = result[:, :, 128:]
 
 
-def last_kernel(in_ref, grad_ref, key_ref, value_ref, skip_ref, key_out, value_out, taps_out, bias_out):
-    def whole(place):
-        at = 2 * place * PIECE
-        left, right = in_ref[:, at : at + PIECE, :], in_ref[:, at + PIECE : at + 2 * PIECE, :]
-        return jnp.concatenate([left.reshape(WIDTH, 128).T, right.reshape(WIDTH, 128).T], 0)
-
-    grad_mixed = whole(0).astype(f32) + skip_ref[...] * grad_ref[...].astype(f32)
-    key_out[...] = (grad_mixed * value_ref[...].astype(f32)).astype(bf16)
-    value_out[...] = (grad_mixed * key_ref[...].astype(f32)).astype(bf16)
-    taps_out[...] = whole(1)
-    bias = in_ref[:, 4 * PIECE :, :].reshape(WIDTH, 128).astype(f32).T
-    bias_out[...] = bias[0:1] + bias[1:2]
-
-
-def call(kernel, name, outs, *operands):
+def last_kernel(
+    in_ref, grad_ref, key_ref, value_ref, skip_ref,
+    key_hbm, value_hbm, taps_hbm, bias_out, key_out, value_out, taps_out, sems,
+):
+    copies = []
+
+    def send(source, target, half):
+        rows = pl.ds(half * 128, 128)
+        copies.append(pltpu.make_async_copy(source.at[rows], target.at[rows], sems.at[len(copies)]))
+        copies[-1].start()
+
+    for half in range(2):
+        rows = pl.ds(half * 128, 128)
+        at = half * PIECE
+        taps_out[rows, :] = in_ref[:, 2 * PIECE + at : 3 * PIECE + at, :].reshape(WIDTH, 128).T
+        send(taps_out, taps_hbm, half)
+        mixed = in_ref[:, at : at + PIECE, :].reshape(WIDTH, 128).T.astype(f32)
+        mixed = mixed + skip_ref[...] * grad_ref[rows, :].astype(f32)
+        key_out[rows, :] = (mixed * value_ref[rows, :].astype(f32)).astype(bf16)
+        send(key_out, key_hbm, half)
+        value_out[rows, :] = (mixed * key_ref[rows, :].astype(f32)).astype(bf16)
+        send(value_out, value_hbm, half)
+    tail = in_ref[:, 4 * PIECE :, :].astype(f32)
+    tail = jnp.concatenate([tail, pltpu.roll(tail, 126, 2)], 1).reshape(WIDTH, 128).T
+    bias_out[...] = tail[0:1] + tail[1:2]
+    for copy in copies:
+        copy.wait()
+
+
+def call(kernel, name, outs, *operands, hbm_in=(), hbm_out=(), scratch=()):
+    vmem, hbm = pl.BlockSpec(memory_space=pltpu.VMEM), pl.BlockSpec(memory_space=pltpu.HBM)
     return pl.pallas_call(
         kernel,
         name=name,
         out_shape=[jax.ShapeDtypeStruct(shape, kind) for shape, kind in outs],
-        compiler_params=pltpu.CompilerParams(vmem_limit_bytes=40 * 1024 * 1024),
+        in_specs=[hbm if place in hbm_in else vmem for place in range(len(operands))],
+        out_specs=[hbm if place in hbm_out else vmem for place in range(len(outs))],
+        scratch_shapes=list(scratch),
+        compiler_params=pltpu.CompilerParams(vmem_limit_bytes=32 * 1024 * 1024),
     )(*operands)
+
+
+def add_over_chan(sums):
+    sums = sums + lax.ppermute(sums, "chan", [(at, at ^ 1) for at in range(GROUP)])
+    sums = sums + lax.ppermute(sums, "chan", [(at, at ^ 2) for at in range(GROUP)])
+    mirror = [(at, (CHIPS - 1 - at // 2) * 2 + at % 2) for at in range(GROUP)]
+    return sums + lax.ppermute(sums, "chan", mirror)
 
 
 def on_device(gate_feat, key_feat, value_feat, filter_taps, skip_bias, norm_gain, cotangent):
@@ -230,22 +274,44 @@
     turned = ((WIDTH, BLOCK), bf16)
     column = ((WIDTH, 128), f32)
     pieces = ((PARTS, PIECE, BLOCK), bf16)
-
-    (packed,) = call(pack_kernel, "pack", [((PARTS, 2 * PIECE, BLOCK), bf16)], key_feat, value_feat, filter_taps)
+    spectra = ((2, ROWS, 2 * BLOCK), bf16)
+    whole = pltpu.VMEM(*natural)
+
+    (packed,) = call(
+        pack_kernel,
+        "pack",
+        [((PARTS, 2 * PIECE, BLOCK), bf16)],
+        key_feat,
+        value_feat,
+        filter_taps,
+        hbm_in=(0, 1, 2),
+        scratch=[whole, whole, whole, pltpu.SemaphoreType.DMA((3,))],
+    )
     arrived = lax.all_to_all(packed, "seq", 0, 0, tiled=True)
     gate_t, cot_t, skip_t, gain_t = call(
         side_kernel, "side", [turned, turned, column, column], gate_feat, cotangent, skip_row, gain_row
     )
     conv, spec = call(
-        forward_kernel, "forward", [pieces, ((2, ROWS, 2 * BLOCK), bf16)], arrived, enter, leave, inner, turn
+        forward_kernel,
+        "forward",
+        [pieces, spectra],
+        arrived,
+        enter,
+        leave,
+        inner,
+        turn,
+        hbm_out=(1,),
+        scratch=[pltpu.VMEM(*spectra), pltpu.SemaphoreType.DMA((2,))],
     )
     conv = lax.all_to_all(conv, "seq", 0, 0, tiled=True)
     sides = (conv, packed, gate_t, cot_t, skip_t, gain_t)
-    (sums,) = call(sums_kernel, "sums", [((GROUP, 2, BLOCK), f32)], *sides)
-    sums = lax.all_to_all(sums, "chan", 0, 0, tiled=True)
+    (sums,) = call(sums_kernel, "sums", [((2, BLOCK), f32)], *sides)
+    sums = add_over_chan(sums)
     (grad,) = call(grad_kernel, "grad", [pieces], sums, *sides)
     grad_arrived = lax.all_to_all(grad, "seq", 0, 0, tiled=True)
-    normed_out, grad_gate, grad_conv = call(norm_kernel, "norm", [natural] * 3, sums, *sides, grad)
+    normed_out, grad_gate, grad_conv, skip_row = call(
+        norm_kernel, "norm", [natural] * 3 + [((1, WIDTH), f32)], sums, *sides, grad, skip_row
+    )
     (result,) = call(
         backward_kernel,
         "backward",
@@ -268,6 +334,8 @@
         key_feat,
         value_feat,
         skip_row,
+        hbm_out=(0, 1, 2),
+        scratch=[whole, whole, whole, pltpu.SemaphoreType.DMA((6,))],
     )
     return normed_out, grad_gate, grad_key, grad_value, grad_filter, grad_bias[0]
 

time: 90.6 us -> 87.4 us (0.965)
  blocking collectives: 47.2 us -> 32 us
  starting transfers between devices: 7.77 us -> 16.2 us
  waiting for transfers between devices: 19.5 us -> 22.5 us
  Pallas kernels: 8.45 us -> 9.8 us
    all_to_all x1 -> x0, blocking collectives: 15.1 us -> none  [on_device(): sums = lax.all_to_all(sums, 'chan', 0, 0, tiled=True)]
    ppermute x0 -> x3, starting transfers between devices: none -> 8.4 us  [the longest x1 5.05 us: add_over_chan(): return sums + lax.ppermute(sums, 'chan', mirror)]
    ppermute x0 -> x3, waiting for transfers between devices: none -> 4.27 us  [the longest x1 1.56 us: add_over_chan(): lax.ppermute(sums, 'chan', [(at, at ^ 2) for at in range(GROUP)])]
    pallas_call x8, Pallas kernels: 8.45 us -> 9.8 us  [call(): pl.pallas_call(kernel, name=name, out_shape=[jax.ShapeDtypeStruct(shape,...]
    all_to_all x1, waiting for transfers between devices: 11.4 us -> 10.1 us  [on_device(): result = lax.all_to_all(result, 'seq', 0, 0, tiled=True)]
    unnamed x36 -> x34, local copies, waits for them, and re-layouts: 5.64 us -> 4.94 us
  transfers between devices with their start and end apart: 2 -> 5, of which waited for: 2 -> 5; matrix products, arithmetic and copies ran while one was open for 0% -> 0% of each run, Pallas kernels for 2% -> 2%
where the time goes in v2:
time: 87.4 us; the launch traced here: 86.3 us
  blocking collectives  32 us (37%)
  waiting for transfers between devices  22.5 us (26%)
  starting transfers between devices  16.2 us (19%)
  Pallas kernels  9.8 us (11%)
  local copies, waits for them, and re-layouts  4.94 us (6%)
    all_to_all x1, blocking collectives, on_device(): arrived = lax.all_to_all(packed, 'seq', 0, 0, tiled=True)  19 us
    all_to_all x1, blocking collectives, on_device(): grad_arrived = lax.all_to_all(grad, 'seq', 0, 0, tiled=True)  13 us
    all_to_all x1, waiting for transfers between devices, on_device(): result = lax.all_to_all(result, 'seq', 0, 0, tiled=True)  10.1 us
    pallas_call x8, Pallas kernels, call(): pl.pallas_call(kernel, name=name, out_shape=[jax.ShapeDtypeStruct(shape,...  9.8 us
    all_to_all x1, waiting for transfers between devices, on_device(): conv = lax.all_to_all(conv, 'seq', 0, 0, tiled=True)  8.12 us
    ppermute x1, starting transfers between devices, add_over_chan(): return sums + lax.ppermute(sums, 'chan', mirror)  5.05 us
    unnamed x34, local copies, waits for them, and re-layouts  4.94 us
    all_to_all x1, starting transfers between devices, on_device(): result = lax.all_to_all(result, 'seq', 0, 0, tiled=True)  3.9 us
  transfers between devices with their start and end apart: 5, of which 5 were waited for; matrix products, arithmetic and copies ran while one was open for 0% of the time, Pallas kernels for 2%

profile of v2, /device:TPU:0, one launch (start us, length us, event | category | flops | bytes accessed | tf_op | source)
XLA Modules:
  0.0 86.3 jit_solution(5237945445741851729)
XLA Ops:
  0.6 0.0 copy-start
  0.6 0.0 copy-start.1
  0.7 0.0 copy-start.5
  0.7 1.0 %copy-done.5 = bf16[256,512]{1,0:T(8,128)(2,1)S(1)} copy-done((bf16[256,512]{1,0:T(8,128)(2,1)S(1)}, bf16[256,512]{1,0:T(8,128)(2,1)}, u32[]{:S(2)}) %copy-start.5) | copy-done | bytes 262168
  1.7 0.0 copy-start.7
  1.7 0.9 %copy-done.7 = bf16[256,512]{1,0:T(8,128)(2,1)S(1)} copy-done((bf16[256,512]{1,0:T(8,128)(2,1)S(1)}, bf16[256,512]{1,0:T(8,128)(2,1)}, u32[]{:S(2)}) %copy-start.7) | copy-done | bytes 262168
  2.6 0.0 copy-start.12
  2.6 0.9 %copy-done.12 = bf16[256,512]{1,0:T(8,128)(2,1)S(1)} copy-done((bf16[256,512]{1,0:T(8,128)(2,1)S(1)}, bf16[256,512]{1,0:T(8,128)(2,1)}, u32[]{:S(2)}) %copy-start.12) | copy-done | bytes 262168
  3.6 0.0 copy-start.9
  3.6 0.0 copy-start.10
  3.6 0.3 pack.1.pack_ref
  3.9 19.0 %all_to_all.20.in_ref.pack_ref = bf16[32,32,256]{2,1,0:T(8,128)(2,1)S(1)} all-to-all(bf16[32,32,256]{2,1,0:T(8,128)(2,1)S(1)} %pack.1.pack_ref), channel_id=1, replica_groups=mesh['seq'=32,'chan'=8] {'seq'}, dimensions={0} | all-to-all | bytes 1048576 | tf_op jit(solution)/shard_map/all_to_all | solution.py:290
  23.0 0.0 copy-done
  23.0 0.0 copy-done.1
  23.0 0.0 copy-done.9
  23.0 0.0 copy-done.10
  23.0 0.0 copy-start.13
  23.0 0.0 copy-start.15
  23.0 0.0 copy-start.16
  23.0 3.1 %forward.1 = (bf16[32,16,256]{2,1,0:T(8,128)(2,1)}, bf16[2,528,512]{2,1,0:T(8,128)(2,1)S(1)}) custom-call(bf16[32,32,256]{2,1,0:T(8,128)(2,1)S(1)} %all_to_all.20.in_ref.pack_ref, bf16[512,256]{1,0:T(8,128)(2,1)S(1)} %copy-done.10, bf16[256,512]{1,0:T(8,128)(2,1)S(1)} %copy-done.9, bf16[512,512]{1,0:T(8,128)(2,1)S(1)} %copy-done.1, f32[2,264,256]{2,1,0:T(8,128)S(1)} %copy-done), custom_call_target="tpu_custom_call" | custom-call | tf_op jit(solution)/shard_map/forward/pallas_call | solution.py:252
  26.1 0.0 copy-start.3
  26.1 1.0 %copy-done.3 = bf16[2,528,512]{2,1,0:T(8,128)(2,1)} copy-done((bf16[2,528,512]{2,1,0:T(8,128)(2,1)}, bf16[2,528,512]{2,1,0:T(8,128)(2,1)S(1)}, u32[]{:S(2)}) %copy-start.3) | copy-done | bytes 1081368
  27.1 3.9 %all-to-all-start.1 = ((bf16[32,16,256]{2,1,0:T(8,128)(2,1)}), bf16[32,16,256]{2,1,0:T(8,128)(2,1)S(1)}, u32[]{:S(2)}, u32[]{:S(2)}) async-start(bf16[32,16,256]{2,1,0:T(8,128)(2,1)} %get-tuple-element.20), calls=%async_computation.1 | async-start | bytes 524288 | tf_op jit(solution)/shard_map/all_to_all | solution.py:306
  31.0 0.0 copy-done.13
  31.0 0.0 copy-done.15
  31.0 0.0 copy-done.16
  31.0 0.0 copy-start.14
  31.0 0.9 %copy-done.14 = bf16[256,512]{1,0:T(8,128)(2,1)S(1)} copy-done((bf16[256,512]{1,0:T(8,128)(2,1)S(1)}, bf16[256,512]{1,0:T(8,128)(2,1)}, u32[]{:S(2)}) %copy-start.14) | copy-done | bytes 262168
  32.0 0.3 side.1
  32.3 8.1 %all-to-all-done.1.conv_ref = bf16[32,16,256]{2,1,0:T(8,128)(2,1)S(1)} async-done(((bf16[32,16,256]{2,1,0:T(8,128)(2,1)}), bf16[32,16,256]{2,1,0:T(8,128)(2,1)S(1)}, u32[]{:S(2)}, u32[]{:S(2)}) %all-to-all-start.1) | async-done | bytes 262176 | tf_op jit(solution)/shard_map/all_to_all | solution.py:306
  40.4 0.3 sums.1
  40.7 0.1 collective-permute-start
  40.8 1.1 %collective-permute-done = f32[2,256]{1,0:T(2,128)S(1)} collective-permute-done((f32[2,256]{1,0:T(2,128)S(1)}, f32[2,256]{1,0:T(2,128)S(1)}, u32[]{:S(2)}, u32[]{:S(2)}) %collective-permute-start) | collective-permute-done | bytes 2080 | tf_op jit(solution)/shard_map/ppermute | solution.py:264
  42.0 3.3 %collective-permute-start.1 = (f32[2,256]{1,0:T(2,128)S(1)}, f32[2,256]{1,0:T(2,128)S(1)}, u32[]{:S(2)}, u32[]{:S(2)}) collective-permute-start(f32[2,256]{1,0:T(2,128)S(1)} %add.9), channel_id=1, source_target_pairs={{0,2},{1,3},{2,0},{3,1},{4,6},{5,7},{6,4},{7,5},{8,10},{9,11},{10,... | collective-permute-start | bytes 6152 | tf_op jit(solution)/shard_map/ppermute | solution.py:265
  45.2 1.6 %collective-permute-done.1 = f32[2,256]{1,0:T(2,128)S(1)} collective-permute-done((f32[2,256]{1,0:T(2,128)S(1)}, f32[2,256]{1,0:T(2,128)S(1)}, u32[]{:S(2)}, u32[]{:S(2)}) %collective-permute-start.1) | collective-permute-done | bytes 2080 | tf_op jit(solution)/shard_map/ppermute | solution.py:265
  46.8 5.0 %collective-permute-start.2 = (f32[2,256]{1,0:T(2,128)S(1)}, f32[2,256]{1,0:T(2,128)S(1)}, u32[]{:S(2)}, u32[]{:S(2)}) collective-permute-start(f32[2,256]{1,0:T(2,128)S(1)} %add.10), channel_id=1, source_target_pairs={{0,6},{1,7},{2,4},{3,5},{4,2},{5,3},{6,0},{7,1},{8,14},{9,15},{10,... | collective-permute-start | bytes 6152 | tf_op jit(solution)/shard_map/ppermute | solution.py:267
  51.9 1.6 %collective-permute-done.2 = f32[2,256]{1,0:T(2,128)S(1)} collective-permute-done((f32[2,256]{1,0:T(2,128)S(1)}, f32[2,256]{1,0:T(2,128)S(1)}, u32[]{:S(2)}, u32[]{:S(2)}) %collective-permute-start.2) | collective-permute-done | bytes 2080 | tf_op jit(solution)/shard_map/ppermute | solution.py:267
  53.4 0.0 copy-start.2
  53.4 0.0 copy-start.4
  53.4 0.0 copy-start.11
  53.4 0.2 grad.1.grad_ref
  53.7 13.0 %all_to_all.21.in_ref = bf16[32,16,256]{2,1,0:T(8,128)(2,1)S(1)} all-to-all(bf16[32,16,256]{2,1,0:T(8,128)(2,1)S(1)} %grad.1.grad_ref), channel_id=1, replica_groups=mesh['seq'=32,'chan'=8] {'seq'}, dimensions={0} | all-to-all | bytes 524288 | tf_op jit(solution)/shard_map/all_to_all | solution.py:311
  66.7 0.0 copy-done.2
  66.7 0.0 copy-done.4
  66.7 0.0 copy-done.11
  66.7 2.8 %backward.1 = bf16[32,72,128]{2,1,0:T(8,128)(2,1)} custom-call(bf16[32,16,256]{2,1,0:T(8,128)(2,1)S(1)} %all_to_all.21.in_ref, bf16[32,32,256]{2,1,0:T(8,128)(2,1)S(1)} %all_to_all.20.in_ref.pack_ref, bf16[2,528,512]{2,1,0:T(8,128)(2,1)S(1)} %copy-done.4, bf16[512,256]{1,0:T(8,128)(2,1)S(1)} %copy-done.11, bf16[256,512]{1,0:T(8,128)(2,1)S(1)} %copy-done.9, ...), custom_call_target="tpu_custom_call" | custom-call | tf_op jit(solution)/shard_map/backward/pallas_call | solution.py:252
  69.5 3.9 %all-to-all-start.3 = ((bf16[32,72,128]{2,1,0:T(8,128)(2,1)}), bf16[32,72,128]{2,1,0:T(8,128)(2,1)S(1)}, u32[]{:S(2)}, u32[]{:S(2)}) async-start(bf16[32,72,128]{2,1,0:T(8,128)(2,1)} %backward.1), calls=%async_computation.3 | async-start | bytes 1179648 | tf_op jit(solution)/shard_map/all_to_all | solution.py:327
  73.4 0.0 copy-start.6
  73.4 0.0 copy-start.8
  73.4 1.1 %norm.1 = (bf16[256,512]{1,0:T(8,128)(2,1)}, bf16[256,512]{1,0:T(8,128)(2,1)}, bf16[256,512]{1,0:T(8,128)(2,1)S(1)}, f32[1,512]{1,0:T(1,128)S(1)}) custom-call(f32[2,256]{1,0:T(2,128)S(1)} %add.11.sums_ref, bf16[32,16,256]{2,1,0:T(8,128)(2,1)S(1)} %all-to-all-done.1.conv_ref, bf16[32,32,256]{2,1,0:T(8,128)(2,1)S(1)} %pack.1.pack_ref, ...), custom_call_target="tpu_custom_call" | custom-call | tf_op jit(solution)/shard_map/norm/pallas_call | solution.py:252
  74.5 10.1 %all-to-all-done.3.in_ref = bf16[32,72,128]{2,1,0:T(8,128)(2,1)S(1)} async-done(((bf16[32,72,128]{2,1,0:T(8,128)(2,1)}), bf16[32,72,128]{2,1,0:T(8,128)(2,1)S(1)}, u32[]{:S(2)}, u32[]{:S(2)}) %all-to-all-start.3) | async-done | bytes 589856 | tf_op jit(solution)/shard_map/all_to_all | solution.py:327
  84.6 0.0 copy-done.6
  84.6 0.0 copy-done.8
  84.6 1.6 %last.1 = (bf16[256,512]{1,0:T(8,128)(2,1)}, bf16[256,512]{1,0:T(8,128)(2,1)}, bf16[256,512]{1,0:T(8,128)(2,1)}, f32[1,512]{1,0:T(1,128)}) custom-call(bf16[32,72,128]{2,1,0:T(8,128)(2,1)S(1)} %all-to-all-done.3.in_ref, bf16[256,512]{1,0:T(8,128)(2,1)S(1)} %get-tuple-element.28.grad_ref, bf16[256,512]{1,0:T(8,128)(2,1)S(1)} %copy-done.6, ...), custom_call_target="tpu_custom_call" | custom-call | tf_op jit(solution)/shard_map/last/pallas_call | solution.py:252
  (3 shorter events, 0.0 us)
Async XLA Ops:
  0.6 22.3 %copy-start = (f32[2,264,256]{2,1,0:T(8,128)S(1)}, f32[2,264,256]{2,1,0:T(8,128)}, u32[]{:S(2)}) copy-start(f32[2,264,256]{2,1,0:T(8,128)} %constant.11.clone.turn_ref) | copy-start | bytes 1622020
  0.6 22.3 %copy-start.1 = (bf16[512,512]{1,0:T(8,128)(2,1)S(1)}, bf16[512,512]{1,0:T(8,128)(2,1)}, u32[]{:S(2)}) copy-start(bf16[512,512]{1,0:T(8,128)(2,1)} %constant.10.clone.inner_ref) | copy-start | bytes 1572868
  0.7 1.0 %copy-start.5 = (bf16[256,512]{1,0:T(8,128)(2,1)S(1)}, bf16[256,512]{1,0:T(8,128)(2,1)}, u32[]{:S(2)}) copy-start(bf16[256,512]{1,0:T(8,128)(2,1)} %key_ref.1) | copy-start | bytes 786436
  1.7 0.9 %copy-start.7 = (bf16[256,512]{1,0:T(8,128)(2,1)S(1)}, bf16[256,512]{1,0:T(8,128)(2,1)}, u32[]{:S(2)}) copy-start(bf16[256,512]{1,0:T(8,128)(2,1)} %value_ref.1) | copy-start | bytes 786436
  2.6 0.9 %copy-start.12 = (bf16[256,512]{1,0:T(8,128)(2,1)S(1)}, bf16[256,512]{1,0:T(8,128)(2,1)}, u32[]{:S(2)}) copy-start(bf16[256,512]{1,0:T(8,128)(2,1)} %taps_hbm.1) | copy-start | bytes 786436
  3.6 19.4 %copy-start.9 = (bf16[256,512]{1,0:T(8,128)(2,1)S(1)}, bf16[256,512]{1,0:T(8,128)(2,1)}, u32[]{:S(2)}) copy-start(bf16[256,512]{1,0:T(8,128)(2,1)} %constant.9.clone.leave_ref) | copy-start | bytes 786436
  3.6 19.4 %copy-start.10 = (bf16[512,256]{1,0:T(8,128)(2,1)S(1)}, bf16[512,256]{1,0:T(8,128)(2,1)}, u32[]{:S(2)}) copy-start(bf16[512,256]{1,0:T(8,128)(2,1)} %constant.8.clone.enter_ref) | copy-start | bytes 786436
  23.0 8.0 %copy-start.13 = (bf16[256,512]{1,0:T(8,128)(2,1)S(1)}, bf16[256,512]{1,0:T(8,128)(2,1)}, u32[]{:S(2)}) copy-start(bf16[256,512]{1,0:T(8,128)(2,1)} %gate_ref.1) | copy-start | bytes 786436
  23.0 8.0 %copy-start.15 = (f32[512]{0:T(512)S(1)}, f32[512]{0:T(512)}, u32[]{:S(2)}) copy-start(f32[512]{0:T(512)} %param.15) | copy-start | bytes 6148
  23.0 8.0 %copy-start.16 = (f32[512]{0:T(512)S(1)}, f32[512]{0:T(512)}, u32[]{:S(2)}) copy-start(f32[512]{0:T(512)} %param.16) | copy-start | bytes 6148
  26.1 1.0 %copy-start.3 = (bf16[2,528,512]{2,1,0:T(8,128)(2,1)}, bf16[2,528,512]{2,1,0:T(8,128)(2,1)S(1)}, u32[]{:S(2)}) copy-start(bf16[2,528,512]{2,1,0:T(8,128)(2,1)S(1)} %get-tuple-element.27.spec_ref) | copy-start | bytes 3244036
  27.1 13.3 %all-to-all-start.1 = ((bf16[32,16,256]{2,1,0:T(8,128)(2,1)}), bf16[32,16,256]{2,1,0:T(8,128)(2,1)S(1)}, u32[]{:S(2)}, u32[]{:S(2)}) async-start(bf16[32,16,256]{2,1,0:T(8,128)(2,1)} %get-tuple-element.20), calls=%async_computation.1 | async-start | bytes 524288 | tf_op jit(solution)/shard_map/all_to_all | solution.py:306
  31.0 1.0 %copy-start.14 = (bf16[256,512]{1,0:T(8,128)(2,1)S(1)}, bf16[256,512]{1,0:T(8,128)(2,1)}, u32[]{:S(2)}) copy-start(bf16[256,512]{1,0:T(8,128)(2,1)} %cot_ref.1) | copy-start | bytes 786436
  40.7 1.2 %collective-permute-start = (f32[2,256]{1,0:T(2,128)S(1)}, f32[2,256]{1,0:T(2,128)S(1)}, u32[]{:S(2)}, u32[]{:S(2)}) collective-permute-start(f32[2,256]{1,0:T(2,128)S(1)} %sums.1), channel_id=1, source_target_pairs={{0,1},{1,0},{2,3},{3,2},{4,5},{5,4},{6,7},{7,6},{8,9},{9,8},{10,11... | collective-permute-start | bytes 6152 | tf_op jit(solution)/shard_map/ppermute | solution.py:264
  42.0 4.8 %collective-permute-start.1 = (f32[2,256]{1,0:T(2,128)S(1)}, f32[2,256]{1,0:T(2,128)S(1)}, u32[]{:S(2)}, u32[]{:S(2)}) collective-permute-start(f32[2,256]{1,0:T(2,128)S(1)} %add.9), channel_id=1, source_target_pairs={{0,2},{1,3},{2,0},{3,1},{4,6},{5,7},{6,4},{7,5},{8,10},{9,11},{10,... | collective-permute-start | bytes 6152 | tf_op jit(solution)/shard_map/ppermute | solution.py:265
  46.8 6.6 %collective-permute-start.2 = (f32[2,256]{1,0:T(2,128)S(1)}, f32[2,256]{1,0:T(2,128)S(1)}, u32[]{:S(2)}, u32[]{:S(2)}) collective-permute-start(f32[2,256]{1,0:T(2,128)S(1)} %add.10), channel_id=1, source_target_pairs={{0,6},{1,7},{2,4},{3,5},{4,2},{5,3},{6,0},{7,1},{8,14},{9,15},{10,... | collective-permute-start | bytes 6152 | tf_op jit(solution)/shard_map/ppermute | solution.py:267
  53.4 13.3 %copy-start.2 = (bf16[512,512]{1,0:T(8,128)(2,1)S(1)}, bf16[512,512]{1,0:T(8,128)(2,1)}, u32[]{:S(2)}) copy-start(bf16[512,512]{1,0:T(8,128)(2,1)} %constant.10.clone.inner_ref) | copy-start | bytes 1572868
  53.4 13.3 %copy-start.4 = (bf16[2,528,512]{2,1,0:T(8,128)(2,1)S(1)}, bf16[2,528,512]{2,1,0:T(8,128)(2,1)}, u32[]{:S(2)}) copy-start(bf16[2,528,512]{2,1,0:T(8,128)(2,1)} %copy-done.3) | copy-start | bytes 3244036
  53.4 13.3 %copy-start.11 = (bf16[512,256]{1,0:T(8,128)(2,1)S(1)}, bf16[512,256]{1,0:T(8,128)(2,1)}, u32[]{:S(2)}) copy-start(bf16[512,256]{1,0:T(8,128)(2,1)} %constant.8.clone.enter_ref) | copy-start | bytes 786436
  69.5 15.1 %all-to-all-start.3 = ((bf16[32,72,128]{2,1,0:T(8,128)(2,1)}), bf16[32,72,128]{2,1,0:T(8,128)(2,1)S(1)}, u32[]{:S(2)}, u32[]{:S(2)}) async-start(bf16[32,72,128]{2,1,0:T(8,128)(2,1)} %backward.1), calls=%async_computation.3 | async-start | bytes 1179648 | tf_op jit(solution)/shard_map/all_to_all | solution.py:327
  73.4 11.2 %copy-start.6 = (bf16[256,512]{1,0:T(8,128)(2,1)S(1)}, bf16[256,512]{1,0:T(8,128)(2,1)}, u32[]{:S(2)}) copy-start(bf16[256,512]{1,0:T(8,128)(2,1)} %key_ref.1) | copy-start | bytes 786436
  73.4 11.2 %copy-start.8 = (bf16[256,512]{1,0:T(8,128)(2,1)S(1)}, bf16[256,512]{1,0:T(8,128)(2,1)}, u32[]{:S(2)}) copy-start(bf16[256,512]{1,0:T(8,128)(2,1)} %value_ref.1) | copy-start | bytes 786436

commit v3 on v1

--- a/solution.py
+++ b/solution.py
@@ -1,5 +1,3 @@
-import functools
-
 import jax
 import jax.numpy as jnp
 import numpy as np
@@ -24,7 +22,8 @@
 SPAN = 2 * PARTS
 BINS = PARTS + 1
 ROWS = BINS * PIECE
-TAIL = 16
+TAIL = 8
+CHIPS = GROUP // 2
 
 
 def tables():
@@ -37,16 +36,23 @@
     weight = np.where((low == 0) | (low == PARTS), 1.0, 2.0)[:, None] / 4
     leave = np.kron(np.concatenate([cosine * weight, (sine * weight)[: PARTS - 1]], 0).T, eye)
     turn = 2 * np.pi * (low[:, None] * inside[None, :] % FULL) / FULL
-    turn = np.stack([np.repeat(np.cos(turn), HALF, 0), np.repeat(-np.sin(turn), HALF, 0)])
+    turn = np.stack([np.cos(turn), -np.sin(turn)])
     inner = 2 * np.pi * (inside[:, None] * inside[None, :] % BLOCK) / BLOCK
     cosine, sine = np.cos(inner) / 16, -np.sin(inner) / 16
     inner = np.block([[cosine, sine], [-sine, cosine]])
-    return (
-        enter.astype(np.float32).astype(bf16),
-        leave.astype(np.float32).astype(bf16),
-        inner.astype(np.float32).astype(bf16),
-        turn.astype(np.float32),
-    )
+    half = SPAN * HALF // 2
+    steps = np.concatenate([inner, leave, np.concatenate([enter[:half], enter[half:]], 1)], 0)
+    return steps.astype(np.float32).astype(bf16), turn.astype(np.float32)
+
+
+def open_tables(steps_ref, turn_ref):
+    inner, leave, last = 2 * BLOCK, 3 * BLOCK, 4 * BLOCK
+    enter = jnp.concatenate([steps_ref[leave:last, :BLOCK], steps_ref[leave:last, BLOCK:]], 0)
+    turn = [
+        jnp.broadcast_to(turn_ref[part][:, None, :], (BINS, HALF, BLOCK)).reshape(BINS * HALF, BLOCK)
+        for part in range(2)
+    ]
+    return enter, steps_ref[inner:leave, :], steps_ref[:inner, :], turn
 
 
 def dot(first, second):
@@ -106,26 +112,36 @@
     return rows.reshape(PARTS, PIECE, BLOCK)
 
 
-def pack_kernel(key_ref, value_ref, taps_ref, out_ref):
-    mixed = (key_ref[...].astype(f32) * value_ref[...].astype(f32)).astype(bf16)
-    out_ref[:, :PIECE, :] = cut(mixed.T)
-    out_ref[:, PIECE:, :] = cut(taps_ref[...].T)
-
-
-def side_kernel(gate_ref, cot_ref, skip_ref, gain_ref, gate_out, cot_out, skip_out, gain_out):
+def pack_kernel(key_hbm, value_hbm, taps_hbm, out_hbm, key_ref, value_ref, taps_ref, out_ref, sems):
+    width, parts = WIDTH // 2, PARTS // 2
+    loads, stores = [], []
+    for half in range(2):
+        columns = pl.ds(half * width, width)
+        for source, target in ((key_hbm, key_ref), (value_hbm, value_ref), (taps_hbm, taps_ref)):
+            loads.append(pltpu.make_async_copy(source.at[:, columns], target.at[:, columns], sems.at[len(loads)]))
+            loads[-1].start()
+    for half in range(2):
+        columns, owners = pl.ds(half * width, width), pl.ds(half * parts, parts)
+        loads[3 * half].wait()
+        loads[3 * half + 1].wait()
+        mixed = key_ref[:, columns].astype(f32) * value_ref[:, columns].astype(f32)
+        out_ref[owners, :PIECE, :] = mixed.astype(bf16).T.reshape(parts, PIECE, BLOCK)
+        loads[3 * half + 2].wait()
+        out_ref[owners, PIECE:, :] = taps_ref[:, columns].T.reshape(parts, PIECE, BLOCK)
+        stores.append(pltpu.make_async_copy(out_ref.at[owners], out_hbm.at[owners], sems.at[6 + half]))
+        stores[-1].start()
+    for store in stores:
+        store.wait()
+
+
+def forward_kernel(
+    in_ref, steps_ref, turn_ref, gate_ref, cot_ref, out_ref, gate_out, cot_out
+):
     gate_out[...] = gate_ref[...].T
     cot_out[...] = cot_ref[...].T
-    skip_out[...] = jnp.broadcast_to(skip_ref[...], (128, WIDTH)).T
-    gain_out[...] = jnp.broadcast_to(gain_ref[...], (128, WIDTH)).T
-
-
-def forward_kernel(in_ref, enter_ref, leave_ref, inner_ref, turn_ref, out_ref, spec_ref):
-    enter, leave, inner = enter_ref[...], leave_ref[...], inner_ref[...]
-    turn = (turn_ref[0], turn_ref[1])
+    enter, leave, inner, turn = open_tables(steps_ref, turn_ref)
     first = spectrum(in_ref[:, :PIECE, :], enter, inner, turn)
-    spec_ref[0] = first.astype(bf16)
     second = spectrum(in_ref[:, PIECE:, :], enter, inner, turn)
-    spec_ref[1] = second.astype(bf16)
     first_re, first_im = first[:, :BLOCK], first[:, BLOCK:]
     second_re, second_im = second[:, :BLOCK], second[:, BLOCK:]
     real = first_re * second_re - first_im * second_im
@@ -133,28 +149,35 @@
     out_ref[...] = invert(real, imag, leave, inner, turn).astype(bf16)
 
 
-def wide_twice(column):
-    return jnp.concatenate([column, column], 1)
+def spectra_kernel(in_ref, steps_ref, turn_ref, after_ref, spec_ref):
+    enter, _, inner, turn = open_tables(steps_ref, turn_ref)
+    for place in range(2):
+        signal = in_ref[:, place * PIECE : (place + 1) * PIECE, :]
+        spec_ref[place] = spectrum(signal, enter, inner, turn).astype(bf16)
+
+
+def column(row_ref):
+    turned = jnp.broadcast_to(row_ref[...], (128, WIDTH)).T
+    return jnp.concatenate([turned, turned], 1)
 
 
 def gate_parts(conv_ref, pack_ref, gate_ref, skip_ref):
     mixed = flat(pack_ref[:, :PIECE, :]).astype(f32)
-    full = flat(conv_ref[...]).astype(f32) + wide_twice(skip_ref[...]) * mixed
+    full = flat(conv_ref[...]).astype(f32) + column(skip_ref) * mixed
     gate = gate_ref[...].astype(f32)
     return full, gate, gate * full
 
 
 def sums_kernel(conv_ref, pack_ref, gate_ref, cot_ref, skip_ref, gain_ref, out_ref):
     _, _, gated = gate_parts(conv_ref, pack_ref, gate_ref, skip_ref)
-    scaled = cot_ref[...].astype(f32) * wide_twice(gain_ref[...])
+    scaled = cot_ref[...].astype(f32) * column(gain_ref)
     squares = jnp.sum(gated * gated, axis=0, keepdims=True)
     inner = jnp.sum(scaled * gated, axis=0, keepdims=True)
-    both = jnp.concatenate([squares, inner], 0)
-    out_ref[...] = jnp.broadcast_to(both[None], (GROUP, 2, BLOCK))
+    out_ref[...] = jnp.concatenate([squares, inner], 0)
 
 
 def norm_parts(sums_ref):
-    sums = jnp.sum(sums_ref[...], axis=0)
+    sums = sums_ref[...]
     inv_rms = lax.rsqrt(sums[0:1] / D + epsilon)
     return inv_rms, inv_rms * inv_rms * inv_rms * sums[1:2] / D
 
@@ -162,33 +185,38 @@
 def grad_kernel(sums_ref, conv_ref, pack_ref, gate_ref, cot_ref, skip_ref, gain_ref, out_ref):
     inv_rms, pull = norm_parts(sums_ref)
     _, gate, gated = gate_parts(conv_ref, pack_ref, gate_ref, skip_ref)
-    scaled = cot_ref[...].astype(f32) * wide_twice(gain_ref[...])
+    scaled = cot_ref[...].astype(f32) * column(gain_ref)
     grad_gated = inv_rms * scaled - gated * pull
     out_ref[...] = cut((grad_gated * gate).astype(bf16))
 
 
 def norm_kernel(
-    sums_ref, conv_ref, pack_ref, gate_ref, cot_ref, skip_ref, gain_ref, grad_ref, normed_out, gate_out, grad_out
+    sums_ref, conv_ref, pack_ref, gate_ref, cot_ref, skip_ref, gain_ref,
+    normed_out, gate_out, grad_out, skip_out,
 ):
     inv_rms, pull = norm_parts(sums_ref)
-    full, _, gated = gate_parts(conv_ref, pack_ref, gate_ref, skip_ref)
-    gain = wide_twice(gain_ref[...])
+    full, gate, gated = gate_parts(conv_ref, pack_ref, gate_ref, skip_ref)
+    gain = column(gain_ref)
     normed_out[...] = (gated * inv_rms * gain).astype(bf16).T
     grad_gated = inv_rms * (cot_ref[...].astype(f32) * gain) - gated * pull
     gate_out[...] = (grad_gated * full).astype(bf16).T
-    grad_out[...] = flat(grad_ref[...]).T
-
-
-def backward_kernel(in_ref, pack_ref, spec_ref, enter_ref, leave_ref, inner_ref, turn_ref, out_ref):
-    enter, leave, inner = enter_ref[...], leave_ref[...], inner_ref[...]
-    turn = (turn_ref[0], turn_ref[1])
+    grad_out[...] = (grad_gated * gate).astype(bf16).T
+    skip_out[...] = skip_ref[...]
+
+
+def backward_kernel(
+    in_ref, pack_ref, spec_ref, steps_ref, turn_ref, after_ref, out_ref
+):
+    enter, leave, inner, turn = open_tables(steps_ref, turn_ref)
     grad = in_ref[...]
     bias = jnp.sum(grad.astype(f32) * pack_ref[:, :PIECE, :].astype(f32), axis=0)
     bias = jnp.sum(bias, axis=1, keepdims=True)
     high = bias.astype(bf16).astype(f32)
-    lane = lax.broadcasted_iota(jnp.int32, (PIECE, 128), 1)
-    bias = jnp.where(lane == 0, high, jnp.where(lane == 1, bias - high, 0.0)).astype(bf16)
-    out_ref[:, 4 * PIECE :, :] = jnp.broadcast_to(bias[None], (PARTS, TAIL, 128))
+    lane = lax.broadcasted_iota(jnp.int32, (TAIL, 128), 1)
+    tail = jnp.zeros((TAIL, 128), f32)
+    for at, part in enumerate((high[:HALF], (bias - high)[:HALF], high[HALF:], (bias - high)[HALF:])):
+        tail = jnp.where(lane == at, part, tail)
+    out_ref[:, 4 * PIECE :, :] = jnp.broadcast_to(tail.astype(bf16)[None], (PARTS, TAIL, 128))
     grad = spectrum(grad, enter, inner, turn)
     grad_re, grad_im = grad[:, :BLOCK], grad[:, BLOCK:]
     for place, other in ((0, 1), (1, 0)):
@@ -210,42 +238,73 @@
     key_out[...] = (grad_mixed * value_ref[...].astype(f32)).astype(bf16)
     value_out[...] = (grad_mixed * key_ref[...].astype(f32)).astype(bf16)
     taps_out[...] = whole(1)
-    bias = in_ref[:, 4 * PIECE :, :].reshape(WIDTH, 128).astype(f32).T
-    bias_out[...] = bias[0:1] + bias[1:2]
-
-
-def call(kernel, name, outs, *operands):
+    tail = in_ref[:, 4 * PIECE :, :].astype(f32)
+    tail = jnp.concatenate([tail, pltpu.roll(tail, 126, 2)], 1).reshape(WIDTH, 128).T
+    bias_out[...] = tail[0:1] + tail[1:2]
+
+
+def call(kernel, name, outs, *operands, hbm_in=(), hbm_out=(), scratch=(), grant=32):
+    vmem, hbm = pl.BlockSpec(memory_space=pltpu.VMEM), pl.BlockSpec(memory_space=pltpu.HBM)
     return pl.pallas_call(
         kernel,
         name=name,
         out_shape=[jax.ShapeDtypeStruct(shape, kind) for shape, kind in outs],
-        compiler_params=pltpu.CompilerParams(vmem_limit_bytes=40 * 1024 * 1024),
+        in_specs=[hbm if place in hbm_in else vmem for place in range(len(operands))],
+        out_specs=[hbm if place in hbm_out else vmem for place in range(len(outs))],
+        scratch_shapes=list(scratch),
+        compiler_params=pltpu.CompilerParams(vmem_limit_bytes=grant * 1024 * 1024),
     )(*operands)
 
 
+def add_over_chan(sums):
+    sums = sums + lax.ppermute(sums, "chan", [(at, at ^ 1) for at in range(GROUP)])
+    sums = sums + lax.ppermute(sums, "chan", [(at, at ^ 2) for at in range(GROUP)])
+    mirror = [(at, (CHIPS - 1 - at // 2) * 2 + at % 2) for at in range(GROUP)]
+    return sums + lax.ppermute(sums, "chan", mirror)
+
+
 def on_device(gate_feat, key_feat, value_feat, filter_taps, skip_bias, norm_gain, cotangent):
-    enter, leave, inner, turn = (jnp.asarray(table) for table in tables())
+    steps, turn = (jnp.asarray(table) for table in tables())
     skip_row, gain_row = skip_bias[None, :], norm_gain[None, :]
     natural = ((BLOCK, WIDTH), bf16)
     turned = ((WIDTH, BLOCK), bf16)
-    column = ((WIDTH, 128), f32)
     pieces = ((PARTS, PIECE, BLOCK), bf16)
-
-    (packed,) = call(pack_kernel, "pack", [((PARTS, 2 * PIECE, BLOCK), bf16)], key_feat, value_feat, filter_taps)
+    spectra = ((2, ROWS, 2 * BLOCK), bf16)
+    whole = pltpu.VMEM(*natural)
+
+    (packed,) = call(
+        pack_kernel,
+        "pack",
+        [((PARTS, 2 * PIECE, BLOCK), bf16)],
+        key_feat,
+        value_feat,
+        filter_taps,
+        hbm_in=(0, 1, 2),
+        hbm_out=(0,),
+        scratch=[whole, whole, whole, pltpu.VMEM((PARTS, 2 * PIECE, BLOCK), bf16), pltpu.SemaphoreType.DMA((8,))],
+        grant=63,
+    )
     arrived = lax.all_to_all(packed, "seq", 0, 0, tiled=True)
-    gate_t, cot_t, skip_t, gain_t = call(
-        side_kernel, "side", [turned, turned, column, column], gate_feat, cotangent, skip_row, gain_row
-    )
-    conv, spec = call(
-        forward_kernel, "forward", [pieces, ((2, ROWS, 2 * BLOCK), bf16)], arrived, enter, leave, inner, turn
+    conv, gate_t, cot_t = call(
+        forward_kernel,
+        "forward",
+        [pieces, turned, turned],
+        arrived,
+        steps,
+        turn,
+        gate_feat,
+        cotangent,
     )
     conv = lax.all_to_all(conv, "seq", 0, 0, tiled=True)
-    sides = (conv, packed, gate_t, cot_t, skip_t, gain_t)
-    (sums,) = call(sums_kernel, "sums", [((GROUP, 2, BLOCK), f32)], *sides)
-    sums = lax.all_to_all(sums, "chan", 0, 0, tiled=True)
+    sides = (conv, packed, gate_t, cot_t, skip_row, gain_row)
+    (sums,) = call(sums_kernel, "sums", [((2, BLOCK), f32)], *sides)
+    sums = add_over_chan(sums)
     (grad,) = call(grad_kernel, "grad", [pieces], sums, *sides)
     grad_arrived = lax.all_to_all(grad, "seq", 0, 0, tiled=True)
-    normed_out, grad_gate, grad_conv = call(norm_kernel, "norm", [natural] * 3, sums, *sides, grad)
+    normed_out, grad_gate, grad_conv, skip_row = call(
+        norm_kernel, "norm", [natural] * 3 + [((1, WIDTH), f32)], sums, *sides
+    )
+    (spec,) = call(spectra_kernel, "spectra", [spectra], arrived, steps, turn, skip_row)
     (result,) = call(
         backward_kernel,
         "backward",
@@ -253,10 +312,9 @@
         grad_arrived,
         arrived,
         spec,
-        enter,
-        leave,
-        inner,
+        steps,
         turn,
+        skip_row,
     )
     result = lax.all_to_all(result, "seq", 0, 0, tiled=True)
     grad_key, grad_value, grad_filter, grad_bias = call(

time: 90.6 us -> 83.3 us (0.919)
  waiting for transfers between devices: 19.5 us -> 10.6 us
  local copies, waits for them, and re-layouts: 5.64 us -> 0.76 us
  starting transfers between devices: 7.77 us -> 12.3 us
  Pallas kernels: 8.45 us -> 10.8 us
    all_to_all x2 -> x1, waiting for transfers between devices: 19.5 us -> 6.28 us  [on_device(): grad_arrived = lax.all_to_all(grad, 'seq', 0, 0, tiled=True)]
    ppermute x0 -> x3, starting transfers between devices: none -> 8.42 us  [the longest x1 5.06 us: add_over_chan(): return sums + lax.ppermute(sums, 'chan', mirror)]
    unnamed x36 -> x22, local copies, waits for them, and re-layouts: 5.64 us -> 0.76 us
    ppermute x0 -> x3, waiting for transfers between devices: none -> 4.27 us  [the longest x1 1.56 us: add_over_chan(): lax.ppermute(sums, 'chan', [(at, at ^ 2) for at in range(GROUP)])]
    all_to_all x2 -> x1, starting transfers between devices: 7.77 us -> 3.87 us  [on_device(): grad_arrived = lax.all_to_all(grad, 'seq', 0, 0, tiled=True)]
    pallas_call x8, Pallas kernels: 8.45 us -> 10.8 us  [call(): pl.pallas_call(kernel, name=name, out_shape=[jax.ShapeDtypeStruct(shape,...]
  transfers between devices with their start and end apart: 2 -> 4, of which waited for: 2 -> 4; matrix products, arithmetic and copies ran while one was open for 0% -> 0% of each run, Pallas kernels for 2% -> 3%
where the time goes in v3:
time: 83.3 us; the launch traced here: 82.1 us
  blocking collectives  46.9 us (56%)
  starting transfers between devices  12.3 us (15%)
  Pallas kernels  10.8 us (13%)
  waiting for transfers between devices  10.6 us (13%)
    all_to_all x1, blocking collectives, on_device(): arrived = lax.all_to_all(packed, 'seq', 0, 0, tiled=True)  19.4 us
    all_to_all x1, blocking collectives, on_device(): result = lax.all_to_all(result, 'seq', 0, 0, tiled=True)  14.8 us
    all_to_all x1, blocking collectives, on_device(): conv = lax.all_to_all(conv, 'seq', 0, 0, tiled=True)  12.8 us
    pallas_call x8, Pallas kernels, call(): pl.pallas_call(kernel, name=name, out_shape=[jax.ShapeDtypeStruct(shape,...  10.8 us
    all_to_all x1, waiting for transfers between devices, on_device(): grad_arrived = lax.all_to_all(grad, 'seq', 0, 0, tiled=True)  6.28 us
    ppermute x1, starting transfers between devices, add_over_chan(): return sums + lax.ppermute(sums, 'chan', mirror)  5.06 us
    all_to_all x1, starting transfers between devices, on_device(): grad_arrived = lax.all_to_all(grad, 'seq', 0, 0, tiled=True)  3.87 us
    ppermute x1, starting transfers between devices, add_over_chan(): lax.ppermute(sums, 'chan', [(at, at ^ 2) for at in range(GROUP)])  3.26 us
  transfers between devices with their start and end apart: 4, of which 4 were waited for; matrix products, arithmetic and copies ran while one was open for 0% of the time, Pallas kernels for 3%

profile of v3, /device:TPU:0, one launch (start us, length us, event | category | flops | bytes accessed | tf_op | source)
XLA Modules:
  0.0 82.1 jit_solution(16280202476538681461)
XLA Ops:
  0.6 0.0 copy-start.4
  0.6 0.0 copy-start.6
  0.7 0.0 copy-start.5
  0.7 2.2 %pack.1.pack_ref = bf16[32,32,256]{2,1,0:T(8,128)(2,1)} custom-call(bf16[256,512]{1,0:T(8,128)(2,1)} %key_ref.1, bf16[256,512]{1,0:T(8,128)(2,1)} %value_ref.1, bf16[256,512]{1,0:T(8,128)(2,1)} %taps_hbm.1), custom_call_target="tpu_custom_call" | custom-call | tf_op jit(solution)/shard_map/pack/pallas_call | solution.py:248
  2.8 0.0 copy-start.1
  2.8 19.4 %all_to_all.20.in_ref.pack_ref = bf16[32,32,256]{2,1,0:T(8,128)(2,1)S(1)} all-to-all(bf16[32,32,256]{2,1,0:T(8,128)(2,1)} %pack.1.pack_ref), channel_id=1, replica_groups=mesh['seq'=32,'chan'=8] {'seq'}, dimensions={0} | all-to-all | bytes 1048576 | tf_op jit(solution)/shard_map/all_to_all | solution.py:287
  22.2 0.0 copy-done.4
  22.2 0.0 copy-done.6
  22.2 0.0 copy-done.5
  22.2 0.0 copy-done.1
  22.2 0.0 copy-start
  22.2 0.0 copy-start.9
  22.2 0.0 copy-start.10
  22.3 1.8 %forward.1 = (bf16[32,16,256]{2,1,0:T(8,128)(2,1)S(1)}, bf16[512,256]{1,0:T(8,128)(2,1)S(1)}, bf16[512,256]{1,0:T(8,128)(2,1)S(1)}) custom-call(bf16[32,32,256]{2,1,0:T(8,128)(2,1)S(1)} %all_to_all.20.in_ref.pack_ref, bf16[1024,512]{1,0:T(8,128)(2,1)S(1)} %copy-done.1, f32[2,33,256]{2,1,0:T(8,128)S(1)} %copy-done.4, bf16[256,512]{1,0:T(8,128)(2,1)S(1)} %copy-done.5, ...), custom_call_target="tpu_custom_call" | custom-call | tf_op jit(solution)/shard_map/forward/pallas_call | solution.py:248
  24.1 12.8 %all_to_all.21.conv_ref = bf16[32,16,256]{2,1,0:T(8,128)(2,1)S(1)} all-to-all(bf16[32,16,256]{2,1,0:T(8,128)(2,1)S(1)} %get-tuple-element.17), channel_id=1, replica_groups=mesh['seq'=32,'chan'=8] {'seq'}, dimensions={0} | all-to-all | bytes 524288 | tf_op jit(solution)/shard_map/all_to_all | solution.py:298
  36.9 0.0 copy-done
  36.9 0.0 copy-done.9
  36.9 0.0 copy-done.10
  36.9 0.3 sums.1
  37.2 0.1 collective-permute-start
  37.3 1.1 %collective-permute-done = f32[2,256]{1,0:T(2,128)S(1)} collective-permute-done((f32[2,256]{1,0:T(2,128)S(1)}, f32[2,256]{1,0:T(2,128)S(1)}, u32[]{:S(2)}, u32[]{:S(2)}) %collective-permute-start) | collective-permute-done | bytes 2080 | tf_op jit(solution)/shard_map/ppermute | solution.py:260
  38.4 3.3 %collective-permute-start.1 = (f32[2,256]{1,0:T(2,128)S(1)}, f32[2,256]{1,0:T(2,128)S(1)}, u32[]{:S(2)}, u32[]{:S(2)}) collective-permute-start(f32[2,256]{1,0:T(2,128)S(1)} %add.9), channel_id=1, source_target_pairs={{0,2},{1,3},{2,0},{3,1},{4,6},{5,7},{6,4},{7,5},{8,10},{9,11},{10,... | collective-permute-start | bytes 6152 | tf_op jit(solution)/shard_map/ppermute | solution.py:261
  41.7 1.6 %collective-permute-done.1 = f32[2,256]{1,0:T(2,128)S(1)} collective-permute-done((f32[2,256]{1,0:T(2,128)S(1)}, f32[2,256]{1,0:T(2,128)S(1)}, u32[]{:S(2)}, u32[]{:S(2)}) %collective-permute-start.1) | collective-permute-done | bytes 2080 | tf_op jit(solution)/shard_map/ppermute | solution.py:261
  43.2 5.1 %collective-permute-start.2 = (f32[2,256]{1,0:T(2,128)S(1)}, f32[2,256]{1,0:T(2,128)S(1)}, u32[]{:S(2)}, u32[]{:S(2)}) collective-permute-start(f32[2,256]{1,0:T(2,128)S(1)} %add.10), channel_id=1, source_target_pairs={{0,6},{1,7},{2,4},{3,5},{4,2},{5,3},{6,0},{7,1},{8,14},{9,15},{10,... | collective-permute-start | bytes 6152 | tf_op jit(solution)/shard_map/ppermute | solution.py:263
  48.3 1.6 %collective-permute-done.2 = f32[2,256]{1,0:T(2,128)S(1)} collective-permute-done((f32[2,256]{1,0:T(2,128)S(1)}, f32[2,256]{1,0:T(2,128)S(1)}, u32[]{:S(2)}, u32[]{:S(2)}) %collective-permute-start.2) | collective-permute-done | bytes 2080 | tf_op jit(solution)/shard_map/ppermute | solution.py:263
  49.9 1.0 %grad.1 = bf16[32,16,256]{2,1,0:T(8,128)(2,1)} custom-call(f32[2,256]{1,0:T(2,128)S(1)} %add.11.sums_ref, bf16[32,16,256]{2,1,0:T(8,128)(2,1)S(1)} %all_to_all.21.conv_ref, bf16[32,32,256]{2,1,0:T(8,128)(2,1)S(1)} %copy-done, bf16[512,256]{1,0:T(8,128)(2,1)S(1)} %get-tuple-element.18.gate_ref, bf16[512,256]{1,0:T(8,128)(2,1)S(1)} %get-tuple-element.19.cot_ref, ...), custom_call_target="tpu_custom_call" | custom-call | tf_op jit(solution)/shard_map/grad/pallas_call | solution.py:248
  50.9 3.9 %all-to-all-start.2 = ((bf16[32,16,256]{2,1,0:T(8,128)(2,1)}), bf16[32,16,256]{2,1,0:T(8,128)(2,1)S(1)}, u32[]{:S(2)}, u32[]{:S(2)}) async-start(bf16[32,16,256]{2,1,0:T(8,128)(2,1)} %grad.1), calls=%async_computation.2 | async-start | bytes 524288 | tf_op jit(solution)/shard_map/all_to_all | solution.py:303
  54.8 1.2 %norm.1 = (bf16[256,512]{1,0:T(8,128)(2,1)}, bf16[256,512]{1,0:T(8,128)(2,1)}, bf16[256,512]{1,0:T(8,128)(2,1)S(1)}, f32[1,512]{1,0:T(1,128)S(1)}) custom-call(f32[2,256]{1,0:T(2,128)S(1)} %add.11.sums_ref, bf16[32,16,256]{2,1,0:T(8,128)(2,1)S(1)} %all_to_all.21.conv_ref, bf16[32,32,256]{2,1,0:T(8,128)(2,1)S(1)} %copy-done, ...), custom_call_target="tpu_custom_call" | custom-call | tf_op jit(solution)/shard_map/norm/pallas_call | solution.py:248
  55.9 0.0 copy-start.7
  55.9 0.7 copy-done.7
  56.6 1.3 %spectra.1.spec_ref = bf16[2,528,512]{2,1,0:T(8,128)(2,1)S(1)} custom-call(bf16[32,32,256]{2,1,0:T(8,128)(2,1)S(1)} %all_to_all.20.in_ref.pack_ref, bf16[1024,512]{1,0:T(8,128)(2,1)S(1)} %copy-done.1, f32[2,33,256]{2,1,0:T(8,128)S(1)} %copy-done.4, f32[1,512]{1,0:T(1,128)S(1)} %get-tuple-element.22.after_ref.skip_ref), custom_call_target="tpu_custom_call" | custom-call | tf_op jit(solution)/shard_map/spectra/pallas_call | solution.py:248
  57.9 6.3 %all-to-all-done.2.in_ref = bf16[32,16,256]{2,1,0:T(8,128)(2,1)S(1)} async-done(((bf16[32,16,256]{2,1,0:T(8,128)(2,1)}), bf16[32,16,256]{2,1,0:T(8,128)(2,1)S(1)}, u32[]{:S(2)}, u32[]{:S(2)}) %all-to-all-start.2) | async-done | bytes 262176 | tf_op jit(solution)/shard_map/all_to_all | solution.py:303
  64.2 2.0 %backward.1 = bf16[32,72,128]{2,1,0:T(8,128)(2,1)S(1)} custom-call(bf16[32,16,256]{2,1,0:T(8,128)(2,1)S(1)} %all-to-all-done.2.in_ref, bf16[32,32,256]{2,1,0:T(8,128)(2,1)S(1)} %all_to_all.20.in_ref.pack_ref, bf16[2,528,512]{2,1,0:T(8,128)(2,1)S(1)} %spectra.1.spec_ref, bf16[1024,512]{1,0:T(8,128)(2,1)S(1)} %copy-done.1, f32[2,33,256]{2,1,0:T(8,128)S(1)} %copy-done.4, ...), custom_call_target="tpu_custom_call" | custom-call | tf_op jit(solution)/shard_map/backward/pallas_call | solution.py:248
  66.2 0.0 copy-start.2
  66.2 0.0 copy-start.3
  66.2 0.0 copy-start.8
  66.2 14.8 %all_to_all.22.in_ref = bf16[32,72,128]{2,1,0:T(8,128)(2,1)S(1)} all-to-all(bf16[32,72,128]{2,1,0:T(8,128)(2,1)S(1)} %backward.1), channel_id=1, replica_groups=mesh['seq'=32,'chan'=8] {'seq'}, dimensions={0} | all-to-all | bytes 1179648 | tf_op jit(solution)/shard_map/all_to_all | solution.py:319
  81.0 0.0 copy-done.2
  81.0 0.0 copy-done.3
  81.0 0.0 copy-done.8
  81.0 1.1 %last.1 = (bf16[256,512]{1,0:T(8,128)(2,1)}, bf16[256,512]{1,0:T(8,128)(2,1)}, bf16[256,512]{1,0:T(8,128)(2,1)}, f32[1,512]{1,0:T(1,128)}) custom-call(bf16[32,72,128]{2,1,0:T(8,128)(2,1)S(1)} %all_to_all.22.in_ref, bf16[256,512]{1,0:T(8,128)(2,1)S(1)} %copy-done.8, bf16[256,512]{1,0:T(8,128)(2,1)S(1)} %copy-done.2, bf16[256,512]{1,0:T(8,128)(2,1)S(1)} %copy-done.3, ...), custom_call_target="tpu_custom_call" | custom-call | tf_op jit(solution)/shard_map/last/pallas_call | solution.py:248
  (3 shorter events, 0.0 us)
Async XLA Ops:
  0.6 21.6 %copy-start.4 = (f32[2,33,256]{2,1,0:T(8,128)S(1)}, f32[2,33,256]{2,1,0:T(8,128)}, u32[]{:S(2)}) copy-start(f32[2,33,256]{2,1,0:T(8,128)} %constant.5.clone.turn_ref) | copy-start | bytes 202756
  0.6 21.6 %copy-start.6 = (bf16[256,512]{1,0:T(8,128)(2,1)S(1)}, bf16[256,512]{1,0:T(8,128)(2,1)}, u32[]{:S(2)}) copy-start(bf16[256,512]{1,0:T(8,128)(2,1)} %cot_ref.1) | copy-start | bytes 786436
  0.7 21.6 %copy-start.5 = (bf16[256,512]{1,0:T(8,128)(2,1)S(1)}, bf16[256,512]{1,0:T(8,128)(2,1)}, u32[]{:S(2)}) copy-start(bf16[256,512]{1,0:T(8,128)(2,1)} %gate_ref.1) | copy-start | bytes 786436
  2.8 19.4 %copy-start.1 = (bf16[1024,512]{1,0:T(8,128)(2,1)S(1)}, bf16[1024,512]{1,0:T(8,128)(2,1)}, u32[]{:S(2)}) copy-start(bf16[1024,512]{1,0:T(8,128)(2,1)} %constant.4.clone.steps_ref) | copy-start | bytes 3145732
  22.2 14.6 %copy-start = (bf16[32,32,256]{2,1,0:T(8,128)(2,1)S(1)}, bf16[32,32,256]{2,1,0:T(8,128)(2,1)}, u32[]{:S(2)}) copy-start(bf16[32,32,256]{2,1,0:T(8,128)(2,1)} %pack.1.pack_ref) | copy-start | bytes 1572868
  22.2 14.6 %copy-start.9 = (f32[512]{0:T(512)S(1)}, f32[512]{0:T(512)}, u32[]{:S(2)}) copy-start(f32[512]{0:T(512)} %param.13) | copy-start | bytes 6148
  22.2 14.6 %copy-start.10 = (f32[512]{0:T(512)S(1)}, f32[512]{0:T(512)}, u32[]{:S(2)}) copy-start(f32[512]{0:T(512)} %param.14) | copy-start | bytes 6148
  37.2 1.2 %collective-permute-start = (f32[2,256]{1,0:T(2,128)S(1)}, f32[2,256]{1,0:T(2,128)S(1)}, u32[]{:S(2)}, u32[]{:S(2)}) collective-permute-start(f32[2,256]{1,0:T(2,128)S(1)} %sums.1), channel_id=1, source_target_pairs={{0,1},{1,0},{2,3},{3,2},{4,5},{5,4},{6,7},{7,6},{8,9},{9,8},{10,11... | collective-permute-start | bytes 6152 | tf_op jit(solution)/shard_map/ppermute | solution.py:260
  38.4 4.8 %collective-permute-start.1 = (f32[2,256]{1,0:T(2,128)S(1)}, f32[2,256]{1,0:T(2,128)S(1)}, u32[]{:S(2)}, u32[]{:S(2)}) collective-permute-start(f32[2,256]{1,0:T(2,128)S(1)} %add.9), channel_id=1, source_target_pairs={{0,2},{1,3},{2,0},{3,1},{4,6},{5,7},{6,4},{7,5},{8,10},{9,11},{10,... | collective-permute-start | bytes 6152 | tf_op jit(solution)/shard_map/ppermute | solution.py:261
  43.2 6.6 %collective-permute-start.2 = (f32[2,256]{1,0:T(2,128)S(1)}, f32[2,256]{1,0:T(2,128)S(1)}, u32[]{:S(2)}, u32[]{:S(2)}) collective-permute-start(f32[2,256]{1,0:T(2,128)S(1)} %add.10), channel_id=1, source_target_pairs={{0,6},{1,7},{2,4},{3,5},{4,2},{5,3},{6,0},{7,1},{8,14},{9,15},{10,... | collective-permute-start | bytes 6152 | tf_op jit(solution)/shard_map/ppermute | solution.py:263
  50.9 13.3 %all-to-all-start.2 = ((bf16[32,16,256]{2,1,0:T(8,128)(2,1)}), bf16[32,16,256]{2,1,0:T(8,128)(2,1)S(1)}, u32[]{:S(2)}, u32[]{:S(2)}) async-start(bf16[32,16,256]{2,1,0:T(8,128)(2,1)} %grad.1), calls=%async_computation.2 | async-start | bytes 524288 | tf_op jit(solution)/shard_map/all_to_all | solution.py:303
  55.9 0.7 copy-start.7
  66.2 14.8 %copy-start.2 = (bf16[256,512]{1,0:T(8,128)(2,1)S(1)}, bf16[256,512]{1,0:T(8,128)(2,1)}, u32[]{:S(2)}) copy-start(bf16[256,512]{1,0:T(8,128)(2,1)} %key_ref.1) | copy-start | bytes 786436
  66.2 14.8 %copy-start.3 = (bf16[256,512]{1,0:T(8,128)(2,1)S(1)}, bf16[256,512]{1,0:T(8,128)(2,1)}, u32[]{:S(2)}) copy-start(bf16[256,512]{1,0:T(8,128)(2,1)} %value_ref.1) | copy-start | bytes 786436
  66.2 14.8 %copy-start.8 = (bf16[256,512]{1,0:T(8,128)(2,1)S(1)}, bf16[256,512]{1,0:T(8,128)(2,1)}, u32[]{:S(2)}) copy-start(bf16[256,512]{1,0:T(8,128)(2,1)} %copy-done.7) | copy-start | bytes 786436

commit v4 on v3

v4 whole, which is shorter than its diff:
```python
import jax
import jax.numpy as jnp
import numpy as np
from jax import lax
from jax.experimental import pallas as pl
from jax.experimental.pallas import tpu as pltpu
from jax.sharding import PartitionSpec as P

D = 4096
LENGTH = 8192
epsilon = 1e-05

f32, bf16 = jnp.float32, jnp.bfloat16

PARTS = 32
GROUP = 8
BLOCK = LENGTH // PARTS
WIDTH = D // GROUP
PIECE = WIDTH // PARTS
HALF = PIECE // 2
NEAR = BLOCK // 2
FULL = 2 * LENGTH
SPAN = 2 * PARTS
BINS = PARTS + 1
ROWS = BINS * PIECE
TAIL = 8
CHIPS = GROUP // 2


def tables():
    low = np.array(list(range(1, PARTS)) + [0, PARTS])
    block, inside, near = np.arange(PARTS), np.arange(BLOCK), np.arange(NEAR)
    outer = 2 * np.pi * (low[:, None] * block[None, :] % SPAN) / SPAN
    cosine, sine = np.cos(outer), np.sin(outer)
    eye = np.eye(HALF)
    enter = np.kron(np.concatenate([cosine, -sine[: PARTS - 1]], 0), eye)
    weight = np.where((low == 0) | (low == PARTS), 1.0, 2.0)[:, None] / 4
    leave = np.kron(np.concatenate([cosine * weight, (sine * weight)[: PARTS - 1]], 0).T, eye)
    inner = 2 * np.pi * (near[:, None] * near[None, :] % NEAR) / NEAR
    cosine, sine = np.cos(inner) / 16, -np.sin(inner) / 16
    inner = np.block([[cosine, sine], [-sine, cosine]])
    half = SPAN * HALF // 2
    steps = np.concatenate([inner, leave, enter[:half], enter[half:]], 1)
    turn = 2 * np.pi * (low[:, None] * inside[None, :] % FULL) / FULL
    pair = 2 * np.pi * inside[None, :] / BLOCK
    turn = np.concatenate([turn, pair], 0)
    turn = np.stack([np.cos(turn), -np.sin(turn)])
    return steps.astype(np.float32).astype(bf16), turn.astype(np.float32)


def open_tables(steps_ref, turn_ref):
    cuts = (BLOCK, BLOCK + SPAN * HALF, 2 * BLOCK + SPAN * HALF)
    enter = jnp.concatenate([steps_ref[:, cuts[1] : cuts[2]], steps_ref[:, cuts[2] :]], 0)
    turn = [
        jnp.broadcast_to(turn_ref[part, :BINS][:, None, :], (BINS, HALF, BLOCK)).reshape(BINS * HALF, BLOCK)
        for part in range(2)
    ]
    pair = [turn_ref[part, BINS:, :NEAR] for part in range(2)]
    return enter, steps_ref[:, cuts[0] : cuts[1]], steps_ref[:, : cuts[0]], turn, pair


def dot(first, second):
    return jnp.dot(first, second, preferred_element_type=f32)


def rotate(real, imag, turn):
    return real * turn[0] - imag * turn[1], real * turn[1] + imag * turn[0]


def rotate_first(real, imag, turn):
    cosine, sine = turn
    own = imag.shape[0]
    turned_re, turned_im = rotate(real[:own], imag, (cosine[:own], sine[:own]))
    turned_re = jnp.concatenate([turned_re, real[own:] * cosine[own:]], 0)
    turned_im = jnp.concatenate([turned_im, real[own:] * sine[own:]], 0)
    return turned_re, turned_im


def join(halves):
    parts = [half.reshape(BINS, HALF, NEAR) for half in halves]
    return jnp.concatenate(parts, 1).reshape(ROWS, NEAR).astype(bf16)


def spectrum(signal, enter, inner, turn, pair):
    wide = signal.astype(f32)
    pieces = ([], [], [], [])
    for half in range(2):
        rows = wide[:, half * HALF : (half + 1) * HALF].reshape(PARTS * HALF, BLOCK)
        mixed = dot(enter, rows.astype(bf16))
        real, imag = rotate_first(mixed[: BINS * HALF], mixed[BINS * HALF :], turn)
        pieces[0].append(real[:, :NEAR] + real[:, NEAR:])
        pieces[1].append(imag[:, :NEAR] + imag[:, NEAR:])
        real, imag = rotate(real[:, :NEAR] - real[:, NEAR:], imag[:, :NEAR] - imag[:, NEAR:], pair)
        pieces[2].append(real)
        pieces[3].append(imag)
    pieces = [join(piece) for piece in pieces]
    return [dot(jnp.concatenate(pieces[at : at + 2], 1), inner) for at in (0, 2)]


def invert(even, odd, leave, inner, turn, pair):
    even, odd = [
        dot(jnp.concatenate([real.astype(bf16), imag.astype(bf16)], 1), inner).reshape(BINS, PIECE, BLOCK)
        for real, imag in (even, odd)
    ]
    outs = []
    for half in range(2):
        rows = slice(half * HALF, (half + 1) * HALF)
        first, second = [part[:, rows].reshape(BINS * HALF, BLOCK) for part in (even, odd)]
        first_re, first_im = first[:, :NEAR], first[:, NEAR:]
        second_re, second_im = rotate(second[:, :NEAR], second[:, NEAR:], pair)
        real = jnp.concatenate([first_re + second_re, first_re - second_re], 1)
        imag = jnp.concatenate([first_im + second_im, first_im - second_im], 1)
        own = (BINS - 2) * HALF
        turned_re = real * turn[0] - imag * turn[1]
        turned_im = real[:own] * turn[1][:own] + imag[:own] * turn[0][:own]
        turned = jnp.concatenate([turned_re, turned_im], 0).astype(bf16)
        outs.append(dot(leave, turned).reshape(PARTS, HALF, BLOCK))
    return jnp.concatenate(outs, 1)


def parts_of(values):
    return values[:, :NEAR].astype(f32), values[:, NEAR:].astype(f32)


def flat(pieces):
    return pieces.reshape(WIDTH, BLOCK)


def cut(rows):
    return rows.reshape(PARTS, PIECE, BLOCK)


def pack_kernel(key_hbm, value_hbm, taps_hbm, out_hbm, key_ref, value_ref, taps_ref, out_ref, sems):
    width, parts = WIDTH // 2, PARTS // 2
    loads, stores = [], []
    for half in range(2):
        columns = pl.ds(half * width, width)
        for source, target in ((key_hbm, key_ref), (value_hbm, value_ref), (taps_hbm, taps_ref)):
            loads.append(pltpu.make_async_copy(source.at[:, columns], target.at[:, columns], sems.at[len(loads)]))
            loads[-1].start()
    for half in range(2):
        columns, owners = pl.ds(half * width, width), pl.ds(half * parts, parts)
        loads[3 * half].wait()
        loads[3 * half + 1].wait()
        mixed = key_ref[:, columns].astype(f32) * value_ref[:, columns].astype(f32)
        out_ref[owners, :PIECE, :] = mixed.astype(bf16).T.reshape(parts, PIECE, BLOCK)
        loads[3 * half + 2].wait()
        out_ref[owners, PIECE:, :] = taps_ref[:, columns].T.reshape(parts, PIECE, BLOCK)
        stores.append(pltpu.make_async_copy(out_ref.at[owners], out_hbm.at[owners], sems.at[6 + half]))
        stores[-1].start()
    for store in stores:
        store.wait()


def forward_kernel(in_ref, steps_ref, turn_ref, gate_ref, cot_ref, out_ref, gate_out, cot_out):
    gate_out[...] = gate_ref[...].T
    cot_out[...] = cot_ref[...].T
    enter, leave, inner, turn, pair = open_tables(steps_ref, turn_ref)
    first = spectrum(in_ref[:, :PIECE, :], enter, inner, turn, pair)
    second = spectrum(in_ref[:, PIECE:, :], enter, inner, turn, pair)
    products = []
    for one, other in zip(first, second, strict=True):
        one_re, one_im = parts_of(one)
        other_re, other_im = parts_of(other)
        products.append((one_re * other_re - one_im * other_im, -(one_re * other_im + one_im * other_re)))
    out_ref[...] = invert(*products, leave, inner, turn, pair).astype(bf16)


def between_kernel(
    in_ref, steps_ref, turn_ref, conv_ref, key_ref, value_ref, skip_ref, after_ref, spec_ref, full_ref
):
    enter, _, inner, turn, pair = open_tables(steps_ref, turn_ref)
    for place in range(2):
        signal = in_ref[:, place * PIECE : (place + 1) * PIECE, :]
        even, odd = spectrum(signal, enter, inner, turn, pair)
        spec_ref[2 * place] = even.astype(bf16)
        spec_ref[2 * place + 1] = odd.astype(bf16)
    mixed = (key_ref[...].astype(f32) * value_ref[...].astype(f32)).astype(bf16)
    full_ref[...] = flat(conv_ref[...]).T.astype(f32) + skip_ref[...] * mixed.astype(f32)


def column(row_ref):
    turned = jnp.broadcast_to(row_ref[...], (128, WIDTH)).T
    return jnp.concatenate([turned, turned], 1)


def gate_parts(conv_ref, pack_ref, gate_ref, skip_ref):
    mixed = flat(pack_ref[:, :PIECE, :]).astype(f32)
    full = flat(conv_ref[...]).astype(f32) + column(skip_ref) * mixed
    gate = gate_ref[...].astype(f32)
    return full, gate, gate * full


def sums_kernel(conv_ref, pack_ref, gate_ref, cot_ref, skip_ref, gain_ref, out_ref):
    _, _, gated = gate_parts(conv_ref, pack_ref, gate_ref, skip_ref)
    scaled = cot_ref[...].astype(f32) * column(gain_ref)
    squares = jnp.sum(gated * gated, axis=0, keepdims=True)
    inner = jnp.sum(scaled * gated, axis=0, keepdims=True)
    out_ref[...] = jnp.concatenate([squares, inner], 0)


def norm_parts(sums_ref):
    sums = sums_ref[...]
    inv_rms = lax.rsqrt(sums[0:1] / D + epsilon)
    return inv_rms, inv_rms * inv_rms * inv_rms * sums[1:2] / D


def grad_kernel(
    sums_ref, conv_ref, pack_ref, gate_ref, cot_ref, skip_ref, gain_ref, after_ref, out_ref
):
    inv_rms, pull = norm_parts(sums_ref)
    _, gate, gated = gate_parts(conv_ref, pack_ref, gate_ref, skip_ref)
    scaled = cot_ref[...].astype(f32) * column(gain_ref)
    grad_gated = inv_rms * scaled - gated * pull
    out_ref[...] = cut((grad_gated * gate).astype(bf16))


def wide_column(row):
    turned = jnp.broadcast_to(row, (128, BLOCK)).T
    return jnp.concatenate([turned] * (WIDTH // 128), 1)


def backward_kernel(
    in_ref, pack_ref, spec_ref, steps_ref, turn_ref, sums_ref, full_ref, gate_ref, cot_ref, gain_ref,
    out_ref, grad_out, normed_hbm, gate_hbm, normed_ref, gate_out, sems,
):
    inv_rms, pull = (wide_column(row) for row in norm_parts(sums_ref))
    full, gate, gain = full_ref[...], gate_ref[...].astype(f32), gain_ref[...]
    gated = gate * full
    normed_ref[...] = (gated * inv_rms * gain).astype(bf16)
    grad_gated = inv_rms * (cot_ref[...].astype(f32) * gain) - gated * pull
    gate_out[...] = (grad_gated * full).astype(bf16)
    grad_out[...] = (grad_gated * gate).astype(bf16)
    copies = [
        pltpu.make_async_copy(normed_ref, normed_hbm, sems.at[0]),
        pltpu.make_async_copy(gate_out, gate_hbm, sems.at[1]),
    ]
    for copy in copies:
        copy.start()
    enter, leave, inner, turn, pair = open_tables(steps_ref, turn_ref)
    grad = in_ref[...]
    bias = jnp.sum(grad.astype(f32) * pack_ref[:, :PIECE, :].astype(f32), axis=0)
    bias = jnp.sum(bias, axis=1, keepdims=True)
    high = bias.astype(bf16).astype(f32)
    lane = lax.broadcasted_iota(jnp.int32, (TAIL, 128), 1)
    tail = jnp.zeros((TAIL, 128), f32)
    for at, part in enumerate((high[:HALF], (bias - high)[:HALF], high[HALF:], (bias - high)[HALF:])):
        tail = jnp.where(lane == at, part, tail)
    out_ref[:, 4 * PIECE :, :] = jnp.broadcast_to(tail.astype(bf16)[None], (PARTS, TAIL, 128))
    spectra = spectrum(grad, enter, inner, turn, pair)
    for place, other in ((0, 1), (1, 0)):
        products = []
        for parity, mine in enumerate(spectra):
            real, imag = parts_of(spec_ref[2 * other + parity])
            mine_re, mine_im = parts_of(mine)
            products.append((real * mine_re + imag * mine_im, imag * mine_re - real * mine_im))
        result = invert(*products, leave, inner, turn, pair).astype(bf16)
        out_ref[:, 2 * place * PIECE : (2 * place + 1) * PIECE, :] = result[:, :, :128]
        out_ref[:, (2 * place + 1) * PIECE : (2 * place + 2) * PIECE, :] = result[:, :, 128:]
    for copy in copies:
        copy.wait()


def last_kernel(in_ref, grad_ref, key_ref, value_ref, skip_ref, key_out, value_out, taps_out, bias_out):
    def whole(place):
        at = 2 * place * PIECE
        left, right = in_ref[:, at : at + PIECE, :], in_ref[:, at + PIECE : at + 2 * PIECE, :]
        return jnp.concatenate([left.reshape(WIDTH, 128).T, right.reshape(WIDTH, 128).T], 0)

    grad_mixed = whole(0).astype(f32) + skip_ref[...] * grad_ref[...].astype(f32)
    key_out[...] = (grad_mixed * value_ref[...].astype(f32)).astype(bf16)
    value_out[...] = (grad_mixed * key_ref[...].astype(f32)).astype(bf16)
    taps_out[...] = whole(1)
    tail = in_ref[:, 4 * PIECE :, :].astype(f32)
    tail = jnp.concatenate([tail, pltpu.roll(tail, 126, 2)], 1).reshape(WIDTH, 128).T
    bias_out[...] = tail[0:1] + tail[1:2]


def call(kernel, name, outs, *operands, hbm_in=(), hbm_out=(), scratch=(), grant=32 * 1024):
    vmem, hbm = pl.BlockSpec(memory_space=pltpu.VMEM), pl.BlockSpec(memory_space=pltpu.HBM)
    return pl.pallas_call(
        kernel,
        name=name,
        out_shape=[jax.ShapeDtypeStruct(shape, kind) for shape, kind in outs],
        in_specs=[hbm if place in hbm_in else vmem for place in range(len(operands))],
        out_specs=[hbm if place in hbm_out else vmem for place in range(len(outs))],
        scratch_shapes=list(scratch),
        compiler_params=pltpu.CompilerParams(vmem_limit_bytes=grant * 1024),
    )(*operands)


def add_over_pairs(sums):
    sums = sums + lax.ppermute(sums, "chan", [(at, at ^ 1) for at in range(GROUP)])
    return sums + lax.ppermute(sums, "chan", [(at, at ^ 2) for at in range(GROUP)])


def add_over_mirror(sums):
    mirror = [(at, (CHIPS - 1 - at // 2) * 2 + at % 2) for at in range(GROUP)]
    return sums + lax.ppermute(sums, "chan", mirror)


def on_device(gate_feat, key_feat, value_feat, filter_taps, skip_bias, norm_gain, cotangent):
    steps, turn = (jnp.asarray(table) for table in tables())
    skip_row, gain_row = skip_bias[None, :], norm_gain[None, :]
    natural = ((BLOCK, WIDTH), bf16)
    turned = ((WIDTH, BLOCK), bf16)
    pieces = ((PARTS, PIECE, BLOCK), bf16)
    spectra = ((4, ROWS, BLOCK), bf16)
    whole = pltpu.VMEM(*natural)

    (packed,) = call(
        pack_kernel,
        "pack",
        [((PARTS, 2 * PIECE, BLOCK), bf16)],
        key_feat,
        value_feat,
        filter_taps,
        hbm_in=(0, 1, 2),
        hbm_out=(0,),
        scratch=[whole, whole, whole, pltpu.VMEM((PARTS, 2 * PIECE, BLOCK), bf16), pltpu.SemaphoreType.DMA((8,))],
        grant=63 * 1024,
    )
    arrived = lax.all_to_all(packed, "seq", 0, 0, tiled=True)
    conv, gate_t, cot_t = call(
        forward_kernel,
        "forward",
        [pieces, turned, turned],
        arrived,
        steps,
        turn,
        gate_feat,
        cotangent,
    )
    conv = lax.all_to_all(conv, "seq", 0, 0, tiled=True)
    sides = (conv, packed, gate_t, cot_t, skip_row, gain_row)
    (sums,) = call(sums_kernel, "sums", [((2, BLOCK), f32)], *sides)
    sums = add_over_pairs(sums)
    spec, full = call(
        between_kernel,
        "between",
        [spectra, ((BLOCK, WIDTH), f32)],
        arrived,
        steps,
        turn,
        conv,
        key_feat,
        value_feat,
        skip_row,
        sums,
    )
    sums = add_over_mirror(sums)
    (grad,) = call(grad_kernel, "grad", [pieces], sums, *sides, full)
    grad_arrived = lax.all_to_all(grad, "seq", 0, 0, tiled=True)
    result, grad_conv, normed_out, grad_gate = call(
        backward_kernel,
        "backward",
        [((PARTS, 4 * PIECE + TAIL, 128), bf16), natural, natural, natural],
        grad_arrived,
        arrived,
        spec,
        steps,
        turn,
        sums,
        full,
        gate_feat,
        cotangent,
        gain_row,
        hbm_out=(2, 3),
        scratch=[whole, whole, pltpu.SemaphoreType.DMA((2,))],
    )
    result = lax.all_to_all(result, "seq", 0, 0, tiled=True)
    grad_key, grad_value, grad_filter, grad_bias = call(
        last_kernel,
        "last",
        [natural] * 3 + [((1, WIDTH), f32)],
        result,
        grad_conv,
        key_feat,
        value_feat,
        skip_row,
    )
    return normed_out, grad_gate, grad_key, grad_value, grad_filter, grad_bias[0]


def solution(mesh):
    wide, row = P("seq", "chan"), P("chan")
    return jax.shard_map(
        on_device,
        mesh=mesh,
        in_specs=(wide, wide, wide, wide, row, row, wide),
        out_specs=(wide, wide, wide, wide, wide, row),
        check_vma=False,
    )
```

time: 83.3 us -> 82.4 us (0.989)
  blocking collectives: 46.9 us -> 59.8 us
  waiting for transfers between devices: 10.6 us -> 3.12 us
  starting transfers between devices: 12.3 us -> 8.42 us
  Pallas kernels: 10.8 us -> 9.2 us
    all_to_all x0 -> x1, blocking collectives: none -> 12.9 us  [on_device(): grad_arrived = lax.all_to_all(grad, 'seq', 0, 0, tiled=True)]
    all_to_all x1 -> x0, waiting for transfers between devices: 6.28 us -> none  [on_device(): grad_arrived = lax.all_to_all(grad, 'seq', 0, 0, tiled=True)]
    all_to_all x1 -> x0, starting transfers between devices: 3.87 us -> none  [on_device(): grad_arrived = lax.all_to_all(grad, 'seq', 0, 0, tiled=True)]
    pallas_call x8 -> x7, Pallas kernels: 10.8 us -> 9.2 us  [call(): pl.pallas_call(kernel, name=name, out_shape=[jax.ShapeDtypeStruct(shape,...]
    ppermute x3, waiting for transfers between devices: 4.27 us -> 3.12 us  [the longest x1 1.56 us: add_over_pairs(): lax.ppermute(sums, 'chan', [(at, at ^ 2) for at in range(GROUP)])]
  transfers between devices with their start and end apart: 4 -> 3, of which waited for: 4 -> 3; matrix products, arithmetic and copies ran while one was open for 0% -> 0% of each run, Pallas kernels for 3% -> 1%
where the time goes in v4:
time: 82.4 us; the launch traced here: 81.4 us
  blocking collectives  59.8 us (73%)
  Pallas kernels  9.2 us (11%)
  starting transfers between devices  8.42 us (10%)
  waiting for transfers between devices  3.12 us (4%)
    all_to_all x1, blocking collectives, on_device(): arrived = lax.all_to_all(packed, 'seq', 0, 0, tiled=True)  19.4 us
    all_to_all x1, blocking collectives, on_device(): result = lax.all_to_all(result, 'seq', 0, 0, tiled=True)  14.7 us
    all_to_all x1, blocking collectives, on_device(): conv = lax.all_to_all(conv, 'seq', 0, 0, tiled=True)  12.9 us
    all_to_all x1, blocking collectives, on_device(): grad_arrived = lax.all_to_all(grad, 'seq', 0, 0, tiled=True)  12.9 us
    pallas_call x7, Pallas kernels, call(): pl.pallas_call(kernel, name=name, out_shape=[jax.ShapeDtypeStruct(shape,...  9.2 us
    ppermute x1, starting transfers between devices, add_over_mirror(): return sums + lax.ppermute(sums, 'chan', mirror)  5.05 us
    ppermute x1, starting transfers between devices, add_over_pairs(): lax.ppermute(sums, 'chan', [(at, at ^ 2) for at in range(GROUP)])  3.27 us
  transfers between devices with their start and end apart: 3, of which 3 were waited for; matrix products, arithmetic and copies ran while one was open for 0% of the time, Pallas kernels for 1%

profile of v4, /device:TPU:0, one launch (start us, length us, event | category | flops | bytes accessed | tf_op | source)
XLA Modules:
  0.0 81.4 jit_solution(15431372624674294866)
XLA Ops:
  0.6 0.0 copy-start.1
  0.6 0.0 copy-start.4
  0.7 2.2 %pack.1.pack_ref = bf16[32,32,256]{2,1,0:T(8,128)(2,1)} custom-call(bf16[256,512]{1,0:T(8,128)(2,1)} %key_ref.3, bf16[256,512]{1,0:T(8,128)(2,1)} %value_ref.3, bf16[256,512]{1,0:T(8,128)(2,1)} %taps_hbm.1), custom_call_target="tpu_custom_call" | custom-call | tf_op jit(solution)/shard_map/pack/pallas_call | solution.py:281
  2.8 0.0 copy-start.5
  2.9 0.0 copy-start.6
  2.9 19.4 %all_to_all.20.in_ref.pack_ref = bf16[32,32,256]{2,1,0:T(8,128)(2,1)S(1)} all-to-all(bf16[32,32,256]{2,1,0:T(8,128)(2,1)} %pack.1.pack_ref), channel_id=1, replica_groups=mesh['seq'=32,'chan'=8] {'seq'}, dimensions={0} | all-to-all | bytes 1048576 | tf_op jit(solution)/shard_map/all_to_all | solution.py:323
  22.2 0.0 copy-done.1
  22.2 0.0 copy-done.4
  22.2 0.0 copy-done.5
  22.2 0.0 copy-done.6
  22.3 0.0 copy-start
  22.3 0.0 copy-start.7
  22.3 0.0 copy-start.8
  22.3 1.6 %forward.1 = (bf16[32,16,256]{2,1,0:T(8,128)(2,1)S(1)}, bf16[512,256]{1,0:T(8,128)(2,1)S(1)}, bf16[512,256]{1,0:T(8,128)(2,1)S(1)}) custom-call(bf16[32,32,256]{2,1,0:T(8,128)(2,1)S(1)} %all_to_all.20.in_ref.pack_ref, bf16[256,1280]{1,0:T(8,128)(2,1)S(1)} %copy-done.1, f32[2,34,256]{2,1,0:T(8,128)S(1)} %copy-done.6, bf16[256,512]{1,0:T(8,128)(2,1)S(1)} %copy-done.4, ...), custom_call_target="tpu_custom_call" | custom-call | tf_op jit(solution)/shard_map/forward/pallas_call | solution.py:281
  23.9 0.0 copy-start.2
  23.9 0.0 copy-start.3
  23.9 12.9 %all_to_all.21.conv_ref = bf16[32,16,256]{2,1,0:T(8,128)(2,1)S(1)} all-to-all(bf16[32,16,256]{2,1,0:T(8,128)(2,1)S(1)} %get-tuple-element.19), channel_id=1, replica_groups=mesh['seq'=32,'chan'=8] {'seq'}, dimensions={0} | all-to-all | bytes 524288 | tf_op jit(solution)/shard_map/all_to_all | solution.py:334
  36.8 0.0 copy-done
  36.8 0.0 copy-done.7
  36.8 0.0 copy-done.8
  36.8 0.3 sums.1
  37.1 0.1 collective-permute-start
  37.2 1.1 %collective-permute-done = f32[2,256]{1,0:T(2,128)S(1)} collective-permute-done((f32[2,256]{1,0:T(2,128)S(1)}, f32[2,256]{1,0:T(2,128)S(1)}, u32[]{:S(2)}, u32[]{:S(2)}) %collective-permute-start) | collective-permute-done | bytes 2080 | tf_op jit(solution)/shard_map/ppermute | solution.py:293
  38.4 3.3 %collective-permute-start.1 = (f32[2,256]{1,0:T(2,128)S(1)}, f32[2,256]{1,0:T(2,128)S(1)}, u32[]{:S(2)}, u32[]{:S(2)}) collective-permute-start(f32[2,256]{1,0:T(2,128)S(1)} %add.9), channel_id=1, source_target_pairs={{0,2},{1,3},{2,0},{3,1},{4,6},{5,7},{6,4},{7,5},{8,10},{9,11},{10,... | collective-permute-start | bytes 6152 | tf_op jit(solution)/shard_map/ppermute | solution.py:294
  41.6 1.6 %collective-permute-done.1 = f32[2,256]{1,0:T(2,128)S(1)} collective-permute-done((f32[2,256]{1,0:T(2,128)S(1)}, f32[2,256]{1,0:T(2,128)S(1)}, u32[]{:S(2)}, u32[]{:S(2)}) %collective-permute-start.1) | collective-permute-done | bytes 2080 | tf_op jit(solution)/shard_map/ppermute | solution.py:294
  43.2 5.1 %collective-permute-start.2 = (f32[2,256]{1,0:T(2,128)S(1)}, f32[2,256]{1,0:T(2,128)S(1)}, u32[]{:S(2)}, u32[]{:S(2)}) collective-permute-start(f32[2,256]{1,0:T(2,128)S(1)} %add.10.after_ref), channel_id=1, source_target_pairs={{0,6},{1,7},{2,4},{3,5},{4,2},{5,3},{6,0},{7,1},{8,14},{9,15},{10,... | collective-permute-start | bytes 6152 | tf_op jit(solution)/shard_map/ppermute | solution.py:299
  48.2 0.0 copy-done.2
  48.2 0.0 copy-done.3
  48.2 1.1 %between.1 = (bf16[4,528,256]{2,1,0:T(8,128)(2,1)S(1)}, f32[256,512]{1,0:T(8,128)S(1)}) custom-call(bf16[32,32,256]{2,1,0:T(8,128)(2,1)S(1)} %all_to_all.20.in_ref.pack_ref, bf16[256,1280]{1,0:T(8,128)(2,1)S(1)} %copy-done.1, f32[2,34,256]{2,1,0:T(8,128)S(1)} %copy-done.6, bf16[32,16,256]{2,1,0:T(8,128)(2,1)S(1)} %all_to_all.21.conv_ref, ...), custom_call_target="tpu_custom_call" | custom-call | tf_op jit(solution)/shard_map/between/pallas_call | solution.py:281
  49.4 0.4 collective-permute-done.2
  49.8 0.3 grad.1
  50.1 12.9 %all_to_all.22.in_ref = bf16[32,16,256]{2,1,0:T(8,128)(2,1)S(1)} all-to-all(bf16[32,16,256]{2,1,0:T(8,128)(2,1)S(1)} %grad.1), channel_id=1, replica_groups=mesh['seq'=32,'chan'=8] {'seq'}, dimensions={0} | all-to-all | bytes 524288 | tf_op jit(solution)/shard_map/all_to_all | solution.py:353
  63.0 2.6 %backward.1 = (bf16[32,72,128]{2,1,0:T(8,128)(2,1)S(1)}, bf16[256,512]{1,0:T(8,128)(2,1)S(1)}, bf16[256,512]{1,0:T(8,128)(2,1)}, bf16[256,512]{1,0:T(8,128)(2,1)}) custom-call(bf16[32,16,256]{2,1,0:T(8,128)(2,1)S(1)} %all_to_all.22.in_ref, bf16[32,32,256]{2,1,0:T(8,128)(2,1)S(1)} %all_to_all.20.in_ref.pack_ref, ...), custom_call_target="tpu_custom_call" | custom-call | tf_op jit(solution)/shard_map/backward/pallas_call | solution.py:281
  65.6 14.7 %all_to_all.23.in_ref = bf16[32,72,128]{2,1,0:T(8,128)(2,1)S(1)} all-to-all(bf16[32,72,128]{2,1,0:T(8,128)(2,1)S(1)} %get-tuple-element.26), channel_id=1, replica_groups=mesh['seq'=32,'chan'=8] {'seq'}, dimensions={0} | all-to-all | bytes 1179648 | tf_op jit(solution)/shard_map/all_to_all | solution.py:371
  80.2 1.1 %last.1 = (bf16[256,512]{1,0:T(8,128)(2,1)}, bf16[256,512]{1,0:T(8,128)(2,1)}, bf16[256,512]{1,0:T(8,128)(2,1)}, f32[1,512]{1,0:T(1,128)}) custom-call(bf16[32,72,128]{2,1,0:T(8,128)(2,1)S(1)} %all_to_all.23.in_ref, bf16[256,512]{1,0:T(8,128)(2,1)S(1)} %get-tuple-element.27.grad_ref, bf16[256,512]{1,0:T(8,128)(2,1)S(1)} %copy-done.2, ...), custom_call_target="tpu_custom_call" | custom-call | tf_op jit(solution)/shard_map/last/pallas_call | solution.py:281
  (3 shorter events, 0.0 us)
Async XLA Ops:
  0.6 21.6 %copy-start.1 = (bf16[256,1280]{1,0:T(8,128)(2,1)S(1)}, bf16[256,1280]{1,0:T(8,128)(2,1)}, u32[]{:S(2)}) copy-start(bf16[256,1280]{1,0:T(8,128)(2,1)} %constant.4.clone.steps_ref) | copy-start | bytes 1966084
  0.6 21.6 %copy-start.4 = (bf16[256,512]{1,0:T(8,128)(2,1)S(1)}, bf16[256,512]{1,0:T(8,128)(2,1)}, u32[]{:S(2)}) copy-start(bf16[256,512]{1,0:T(8,128)(2,1)} %gate_ref.3) | copy-start | bytes 786436
  2.8 19.4 %copy-start.5 = (bf16[256,512]{1,0:T(8,128)(2,1)S(1)}, bf16[256,512]{1,0:T(8,128)(2,1)}, u32[]{:S(2)}) copy-start(bf16[256,512]{1,0:T(8,128)(2,1)} %cot_ref.3) | copy-start | bytes 786436
  2.9 19.4 %copy-start.6 = (f32[2,34,256]{2,1,0:T(8,128)S(1)}, f32[2,34,256]{2,1,0:T(8,128)}, u32[]{:S(2)}) copy-start(f32[2,34,256]{2,1,0:T(8,128)} %constant.5.clone.turn_ref) | copy-start | bytes 208900
  22.3 14.5 %copy-start = (bf16[32,32,256]{2,1,0:T(8,128)(2,1)S(1)}, bf16[32,32,256]{2,1,0:T(8,128)(2,1)}, u32[]{:S(2)}) copy-start(bf16[32,32,256]{2,1,0:T(8,128)(2,1)} %pack.1.pack_ref) | copy-start | bytes 1572868
  22.3 14.5 %copy-start.7 = (f32[512]{0:T(512)S(1)}, f32[512]{0:T(512)}, u32[]{:S(2)}) copy-start(f32[512]{0:T(512)} %param.13) | copy-start | bytes 6148
  22.3 14.5 %copy-start.8 = (f32[512]{0:T(512)S(1)}, f32[512]{0:T(512)}, u32[]{:S(2)}) copy-start(f32[512]{0:T(512)} %param.14) | copy-start | bytes 6148
  23.9 24.4 %copy-start.2 = (bf16[256,512]{1,0:T(8,128)(2,1)S(1)}, bf16[256,512]{1,0:T(8,128)(2,1)}, u32[]{:S(2)}) copy-start(bf16[256,512]{1,0:T(8,128)(2,1)} %key_ref.3) | copy-start | bytes 786436
  23.9 24.3 %copy-start.3 = (bf16[256,512]{1,0:T(8,128)(2,1)S(1)}, bf16[256,512]{1,0:T(8,128)(2,1)}, u32[]{:S(2)}) copy-start(bf16[256,512]{1,0:T(8,128)(2,1)} %value_ref.3) | copy-start | bytes 786436
  37.1 1.2 %collective-permute-start = (f32[2,256]{1,0:T(2,128)S(1)}, f32[2,256]{1,0:T(2,128)S(1)}, u32[]{:S(2)}, u32[]{:S(2)}) collective-permute-start(f32[2,256]{1,0:T(2,128)S(1)} %sums.1), channel_id=1, source_target_pairs={{0,1},{1,0},{2,3},{3,2},{4,5},{5,4},{6,7},{7,6},{8,9},{9,8},{10,11... | collective-permute-start | bytes 6152 | tf_op jit(solution)/shard_map/ppermute | solution.py:293
  38.4 4.8 %collective-permute-start.1 = (f32[2,256]{1,0:T(2,128)S(1)}, f32[2,256]{1,0:T(2,128)S(1)}, u32[]{:S(2)}, u32[]{:S(2)}) collective-permute-start(f32[2,256]{1,0:T(2,128)S(1)} %add.9), channel_id=1, source_target_pairs={{0,2},{1,3},{2,0},{3,1},{4,6},{5,7},{6,4},{7,5},{8,10},{9,11},{10,... | collective-permute-start | bytes 6152 | tf_op jit(solution)/shard_map/ppermute | solution.py:294
  43.2 6.6 %collective-permute-start.2 = (f32[2,256]{1,0:T(2,128)S(1)}, f32[2,256]{1,0:T(2,128)S(1)}, u32[]{:S(2)}, u32[]{:S(2)}) collective-permute-start(f32[2,256]{1,0:T(2,128)S(1)} %add.10.after_ref), channel_id=1, source_target_pairs={{0,6},{1,7},{2,4},{3,5},{4,2},{5,3},{6,0},{7,1},{8,14},{9,15},{10,... | collective-permute-start | bytes 6152 | tf_op jit(solution)/shard_map/ppermute | solution.py:299

commit v5 on v4

--- a/solution.py
+++ b/solution.py
@@ -130,26 +130,9 @@
     return rows.reshape(PARTS, PIECE, BLOCK)
 
 
-def pack_kernel(key_hbm, value_hbm, taps_hbm, out_hbm, key_ref, value_ref, taps_ref, out_ref, sems):
-    width, parts = WIDTH // 2, PARTS // 2
-    loads, stores = [], []
-    for half in range(2):
-        columns = pl.ds(half * width, width)
-        for source, target in ((key_hbm, key_ref), (value_hbm, value_ref), (taps_hbm, taps_ref)):
-            loads.append(pltpu.make_async_copy(source.at[:, columns], target.at[:, columns], sems.at[len(loads)]))
-            loads[-1].start()
-    for half in range(2):
-        columns, owners = pl.ds(half * width, width), pl.ds(half * parts, parts)
-        loads[3 * half].wait()
-        loads[3 * half + 1].wait()
-        mixed = key_ref[:, columns].astype(f32) * value_ref[:, columns].astype(f32)
-        out_ref[owners, :PIECE, :] = mixed.astype(bf16).T.reshape(parts, PIECE, BLOCK)
-        loads[3 * half + 2].wait()
-        out_ref[owners, PIECE:, :] = taps_ref[:, columns].T.reshape(parts, PIECE, BLOCK)
-        stores.append(pltpu.make_async_copy(out_ref.at[owners], out_hbm.at[owners], sems.at[6 + half]))
-        stores[-1].start()
-    for store in stores:
-        store.wait()
+def pack_kernel(mixed_ref, taps_ref, out_ref):
+    out_ref[:, :PIECE, :] = cut(mixed_ref[...].T)
+    out_ref[:, PIECE:, :] = cut(taps_ref[...].T)
 
 
 def forward_kernel(in_ref, steps_ref, turn_ref, gate_ref, cot_ref, out_ref, gate_out, cot_out):
@@ -222,21 +205,15 @@
 
 def backward_kernel(
     in_ref, pack_ref, spec_ref, steps_ref, turn_ref, sums_ref, full_ref, gate_ref, cot_ref, gain_ref,
-    out_ref, grad_out, normed_hbm, gate_hbm, normed_ref, gate_out, sems,
+    out_ref, grad_out, normed_out, gate_out,
 ):
     inv_rms, pull = (wide_column(row) for row in norm_parts(sums_ref))
     full, gate, gain = full_ref[...], gate_ref[...].astype(f32), gain_ref[...]
     gated = gate * full
-    normed_ref[...] = (gated * inv_rms * gain).astype(bf16)
+    normed_out[...] = (gated * inv_rms * gain).astype(bf16)
     grad_gated = inv_rms * (cot_ref[...].astype(f32) * gain) - gated * pull
     gate_out[...] = (grad_gated * full).astype(bf16)
     grad_out[...] = (grad_gated * gate).astype(bf16)
-    copies = [
-        pltpu.make_async_copy(normed_ref, normed_hbm, sems.at[0]),
-        pltpu.make_async_copy(gate_out, gate_hbm, sems.at[1]),
-    ]
-    for copy in copies:
-        copy.start()
     enter, leave, inner, turn, pair = open_tables(steps_ref, turn_ref)
     grad = in_ref[...]
     bias = jnp.sum(grad.astype(f32) * pack_ref[:, :PIECE, :].astype(f32), axis=0)
@@ -257,11 +234,19 @@
         result = invert(*products, leave, inner, turn, pair).astype(bf16)
         out_ref[:, 2 * place * PIECE : (2 * place + 1) * PIECE, :] = result[:, :, :128]
         out_ref[:, (2 * place + 1) * PIECE : (2 * place + 2) * PIECE, :] = result[:, :, 128:]
+
+
+def last_kernel(
+    in_ref, grad_ref, key_ref, value_ref, skip_ref, normed_ref, gate_ref,
+    key_out, value_out, taps_out, bias_out, normed_hbm, gate_hbm, sems,
+):
+    copies = [
+        pltpu.make_async_copy(normed_ref, normed_hbm, sems.at[0]),
+        pltpu.make_async_copy(gate_ref, gate_hbm, sems.at[1]),
+    ]
     for copy in copies:
-        copy.wait()
-
-
-def last_kernel(in_ref, grad_ref, key_ref, value_ref, skip_ref, key_out, value_out, taps_out, bias_out):
+        copy.start()
+
     def whole(place):
         at = 2 * place * PIECE
         left, right = in_ref[:, at : at + PIECE, :], in_ref[:, at + PIECE : at + 2 * PIECE, :]
@@ -274,18 +259,20 @@
     tail = in_ref[:, 4 * PIECE :, :].astype(f32)
     tail = jnp.concatenate([tail, pltpu.roll(tail, 126, 2)], 1).reshape(WIDTH, 128).T
     bias_out[...] = tail[0:1] + tail[1:2]
-
-
-def call(kernel, name, outs, *operands, hbm_in=(), hbm_out=(), scratch=(), grant=32 * 1024):
+    for copy in copies:
+        copy.wait()
+
+
+def call(kernel, name, outs, *operands, hbm_out=(), scratch=()):
     vmem, hbm = pl.BlockSpec(memory_space=pltpu.VMEM), pl.BlockSpec(memory_space=pltpu.HBM)
     return pl.pallas_call(
         kernel,
         name=name,
         out_shape=[jax.ShapeDtypeStruct(shape, kind) for shape, kind in outs],
-        in_specs=[hbm if place in hbm_in else vmem for place in range(len(operands))],
+        in_specs=[vmem] * len(operands),
         out_specs=[hbm if place in hbm_out else vmem for place in range(len(outs))],
         scratch_shapes=list(scratch),
-        compiler_params=pltpu.CompilerParams(vmem_limit_bytes=grant * 1024),
+        compiler_params=pltpu.CompilerParams(vmem_limit_bytes=32 * 1024 * 1024),
     )(*operands)
 
 
@@ -306,20 +293,10 @@
     turned = ((WIDTH, BLOCK), bf16)
     pieces = ((PARTS, PIECE, BLOCK), bf16)
     spectra = ((4, ROWS, BLOCK), bf16)
-    whole = pltpu.VMEM(*natural)
-
-    (packed,) = call(
-        pack_kernel,
-        "pack",
-        [((PARTS, 2 * PIECE, BLOCK), bf16)],
-        key_feat,
-        value_feat,
-        filter_taps,
-        hbm_in=(0, 1, 2),
-        hbm_out=(0,),
-        scratch=[whole, whole, whole, pltpu.VMEM((PARTS, 2 * PIECE, BLOCK), bf16), pltpu.SemaphoreType.DMA((8,))],
-        grant=63 * 1024,
-    )
+
+    mixed = (key_feat.astype(f32) * value_feat.astype(f32)).astype(bf16)
+    taps = jnp.where(key_feat == key_feat, filter_taps, mixed)
+    (packed,) = call(pack_kernel, "pack", [((PARTS, 2 * PIECE, BLOCK), bf16)], mixed, taps)
     arrived = lax.all_to_all(packed, "seq", 0, 0, tiled=True)
     conv, gate_t, cot_t = call(
         forward_kernel,
@@ -351,7 +328,7 @@
     sums = add_over_mirror(sums)
     (grad,) = call(grad_kernel, "grad", [pieces], sums, *sides, full)
     grad_arrived = lax.all_to_all(grad, "seq", 0, 0, tiled=True)
-    result, grad_conv, normed_out, grad_gate = call(
+    result, grad_conv, normed, gate = call(
         backward_kernel,
         "backward",
         [((PARTS, 4 * PIECE + TAIL, 128), bf16), natural, natural, natural],
@@ -365,19 +342,21 @@
         gate_feat,
         cotangent,
         gain_row,
-        hbm_out=(2, 3),
-        scratch=[whole, whole, pltpu.SemaphoreType.DMA((2,))],
     )
     result = lax.all_to_all(result, "seq", 0, 0, tiled=True)
-    grad_key, grad_value, grad_filter, grad_bias = call(
+    grad_key, grad_value, grad_filter, grad_bias, normed_out, grad_gate = call(
         last_kernel,
         "last",
-        [natural] * 3 + [((1, WIDTH), f32)],
+        [natural] * 3 + [((1, WIDTH), f32)] + [natural] * 2,
         result,
         grad_conv,
         key_feat,
         value_feat,
         skip_row,
+        normed,
+        gate,
+        hbm_out=(4, 5),
+        scratch=[pltpu.SemaphoreType.DMA((2,))],
     )
     return normed_out, grad_gate, grad_key, grad_value, grad_filter, grad_bias[0]
 

time: 82.4 us -> 81.4 us (0.988)
  Pallas kernels: 9.2 us -> 7.11 us
  other arithmetic: 0.01 us -> 1.34 us
    pallas_call x7, Pallas kernels: 9.2 us -> 7.11 us  [call(): pl.pallas_call(kernel, name=name, out_shape=[jax.ShapeDtypeStruct(shape,...]
    select_n x0 -> x1, other arithmetic: none -> 1.33 us  [on_device(): taps = jnp.where(key_feat == key_feat, filter_taps, mixed)]
where the time goes in v5:
time: 81.4 us; the launch traced here: 80.4 us
  blocking collectives  59.6 us (73%)
  starting transfers between devices  8.42 us (10%)
  Pallas kernels  7.11 us (9%)
  waiting for transfers between devices  3.13 us (4%)
  other arithmetic  1.34 us (2%)
    all_to_all x1, blocking collectives, on_device(): arrived = lax.all_to_all(packed, 'seq', 0, 0, tiled=True)  19.2 us
    all_to_all x1, blocking collectives, on_device(): result = lax.all_to_all(result, 'seq', 0, 0, tiled=True)  14.7 us
    all_to_all x1, blocking collectives, on_device(): conv = lax.all_to_all(conv, 'seq', 0, 0, tiled=True)  12.9 us
    all_to_all x1, blocking collectives, on_device(): grad_arrived = lax.all_to_all(grad, 'seq', 0, 0, tiled=True)  12.9 us
    pallas_call x7, Pallas kernels, call(): pl.pallas_call(kernel, name=name, out_shape=[jax.ShapeDtypeStruct(shape,...  7.11 us
    ppermute x1, starting transfers between devices, add_over_mirror(): return sums + lax.ppermute(sums, 'chan', mirror)  5.05 us
    ppermute x1, starting transfers between devices, add_over_pairs(): lax.ppermute(sums, 'chan', [(at, at ^ 2) for at in range(GROUP)])  3.27 us
  transfers between devices with their start and end apart: 3, of which 3 were waited for; matrix products, arithmetic and copies ran while one was open for 0% of the time, Pallas kernels for 1%

profile of v5, /device:TPU:0, one launch (start us, length us, event | category | flops | bytes accessed | tf_op | source)
XLA Modules:
  0.0 80.4 jit_solution(15867823829003150558)
XLA Ops:
  0.6 1.3 %compare_select_fusion = (bf16[256,512]{1,0:T(8,128)(2,1)S(1)}, bf16[256,512]{1,0:T(8,128)(2,1)S(1)}) fusion(bf16[256,512]{1,0:T(8,128)(2,1)} %param.12, bf16[256,512]{1,0:T(8,128)(2,1)} %key_ref.3, bf16[256,512]{1,0:T(8,128)(2,1)} %value_ref.3), kind=kLoop, calls=%fused_computation.1 | loop fusion | flops 786432 | bytes 1310720 | tf_op jit(solution)/shard_map/jit(_where)/select_n | solution.py:298
  2.0 0.0 copy-start
  2.0 0.0 copy-start.3
  2.0 0.0 copy-start.4
  2.0 0.0 copy-start.5
  2.0 0.2 pack.1.pack_ref
  2.2 19.2 %all_to_all.20.in_ref.pack_ref = bf16[32,32,256]{2,1,0:T(8,128)(2,1)S(1)} all-to-all(bf16[32,32,256]{2,1,0:T(8,128)(2,1)S(1)} %pack.1.pack_ref), channel_id=1, replica_groups=mesh['seq'=32,'chan'=8] {'seq'}, dimensions={0} | all-to-all | bytes 1048576 | tf_op jit(solution)/shard_map/all_to_all | solution.py:300
  21.4 0.0 copy-done
  21.4 0.0 copy-done.3
  21.4 0.0 copy-done.4
  21.4 0.0 copy-done.5
  21.4 0.0 copy-start.6
  21.4 0.0 copy-start.7
  21.4 1.6 %forward.1 = (bf16[32,16,256]{2,1,0:T(8,128)(2,1)S(1)}, bf16[512,256]{1,0:T(8,128)(2,1)S(1)}, bf16[512,256]{1,0:T(8,128)(2,1)S(1)}) custom-call(bf16[32,32,256]{2,1,0:T(8,128)(2,1)S(1)} %all_to_all.20.in_ref.pack_ref, bf16[256,1280]{1,0:T(8,128)(2,1)S(1)} %copy-done, f32[2,34,256]{2,1,0:T(8,128)S(1)} %copy-done.5, bf16[256,512]{1,0:T(8,128)(2,1)S(1)} %copy-done.3, ...), custom_call_target="tpu_custom_call" | custom-call | tf_op jit(solution)/shard_map/forward/pallas_call | solution.py:268
  23.0 0.0 copy-start.1
  23.0 0.0 copy-start.2
  23.0 12.9 %all_to_all.21.conv_ref = bf16[32,16,256]{2,1,0:T(8,128)(2,1)S(1)} all-to-all(bf16[32,16,256]{2,1,0:T(8,128)(2,1)S(1)} %get-tuple-element.21), channel_id=1, replica_groups=mesh['seq'=32,'chan'=8] {'seq'}, dimensions={0} | all-to-all | bytes 524288 | tf_op jit(solution)/shard_map/all_to_all | solution.py:311
  35.9 0.0 copy-done.6
  35.9 0.0 copy-done.7
  35.9 0.3 sums.1
  36.2 0.1 collective-permute-start
  36.3 1.1 %collective-permute-done = f32[2,256]{1,0:T(2,128)S(1)} collective-permute-done((f32[2,256]{1,0:T(2,128)S(1)}, f32[2,256]{1,0:T(2,128)S(1)}, u32[]{:S(2)}, u32[]{:S(2)}) %collective-permute-start) | collective-permute-done | bytes 2080 | tf_op jit(solution)/shard_map/ppermute | solution.py:280
  37.5 3.3 %collective-permute-start.1 = (f32[2,256]{1,0:T(2,128)S(1)}, f32[2,256]{1,0:T(2,128)S(1)}, u32[]{:S(2)}, u32[]{:S(2)}) collective-permute-start(f32[2,256]{1,0:T(2,128)S(1)} %add.9), channel_id=1, source_target_pairs={{0,2},{1,3},{2,0},{3,1},{4,6},{5,7},{6,4},{7,5},{8,10},{9,11},{10,... | collective-permute-start | bytes 6152 | tf_op jit(solution)/shard_map/ppermute | solution.py:281
  40.8 1.6 %collective-permute-done.1 = f32[2,256]{1,0:T(2,128)S(1)} collective-permute-done((f32[2,256]{1,0:T(2,128)S(1)}, f32[2,256]{1,0:T(2,128)S(1)}, u32[]{:S(2)}, u32[]{:S(2)}) %collective-permute-start.1) | collective-permute-done | bytes 2080 | tf_op jit(solution)/shard_map/ppermute | solution.py:281
  42.3 5.1 %collective-permute-start.2 = (f32[2,256]{1,0:T(2,128)S(1)}, f32[2,256]{1,0:T(2,128)S(1)}, u32[]{:S(2)}, u32[]{:S(2)}) collective-permute-start(f32[2,256]{1,0:T(2,128)S(1)} %add.10.after_ref), channel_id=1, source_target_pairs={{0,6},{1,7},{2,4},{3,5},{4,2},{5,3},{6,0},{7,1},{8,14},{9,15},{10,... | collective-permute-start | bytes 6152 | tf_op jit(solution)/shard_map/ppermute | solution.py:286
  47.4 0.0 copy-done.1
  47.4 0.0 copy-done.2
  47.4 1.1 %between.1 = (bf16[4,528,256]{2,1,0:T(8,128)(2,1)S(1)}, f32[256,512]{1,0:T(8,128)S(1)}) custom-call(bf16[32,32,256]{2,1,0:T(8,128)(2,1)S(1)} %all_to_all.20.in_ref.pack_ref, bf16[256,1280]{1,0:T(8,128)(2,1)S(1)} %copy-done, f32[2,34,256]{2,1,0:T(8,128)S(1)} %copy-done.5, bf16[32,16,256]{2,1,0:T(8,128)(2,1)S(1)} %all_to_all.21.conv_ref, ...), custom_call_target="tpu_custom_call" | custom-call | tf_op jit(solution)/shard_map/between/pallas_call | solution.py:268
  48.5 0.4 collective-permute-done.2
  48.9 0.3 grad.1
  49.3 12.9 %all_to_all.22.in_ref = bf16[32,16,256]{2,1,0:T(8,128)(2,1)S(1)} all-to-all(bf16[32,16,256]{2,1,0:T(8,128)(2,1)S(1)} %grad.1), channel_id=1, replica_groups=mesh['seq'=32,'chan'=8] {'seq'}, dimensions={0} | all-to-all | bytes 524288 | tf_op jit(solution)/shard_map/all_to_all | solution.py:330
  62.1 1.8 %backward.1 = (bf16[32,72,128]{2,1,0:T(8,128)(2,1)S(1)}, bf16[256,512]{1,0:T(8,128)(2,1)S(1)}, bf16[256,512]{1,0:T(8,128)(2,1)S(1)}, bf16[256,512]{1,0:T(8,128)(2,1)S(1)}) custom-call(bf16[32,16,256]{2,1,0:T(8,128)(2,1)S(1)} %all_to_all.22.in_ref, bf16[32,32,256]{2,1,0:T(8,128)(2,1)S(1)} %all_to_all.20.in_ref.pack_ref, ...), custom_call_target="tpu_custom_call" | custom-call | tf_op jit(solution)/shard_map/backward/pallas_call | solution.py:268
  63.9 14.7 %all_to_all.23.in_ref = bf16[32,72,128]{2,1,0:T(8,128)(2,1)S(1)} all-to-all(bf16[32,72,128]{2,1,0:T(8,128)(2,1)S(1)} %get-tuple-element.26), channel_id=1, replica_groups=mesh['seq'=32,'chan'=8] {'seq'}, dimensions={0} | all-to-all | bytes 1179648 | tf_op jit(solution)/shard_map/all_to_all | solution.py:346
  78.6 1.8 %last.1 = (bf16[256,512]{1,0:T(8,128)(2,1)}, bf16[256,512]{1,0:T(8,128)(2,1)}, bf16[256,512]{1,0:T(8,128)(2,1)}, f32[1,512]{1,0:T(1,128)}, bf16[256,512]{1,0:T(8,128)(2,1)}, /*index=5*/bf16[256,512]{1,0:T(8,128)(2,1)}) custom-call(bf16[32,72,128]{2,1,0:T(8,128)(2,1)S(1)} %all_to_all.23.in_ref, bf16[256,512]{1,0:T(8,128)(2,1)S(1)} %get-tuple-element.27.grad_ref, ...), custom_call_target="tpu_custom_call" | custom-call | tf_op jit(solution)/shard_map/last/pallas_call | solution.py:268
  (3 shorter events, 0.0 us)
Async XLA Ops:
  2.0 19.4 %copy-start = (bf16[256,1280]{1,0:T(8,128)(2,1)S(1)}, bf16[256,1280]{1,0:T(8,128)(2,1)}, u32[]{:S(2)}) copy-start(bf16[256,1280]{1,0:T(8,128)(2,1)} %constant.4.clone.steps_ref) | copy-start | bytes 1966084
  2.0 19.4 %copy-start.3 = (bf16[256,512]{1,0:T(8,128)(2,1)S(1)}, bf16[256,512]{1,0:T(8,128)(2,1)}, u32[]{:S(2)}) copy-start(bf16[256,512]{1,0:T(8,128)(2,1)} %gate_ref.3) | copy-start | bytes 786436
  2.0 19.4 %copy-start.4 = (bf16[256,512]{1,0:T(8,128)(2,1)S(1)}, bf16[256,512]{1,0:T(8,128)(2,1)}, u32[]{:S(2)}) copy-start(bf16[256,512]{1,0:T(8,128)(2,1)} %cot_ref.3) | copy-start | bytes 786436
  2.0 19.4 %copy-start.5 = (f32[2,34,256]{2,1,0:T(8,128)S(1)}, f32[2,34,256]{2,1,0:T(8,128)}, u32[]{:S(2)}) copy-start(f32[2,34,256]{2,1,0:T(8,128)} %constant.5.clone.turn_ref) | copy-start | bytes 208900
  21.4 14.6 %copy-start.6 = (f32[512]{0:T(512)S(1)}, f32[512]{0:T(512)}, u32[]{:S(2)}) copy-start(f32[512]{0:T(512)} %param.13) | copy-start | bytes 6148
  21.4 14.5 %copy-start.7 = (f32[512]{0:T(512)S(1)}, f32[512]{0:T(512)}, u32[]{:S(2)}) copy-start(f32[512]{0:T(512)} %param.14) | copy-start | bytes 6148
  23.0 24.4 %copy-start.1 = (bf16[256,512]{1,0:T(8,128)(2,1)S(1)}, bf16[256,512]{1,0:T(8,128)(2,1)}, u32[]{:S(2)}) copy-start(bf16[256,512]{1,0:T(8,128)(2,1)} %key_ref.3) | copy-start | bytes 786436
  23.0 24.4 %copy-start.2 = (bf16[256,512]{1,0:T(8,128)(2,1)S(1)}, bf16[256,512]{1,0:T(8,128)(2,1)}, u32[]{:S(2)}) copy-start(bf16[256,512]{1,0:T(8,128)(2,1)} %value_ref.3) | copy-start | bytes 786436
  36.2 1.2 %collective-permute-start = (f32[2,256]{1,0:T(2,128)S(1)}, f32[2,256]{1,0:T(2,128)S(1)}, u32[]{:S(2)}, u32[]{:S(2)}) collective-permute-start(f32[2,256]{1,0:T(2,128)S(1)} %sums.1), channel_id=1, source_target_pairs={{0,1},{1,0},{2,3},{3,2},{4,5},{5,4},{6,7},{7,6},{8,9},{9,8},{10,11... | collective-permute-start | bytes 6152 | tf_op jit(solution)/shard_map/ppermute | solution.py:280
  37.5 4.8 %collective-permute-start.1 = (f32[2,256]{1,0:T(2,128)S(1)}, f32[2,256]{1,0:T(2,128)S(1)}, u32[]{:S(2)}, u32[]{:S(2)}) collective-permute-start(f32[2,256]{1,0:T(2,128)S(1)} %add.9), channel_id=1, source_target_pairs={{0,2},{1,3},{2,0},{3,1},{4,6},{5,7},{6,4},{7,5},{8,10},{9,11},{10,... | collective-permute-start | bytes 6152 | tf_op jit(solution)/shard_map/ppermute | solution.py:281
  42.3 6.6 %collective-permute-start.2 = (f32[2,256]{1,0:T(2,128)S(1)}, f32[2,256]{1,0:T(2,128)S(1)}, u32[]{:S(2)}, u32[]{:S(2)}) collective-permute-start(f32[2,256]{1,0:T(2,128)S(1)} %add.10.after_ref), channel_id=1, source_target_pairs={{0,6},{1,7},{2,4},{3,5},{4,2},{5,3},{6,0},{7,1},{8,14},{9,15},{10,... | collective-permute-start | bytes 6152 | tf_op jit(solution)/shard_map/ppermute | solution.py:286

commit v6 on v5

--- a/solution.py
+++ b/solution.py
@@ -81,12 +81,15 @@
     return jnp.concatenate(parts, 1).reshape(ROWS, NEAR).astype(bf16)
 
 
-def spectrum(signal, enter, inner, turn, pair):
+def enter_blocks(signal, enter):
     wide = signal.astype(f32)
+    halves = [wide[:, half * HALF : (half + 1) * HALF].reshape(PARTS * HALF, BLOCK) for half in range(2)]
+    return [dot(enter, half.astype(bf16)) for half in halves]
+
+
+def finish_spectrum(halves, inner, turn, pair):
     pieces = ([], [], [], [])
-    for half in range(2):
-        rows = wide[:, half * HALF : (half + 1) * HALF].reshape(PARTS * HALF, BLOCK)
-        mixed = dot(enter, rows.astype(bf16))
+    for mixed in halves:
         real, imag = rotate_first(mixed[: BINS * HALF], mixed[BINS * HALF :], turn)
         pieces[0].append(real[:, :NEAR] + real[:, NEAR:])
         pieces[1].append(imag[:, :NEAR] + imag[:, NEAR:])
@@ -97,15 +100,18 @@
     return [dot(jnp.concatenate(pieces[at : at + 2], 1), inner) for at in (0, 2)]
 
 
-def invert(even, odd, leave, inner, turn, pair):
-    even, odd = [
+def invert_inner(products, inner):
+    return [
         dot(jnp.concatenate([real.astype(bf16), imag.astype(bf16)], 1), inner).reshape(BINS, PIECE, BLOCK)
-        for real, imag in (even, odd)
+        for real, imag in products
     ]
+
+
+def finish_inverse(parts, leave, turn, pair):
     outs = []
     for half in range(2):
         rows = slice(half * HALF, (half + 1) * HALF)
-        first, second = [part[:, rows].reshape(BINS * HALF, BLOCK) for part in (even, odd)]
+        first, second = [part[:, rows].reshape(BINS * HALF, BLOCK) for part in parts]
         first_re, first_im = first[:, :NEAR], first[:, NEAR:]
         second_re, second_im = rotate(second[:, :NEAR], second[:, NEAR:], pair)
         real = jnp.concatenate([first_re + second_re, first_re - second_re], 1)
@@ -139,14 +145,15 @@
     gate_out[...] = gate_ref[...].T
     cot_out[...] = cot_ref[...].T
     enter, leave, inner, turn, pair = open_tables(steps_ref, turn_ref)
-    first = spectrum(in_ref[:, :PIECE, :], enter, inner, turn, pair)
-    second = spectrum(in_ref[:, PIECE:, :], enter, inner, turn, pair)
+    first = enter_blocks(in_ref[:, :PIECE, :], enter)
+    second = enter_blocks(in_ref[:, PIECE:, :], enter)
+    first, second = [finish_spectrum(halves, inner, turn, pair) for halves in (first, second)]
     products = []
     for one, other in zip(first, second, strict=True):
         one_re, one_im = parts_of(one)
         other_re, other_im = parts_of(other)
         products.append((one_re * other_re - one_im * other_im, -(one_re * other_im + one_im * other_re)))
-    out_ref[...] = invert(*products, leave, inner, turn, pair).astype(bf16)
+    out_ref[...] = finish_inverse(invert_inner(products, inner), leave, turn, pair).astype(bf16)
 
 
 def between_kernel(
@@ -155,7 +162,7 @@
     enter, _, inner, turn, pair = open_tables(steps_ref, turn_ref)
     for place in range(2):
         signal = in_ref[:, place * PIECE : (place + 1) * PIECE, :]
-        even, odd = spectrum(signal, enter, inner, turn, pair)
+        even, odd = finish_spectrum(enter_blocks(signal, enter), inner, turn, pair)
         spec_ref[2 * place] = even.astype(bf16)
         spec_ref[2 * place + 1] = odd.astype(bf16)
     mixed = (key_ref[...].astype(f32) * value_ref[...].astype(f32)).astype(bf16)
@@ -224,28 +231,27 @@
     for at, part in enumerate((high[:HALF], (bias - high)[:HALF], high[HALF:], (bias - high)[HALF:])):
         tail = jnp.where(lane == at, part, tail)
     out_ref[:, 4 * PIECE :, :] = jnp.broadcast_to(tail.astype(bf16)[None], (PARTS, TAIL, 128))
-    spectra = spectrum(grad, enter, inner, turn, pair)
-    for place, other in ((0, 1), (1, 0)):
+    spectra = finish_spectrum(enter_blocks(grad, enter), inner, turn, pair)
+    inverses = []
+    for other in (1, 0):
         products = []
         for parity, mine in enumerate(spectra):
             real, imag = parts_of(spec_ref[2 * other + parity])
             mine_re, mine_im = parts_of(mine)
             products.append((real * mine_re + imag * mine_im, imag * mine_re - real * mine_im))
-        result = invert(*products, leave, inner, turn, pair).astype(bf16)
+        inverses.append(invert_inner(products, inner))
+    for place, parts in enumerate(inverses):
+        result = finish_inverse(parts, leave, turn, pair).astype(bf16)
         out_ref[:, 2 * place * PIECE : (2 * place + 1) * PIECE, :] = result[:, :, :128]
         out_ref[:, (2 * place + 1) * PIECE : (2 * place + 2) * PIECE, :] = result[:, :, 128:]
 
 
 def last_kernel(
     in_ref, grad_ref, key_ref, value_ref, skip_ref, normed_ref, gate_ref,
-    key_out, value_out, taps_out, bias_out, normed_hbm, gate_hbm, sems,
+    key_out, value_out, taps_out, bias_out, normed_out, gate_out,
 ):
-    copies = [
-        pltpu.make_async_copy(normed_ref, normed_hbm, sems.at[0]),
-        pltpu.make_async_copy(gate_ref, gate_hbm, sems.at[1]),
-    ]
-    for copy in copies:
-        copy.start()
+    normed_out[...] = normed_ref[...]
+    gate_out[...] = gate_ref[...]
 
     def whole(place):
         at = 2 * place * PIECE
@@ -259,19 +265,16 @@
     tail = in_ref[:, 4 * PIECE :, :].astype(f32)
     tail = jnp.concatenate([tail, pltpu.roll(tail, 126, 2)], 1).reshape(WIDTH, 128).T
     bias_out[...] = tail[0:1] + tail[1:2]
-    for copy in copies:
-        copy.wait()
-
-
-def call(kernel, name, outs, *operands, hbm_out=(), scratch=()):
-    vmem, hbm = pl.BlockSpec(memory_space=pltpu.VMEM), pl.BlockSpec(memory_space=pltpu.HBM)
+
+
+def call(kernel, name, outs, *operands):
+    vmem = pl.BlockSpec(memory_space=pltpu.VMEM)
     return pl.pallas_call(
         kernel,
         name=name,
         out_shape=[jax.ShapeDtypeStruct(shape, kind) for shape, kind in outs],
         in_specs=[vmem] * len(operands),
-        out_specs=[hbm if place in hbm_out else vmem for place in range(len(outs))],
-        scratch_shapes=list(scratch),
+        out_specs=[vmem] * len(outs),
         compiler_params=pltpu.CompilerParams(vmem_limit_bytes=32 * 1024 * 1024),
     )(*operands)
 
@@ -355,8 +358,6 @@
         skip_row,
         normed,
         gate,
-        hbm_out=(4, 5),
-        scratch=[pltpu.SemaphoreType.DMA((2,))],
     )
     return normed_out, grad_gate, grad_key, grad_value, grad_filter, grad_bias[0]
 

time: 81.4 us -> 80.8 us (level)
  no operation moved by 1% of the time
where the time goes in v6:
time: 80.8 us; the launch traced here: 79.8 us
  blocking collectives  59.6 us (74%)
  starting transfers between devices  8.42 us (10%)
  Pallas kernels  6.53 us (8%)
  waiting for transfers between devices  3.12 us (4%)
  other arithmetic  1.34 us (2%)
    all_to_all x1, blocking collectives, on_device(): arrived = lax.all_to_all(packed, 'seq', 0, 0, tiled=True)  19.2 us
    all_to_all x1, blocking collectives, on_device(): result = lax.all_to_all(result, 'seq', 0, 0, tiled=True)  14.7 us
    all_to_all x1, blocking collectives, on_device(): conv = lax.all_to_all(conv, 'seq', 0, 0, tiled=True)  12.9 us
    all_to_all x1, blocking collectives, on_device(): grad_arrived = lax.all_to_all(grad, 'seq', 0, 0, tiled=True)  12.9 us
    pallas_call x7, Pallas kernels, call(): pl.pallas_call(kernel, name=name, out_shape=[jax.ShapeDtypeStruct(shape,...  6.53 us
    ppermute x1, starting transfers between devices, add_over_mirror(): return sums + lax.ppermute(sums, 'chan', mirror)  5.05 us
    ppermute x1, starting transfers between devices, add_over_pairs(): lax.ppermute(sums, 'chan', [(at, at ^ 2) for at in range(GROUP)])  3.27 us
  transfers between devices with their start and end apart: 3, of which 3 were waited for; matrix products, arithmetic and copies ran while one was open for 0% of the time, Pallas kernels for 1%

profile of v6, /device:TPU:0, one launch (start us, length us, event | category | flops | bytes accessed | tf_op | source)
XLA Modules:
  0.0 79.8 jit_solution(15937816597214527182)
XLA Ops:
  0.6 1.3 %compare_select_fusion = (bf16[256,512]{1,0:T(8,128)(2,1)S(1)}, bf16[256,512]{1,0:T(8,128)(2,1)S(1)}) fusion(bf16[256,512]{1,0:T(8,128)(2,1)} %param.12, bf16[256,512]{1,0:T(8,128)(2,1)} %key_ref.3, bf16[256,512]{1,0:T(8,128)(2,1)} %value_ref.3), kind=kLoop, calls=%fused_computation.1 | loop fusion | flops 786432 | bytes 1310720 | tf_op jit(solution)/shard_map/jit(_where)/select_n | solution.py:301
  2.0 0.0 copy-start
  2.0 0.0 copy-start.3
  2.0 0.0 copy-start.4
  2.0 0.0 copy-start.5
  2.0 0.2 pack.1.pack_ref
  2.2 19.2 %all_to_all.20.in_ref.pack_ref = bf16[32,32,256]{2,1,0:T(8,128)(2,1)S(1)} all-to-all(bf16[32,32,256]{2,1,0:T(8,128)(2,1)S(1)} %pack.1.pack_ref), channel_id=1, replica_groups=mesh['seq'=32,'chan'=8] {'seq'}, dimensions={0} | all-to-all | bytes 1048576 | tf_op jit(solution)/shard_map/all_to_all | solution.py:303
  21.4 0.0 copy-done
  21.4 0.0 copy-done.3
  21.4 0.0 copy-done.4
  21.4 0.0 copy-done.5
  21.4 0.0 copy-start.6
  21.4 0.0 copy-start.7
  21.4 1.5 %forward.1 = (bf16[32,16,256]{2,1,0:T(8,128)(2,1)S(1)}, bf16[512,256]{1,0:T(8,128)(2,1)S(1)}, bf16[512,256]{1,0:T(8,128)(2,1)S(1)}) custom-call(bf16[32,32,256]{2,1,0:T(8,128)(2,1)S(1)} %all_to_all.20.in_ref.pack_ref, bf16[256,1280]{1,0:T(8,128)(2,1)S(1)} %copy-done, f32[2,34,256]{2,1,0:T(8,128)S(1)} %copy-done.5, bf16[256,512]{1,0:T(8,128)(2,1)S(1)} %copy-done.3, ...), custom_call_target="tpu_custom_call" | custom-call | tf_op jit(solution)/shard_map/forward/pallas_call | solution.py:272
  22.9 0.0 copy-start.1
  22.9 0.0 copy-start.2
  23.0 12.9 %all_to_all.21.conv_ref = bf16[32,16,256]{2,1,0:T(8,128)(2,1)S(1)} all-to-all(bf16[32,16,256]{2,1,0:T(8,128)(2,1)S(1)} %get-tuple-element.21), channel_id=1, replica_groups=mesh['seq'=32,'chan'=8] {'seq'}, dimensions={0} | all-to-all | bytes 524288 | tf_op jit(solution)/shard_map/all_to_all | solution.py:314
  35.9 0.0 copy-done.6
  35.9 0.0 copy-done.7
  35.9 0.3 sums.1
  36.2 0.1 collective-permute-start
  36.3 1.1 %collective-permute-done = f32[2,256]{1,0:T(2,128)S(1)} collective-permute-done((f32[2,256]{1,0:T(2,128)S(1)}, f32[2,256]{1,0:T(2,128)S(1)}, u32[]{:S(2)}, u32[]{:S(2)}) %collective-permute-start) | collective-permute-done | bytes 2080 | tf_op jit(solution)/shard_map/ppermute | solution.py:283
  37.4 3.3 %collective-permute-start.1 = (f32[2,256]{1,0:T(2,128)S(1)}, f32[2,256]{1,0:T(2,128)S(1)}, u32[]{:S(2)}, u32[]{:S(2)}) collective-permute-start(f32[2,256]{1,0:T(2,128)S(1)} %add.9), channel_id=1, source_target_pairs={{0,2},{1,3},{2,0},{3,1},{4,6},{5,7},{6,4},{7,5},{8,10},{9,11},{10,... | collective-permute-start | bytes 6152 | tf_op jit(solution)/shard_map/ppermute | solution.py:284
  40.7 1.6 %collective-permute-done.1 = f32[2,256]{1,0:T(2,128)S(1)} collective-permute-done((f32[2,256]{1,0:T(2,128)S(1)}, f32[2,256]{1,0:T(2,128)S(1)}, u32[]{:S(2)}, u32[]{:S(2)}) %collective-permute-start.1) | collective-permute-done | bytes 2080 | tf_op jit(solution)/shard_map/ppermute | solution.py:284
  42.2 5.1 %collective-permute-start.2 = (f32[2,256]{1,0:T(2,128)S(1)}, f32[2,256]{1,0:T(2,128)S(1)}, u32[]{:S(2)}, u32[]{:S(2)}) collective-permute-start(f32[2,256]{1,0:T(2,128)S(1)} %add.10.after_ref), channel_id=1, source_target_pairs={{0,6},{1,7},{2,4},{3,5},{4,2},{5,3},{6,0},{7,1},{8,14},{9,15},{10,... | collective-permute-start | bytes 6152 | tf_op jit(solution)/shard_map/ppermute | solution.py:289
  47.3 0.0 copy-done.1
  47.3 0.0 copy-done.2
  47.3 1.1 %between.1 = (bf16[4,528,256]{2,1,0:T(8,128)(2,1)S(1)}, f32[256,512]{1,0:T(8,128)S(1)}) custom-call(bf16[32,32,256]{2,1,0:T(8,128)(2,1)S(1)} %all_to_all.20.in_ref.pack_ref, bf16[256,1280]{1,0:T(8,128)(2,1)S(1)} %copy-done, f32[2,34,256]{2,1,0:T(8,128)S(1)} %copy-done.5, bf16[32,16,256]{2,1,0:T(8,128)(2,1)S(1)} %all_to_all.21.conv_ref, ...), custom_call_target="tpu_custom_call" | custom-call | tf_op jit(solution)/shard_map/between/pallas_call | solution.py:272
  48.4 0.4 collective-permute-done.2
  48.9 0.3 grad.1
  49.2 12.9 %all_to_all.22.in_ref = bf16[32,16,256]{2,1,0:T(8,128)(2,1)S(1)} all-to-all(bf16[32,16,256]{2,1,0:T(8,128)(2,1)S(1)} %grad.1), channel_id=1, replica_groups=mesh['seq'=32,'chan'=8] {'seq'}, dimensions={0} | all-to-all | bytes 524288 | tf_op jit(solution)/shard_map/all_to_all | solution.py:333
  62.1 1.8 %backward.1 = (bf16[32,72,128]{2,1,0:T(8,128)(2,1)S(1)}, bf16[256,512]{1,0:T(8,128)(2,1)S(1)}, bf16[256,512]{1,0:T(8,128)(2,1)S(1)}, bf16[256,512]{1,0:T(8,128)(2,1)S(1)}) custom-call(bf16[32,16,256]{2,1,0:T(8,128)(2,1)S(1)} %all_to_all.22.in_ref, bf16[32,32,256]{2,1,0:T(8,128)(2,1)S(1)} %all_to_all.20.in_ref.pack_ref, ...), custom_call_target="tpu_custom_call" | custom-call | tf_op jit(solution)/shard_map/backward/pallas_call | solution.py:272
  63.9 14.7 %all_to_all.23.in_ref = bf16[32,72,128]{2,1,0:T(8,128)(2,1)S(1)} all-to-all(bf16[32,72,128]{2,1,0:T(8,128)(2,1)S(1)} %get-tuple-element.26), channel_id=1, replica_groups=mesh['seq'=32,'chan'=8] {'seq'}, dimensions={0} | all-to-all | bytes 1179648 | tf_op jit(solution)/shard_map/all_to_all | solution.py:349
  78.5 1.3 %last.1 = (bf16[256,512]{1,0:T(8,128)(2,1)}, bf16[256,512]{1,0:T(8,128)(2,1)}, bf16[256,512]{1,0:T(8,128)(2,1)}, f32[1,512]{1,0:T(1,128)}, bf16[256,512]{1,0:T(8,128)(2,1)}, /*index=5*/bf16[256,512]{1,0:T(8,128)(2,1)}) custom-call(bf16[32,72,128]{2,1,0:T(8,128)(2,1)S(1)} %all_to_all.23.in_ref, bf16[256,512]{1,0:T(8,128)(2,1)S(1)} %get-tuple-element.27.grad_ref, ...), custom_call_target="tpu_custom_call" | custom-call | tf_op jit(solution)/shard_map/last/pallas_call | solution.py:272
  (3 shorter events, 0.0 us)
Async XLA Ops:
  2.0 19.4 %copy-start = (bf16[256,1280]{1,0:T(8,128)(2,1)S(1)}, bf16[256,1280]{1,0:T(8,128)(2,1)}, u32[]{:S(2)}) copy-start(bf16[256,1280]{1,0:T(8,128)(2,1)} %constant.4.clone.steps_ref) | copy-start | bytes 1966084
  2.0 19.4 %copy-start.3 = (bf16[256,512]{1,0:T(8,128)(2,1)S(1)}, bf16[256,512]{1,0:T(8,128)(2,1)}, u32[]{:S(2)}) copy-start(bf16[256,512]{1,0:T(8,128)(2,1)} %gate_ref.3) | copy-start | bytes 786436
  2.0 19.4 %copy-start.4 = (bf16[256,512]{1,0:T(8,128)(2,1)S(1)}, bf16[256,512]{1,0:T(8,128)(2,1)}, u32[]{:S(2)}) copy-start(bf16[256,512]{1,0:T(8,128)(2,1)} %cot_ref.3) | copy-start | bytes 786436
  2.0 19.4 %copy-start.5 = (f32[2,34,256]{2,1,0:T(8,128)S(1)}, f32[2,34,256]{2,1,0:T(8,128)}, u32[]{:S(2)}) copy-start(f32[2,34,256]{2,1,0:T(8,128)} %constant.5.clone.turn_ref) | copy-start | bytes 208900
  21.4 14.5 %copy-start.6 = (f32[512]{0:T(512)S(1)}, f32[512]{0:T(512)}, u32[]{:S(2)}) copy-start(f32[512]{0:T(512)} %param.13) | copy-start | bytes 6148
  21.4 14.5 %copy-start.7 = (f32[512]{0:T(512)S(1)}, f32[512]{0:T(512)}, u32[]{:S(2)}) copy-start(f32[512]{0:T(512)} %param.14) | copy-start | bytes 6148
  22.9 24.4 %copy-start.1 = (bf16[256,512]{1,0:T(8,128)(2,1)S(1)}, bf16[256,512]{1,0:T(8,128)(2,1)}, u32[]{:S(2)}) copy-start(bf16[256,512]{1,0:T(8,128)(2,1)} %key_ref.3) | copy-start | bytes 786436
  22.9 24.4 %copy-start.2 = (bf16[256,512]{1,0:T(8,128)(2,1)S(1)}, bf16[256,512]{1,0:T(8,128)(2,1)}, u32[]{:S(2)}) copy-start(bf16[256,512]{1,0:T(8,128)(2,1)} %value_ref.3) | copy-start | bytes 786436
  36.2 1.2 %collective-permute-start = (f32[2,256]{1,0:T(2,128)S(1)}, f32[2,256]{1,0:T(2,128)S(1)}, u32[]{:S(2)}, u32[]{:S(2)}) collective-permute-start(f32[2,256]{1,0:T(2,128)S(1)} %sums.1), channel_id=1, source_target_pairs={{0,1},{1,0},{2,3},{3,2},{4,5},{5,4},{6,7},{7,6},{8,9},{9,8},{10,11... | collective-permute-start | bytes 6152 | tf_op jit(solution)/shard_map/ppermute | solution.py:283
  37.4 4.8 %collective-permute-start.1 = (f32[2,256]{1,0:T(2,128)S(1)}, f32[2,256]{1,0:T(2,128)S(1)}, u32[]{:S(2)}, u32[]{:S(2)}) collective-permute-start(f32[2,256]{1,0:T(2,128)S(1)} %add.9), channel_id=1, source_target_pairs={{0,2},{1,3},{2,0},{3,1},{4,6},{5,7},{6,4},{7,5},{8,10},{9,11},{10,... | collective-permute-start | bytes 6152 | tf_op jit(solution)/shard_map/ppermute | solution.py:284
  42.2 6.6 %collective-permute-start.2 = (f32[2,256]{1,0:T(2,128)S(1)}, f32[2,256]{1,0:T(2,128)S(1)}, u32[]{:S(2)}, u32[]{:S(2)}) collective-permute-start(f32[2,256]{1,0:T(2,128)S(1)} %add.10.after_ref), channel_id=1, source_target_pairs={{0,6},{1,7},{2,4},{3,5},{4,2},{5,3},{6,0},{7,1},{8,14},{9,15},{10,... | collective-permute-start | bytes 6152 | tf_op jit(solution)/shard_map/ppermute | solution.py:289

commit v7 on v6

--- a/solution.py
+++ b/solution.py
@@ -125,7 +125,7 @@
 
 
 def parts_of(values):
-    return values[:, :NEAR].astype(f32), values[:, NEAR:].astype(f32)
+    return values[:, :NEAR], values[:, NEAR:]
 
 
 def flat(pieces):
@@ -157,14 +157,18 @@
 
 
 def between_kernel(
-    in_ref, steps_ref, turn_ref, conv_ref, key_ref, value_ref, skip_ref, after_ref, spec_ref, full_ref
+    in_ref, steps_ref, turn_ref, key_ref, value_ref, conv_ref, pack_ref, gate_ref, cot_ref, skip_ref, gain_ref,
+    after_ref, spec_ref, full_ref, push_ref, hold_ref,
 ):
+    _, gate, gated = gate_parts(conv_ref, pack_ref, gate_ref, skip_ref)
+    push_ref[...] = cot_ref[...].astype(f32) * column(gain_ref) * gate
+    hold_ref[...] = gated * gate
     enter, _, inner, turn, pair = open_tables(steps_ref, turn_ref)
     for place in range(2):
         signal = in_ref[:, place * PIECE : (place + 1) * PIECE, :]
         even, odd = finish_spectrum(enter_blocks(signal, enter), inner, turn, pair)
-        spec_ref[2 * place] = even.astype(bf16)
-        spec_ref[2 * place + 1] = odd.astype(bf16)
+        spec_ref[2 * place] = even
+        spec_ref[2 * place + 1] = odd
     mixed = (key_ref[...].astype(f32) * value_ref[...].astype(f32)).astype(bf16)
     full_ref[...] = flat(conv_ref[...]).T.astype(f32) + skip_ref[...] * mixed.astype(f32)
 
@@ -195,14 +199,9 @@
     return inv_rms, inv_rms * inv_rms * inv_rms * sums[1:2] / D
 
 
-def grad_kernel(
-    sums_ref, conv_ref, pack_ref, gate_ref, cot_ref, skip_ref, gain_ref, after_ref, out_ref
-):
+def grad_kernel(sums_ref, push_ref, hold_ref, out_ref):
     inv_rms, pull = norm_parts(sums_ref)
-    _, gate, gated = gate_parts(conv_ref, pack_ref, gate_ref, skip_ref)
-    scaled = cot_ref[...].astype(f32) * column(gain_ref)
-    grad_gated = inv_rms * scaled - gated * pull
-    out_ref[...] = cut((grad_gated * gate).astype(bf16))
+    out_ref[...] = cut((inv_rms * push_ref[...] - pull * hold_ref[...]).astype(bf16))
 
 
 def wide_column(row):
@@ -295,7 +294,7 @@
     natural = ((BLOCK, WIDTH), bf16)
     turned = ((WIDTH, BLOCK), bf16)
     pieces = ((PARTS, PIECE, BLOCK), bf16)
-    spectra = ((4, ROWS, BLOCK), bf16)
+    spectra = ((4, ROWS, BLOCK), f32)
 
     mixed = (key_feat.astype(f32) * value_feat.astype(f32)).astype(bf16)
     taps = jnp.where(key_feat == key_feat, filter_taps, mixed)
@@ -315,21 +314,20 @@
     sides = (conv, packed, gate_t, cot_t, skip_row, gain_row)
     (sums,) = call(sums_kernel, "sums", [((2, BLOCK), f32)], *sides)
     sums = add_over_pairs(sums)
-    spec, full = call(
+    spec, full, push, hold = call(
         between_kernel,
         "between",
-        [spectra, ((BLOCK, WIDTH), f32)],
+        [spectra, ((BLOCK, WIDTH), f32), ((WIDTH, BLOCK), f32), ((WIDTH, BLOCK), f32)],
         arrived,
         steps,
         turn,
-        conv,
         key_feat,
         value_feat,
-        skip_row,
+        *sides,
         sums,
     )
     sums = add_over_mirror(sums)
-    (grad,) = call(grad_kernel, "grad", [pieces], sums, *sides, full)
+    (grad,) = call(grad_kernel, "grad", [pieces], sums, push, hold)
     grad_arrived = lax.all_to_all(grad, "seq", 0, 0, tiled=True)
     result, grad_conv, normed, gate = call(
         backward_kernel,

time: 80.8 us -> 80.5 us (level)
  transfers between devices with their start and end apart: 3 -> 3, of which waited for: 3 -> 3; matrix products, arithmetic and copies ran while one was open for 0% -> 0% of each run, Pallas kernels for 1% -> 2%
where the time goes in v7:
time: 80.5 us; the launch traced here: 79.5 us
  blocking collectives  59.4 us (74%)
  starting transfers between devices  8.41 us (10%)
  Pallas kernels  6.36 us (8%)
  waiting for transfers between devices  3 us (4%)
  other arithmetic  1.43 us (2%)
    all_to_all x1, blocking collectives, on_device(): arrived = lax.all_to_all(packed, 'seq', 0, 0, tiled=True)  19.2 us
    all_to_all x1, blocking collectives, on_device(): result = lax.all_to_all(result, 'seq', 0, 0, tiled=True)  14.7 us
    all_to_all x1, blocking collectives, on_device(): grad_arrived = lax.all_to_all(grad, 'seq', 0, 0, tiled=True)  12.9 us
    all_to_all x1, blocking collectives, on_device(): conv = lax.all_to_all(conv, 'seq', 0, 0, tiled=True)  12.8 us
    pallas_call x7, Pallas kernels, call(): pl.pallas_call(kernel, name=name, out_shape=[jax.ShapeDtypeStruct(shape,...  6.36 us
    ppermute x1, starting transfers between devices, add_over_mirror(): return sums + lax.ppermute(sums, 'chan', mirror)  5.05 us
    ppermute x1, starting transfers between devices, add_over_pairs(): lax.ppermute(sums, 'chan', [(at, at ^ 2) for at in range(GROUP)])  3.27 us
  transfers between devices with their start and end apart: 3, of which 3 were waited for; matrix products, arithmetic and copies ran while one was open for 0% of the time, Pallas kernels for 2%

profile of v7, /device:TPU:0, one launch (start us, length us, event | category | flops | bytes accessed | tf_op | source)
XLA Modules:
  0.0 79.5 jit_solution(16478758146787211748)
XLA Ops:
  0.6 0.0 copy-start
  0.6 0.0 copy-start.5
  0.7 0.0 copy-start.4
  0.7 0.0 copy-start.3
  0.7 1.4 %compare_select_fusion = (bf16[256,512]{1,0:T(8,128)(2,1)S(1)}, bf16[256,512]{1,0:T(8,128)(2,1)S(1)}) fusion(bf16[256,512]{1,0:T(8,128)(2,1)} %param.12, bf16[256,512]{1,0:T(8,128)(2,1)} %key_ref.3, bf16[256,512]{1,0:T(8,128)(2,1)} %value_ref.3), kind=kLoop, calls=%fused_computation.1 | loop fusion | flops 786432 | bytes 1310720 | tf_op jit(solution)/shard_map/jit(_where)/select_n | solution.py:300
  2.1 0.0 copy-start.6
  2.1 0.0 copy-start.7
  2.1 0.2 pack.1.pack_ref
  2.3 0.0 copy-start.1
  2.3 0.0 copy-start.2
  2.3 19.2 %all_to_all.20.in_ref.pack_ref = bf16[32,32,256]{2,1,0:T(8,128)(2,1)S(1)} all-to-all(bf16[32,32,256]{2,1,0:T(8,128)(2,1)S(1)} %pack.1.pack_ref), channel_id=1, replica_groups=mesh['seq'=32,'chan'=8] {'seq'}, dimensions={0} | all-to-all | bytes 1048576 | tf_op jit(solution)/shard_map/all_to_all | solution.py:302
  21.5 0.0 copy-done
  21.5 0.0 copy-done.5
  21.5 0.0 copy-done.4
  21.5 0.0 copy-done.3
  21.5 1.5 %forward.1 = (bf16[32,16,256]{2,1,0:T(8,128)(2,1)S(1)}, bf16[512,256]{1,0:T(8,128)(2,1)S(1)}, bf16[512,256]{1,0:T(8,128)(2,1)S(1)}) custom-call(bf16[32,32,256]{2,1,0:T(8,128)(2,1)S(1)} %all_to_all.20.in_ref.pack_ref, bf16[256,1280]{1,0:T(8,128)(2,1)S(1)} %copy-done, f32[2,34,256]{2,1,0:T(8,128)S(1)} %copy-done.5, bf16[256,512]{1,0:T(8,128)(2,1)S(1)} %copy-done.3, ...), custom_call_target="tpu_custom_call" | custom-call | tf_op jit(solution)/shard_map/forward/pallas_call | solution.py:271
  23.0 12.8 %all_to_all.21.conv_ref = bf16[32,16,256]{2,1,0:T(8,128)(2,1)S(1)} all-to-all(bf16[32,16,256]{2,1,0:T(8,128)(2,1)S(1)} %get-tuple-element.23), channel_id=1, replica_groups=mesh['seq'=32,'chan'=8] {'seq'}, dimensions={0} | all-to-all | bytes 524288 | tf_op jit(solution)/shard_map/all_to_all | solution.py:313
  35.8 0.0 copy-done.6
  35.8 0.0 copy-done.7
  35.8 0.3 sums.1
  36.1 0.1 collective-permute-start
  36.2 1.1 %collective-permute-done = f32[2,256]{1,0:T(2,128)S(1)} collective-permute-done((f32[2,256]{1,0:T(2,128)S(1)}, f32[2,256]{1,0:T(2,128)S(1)}, u32[]{:S(2)}, u32[]{:S(2)}) %collective-permute-start) | collective-permute-done | bytes 2080 | tf_op jit(solution)/shard_map/ppermute | solution.py:282
  37.3 3.3 %collective-permute-start.1 = (f32[2,256]{1,0:T(2,128)S(1)}, f32[2,256]{1,0:T(2,128)S(1)}, u32[]{:S(2)}, u32[]{:S(2)}) collective-permute-start(f32[2,256]{1,0:T(2,128)S(1)} %add.9), channel_id=1, source_target_pairs={{0,2},{1,3},{2,0},{3,1},{4,6},{5,7},{6,4},{7,5},{8,10},{9,11},{10,... | collective-permute-start | bytes 6152 | tf_op jit(solution)/shard_map/ppermute | solution.py:283
  40.6 1.6 %collective-permute-done.1 = f32[2,256]{1,0:T(2,128)S(1)} collective-permute-done((f32[2,256]{1,0:T(2,128)S(1)}, f32[2,256]{1,0:T(2,128)S(1)}, u32[]{:S(2)}, u32[]{:S(2)}) %collective-permute-start.1) | collective-permute-done | bytes 2080 | tf_op jit(solution)/shard_map/ppermute | solution.py:283
  42.2 5.1 %collective-permute-start.2 = (f32[2,256]{1,0:T(2,128)S(1)}, f32[2,256]{1,0:T(2,128)S(1)}, u32[]{:S(2)}, u32[]{:S(2)}) collective-permute-start(f32[2,256]{1,0:T(2,128)S(1)} %add.10.after_ref), channel_id=1, source_target_pairs={{0,6},{1,7},{2,4},{3,5},{4,2},{5,3},{6,0},{7,1},{8,14},{9,15},{10,... | collective-permute-start | bytes 6152 | tf_op jit(solution)/shard_map/ppermute | solution.py:288
  47.2 0.0 copy-done.1
  47.2 0.0 copy-done.2
  47.2 1.3 %between.1 = (f32[4,528,256]{2,1,0:T(8,128)S(1)}, f32[256,512]{1,0:T(8,128)S(1)}, f32[512,256]{1,0:T(8,128)S(1)}, f32[512,256]{1,0:T(8,128)S(1)}) custom-call(bf16[32,32,256]{2,1,0:T(8,128)(2,1)S(1)} %all_to_all.20.in_ref.pack_ref, bf16[256,1280]{1,0:T(8,128)(2,1)S(1)} %copy-done, f32[2,34,256]{2,1,0:T(8,128)S(1)} %copy-done.5, ...), custom_call_target="tpu_custom_call" | custom-call | tf_op jit(solution)/shard_map/between/pallas_call | solution.py:271
  48.5 0.3 collective-permute-done.2
  48.8 0.1 grad.1
  48.9 12.9 %all_to_all.22.in_ref = bf16[32,16,256]{2,1,0:T(8,128)(2,1)S(1)} all-to-all(bf16[32,16,256]{2,1,0:T(8,128)(2,1)S(1)} %grad.1), channel_id=1, replica_groups=mesh['seq'=32,'chan'=8] {'seq'}, dimensions={0} | all-to-all | bytes 524288 | tf_op jit(solution)/shard_map/all_to_all | solution.py:331
  61.8 1.7 %backward.1 = (bf16[32,72,128]{2,1,0:T(8,128)(2,1)S(1)}, bf16[256,512]{1,0:T(8,128)(2,1)S(1)}, bf16[256,512]{1,0:T(8,128)(2,1)S(1)}, bf16[256,512]{1,0:T(8,128)(2,1)S(1)}) custom-call(bf16[32,16,256]{2,1,0:T(8,128)(2,1)S(1)} %all_to_all.22.in_ref, bf16[32,32,256]{2,1,0:T(8,128)(2,1)S(1)} %all_to_all.20.in_ref.pack_ref, ...), custom_call_target="tpu_custom_call" | custom-call | tf_op jit(solution)/shard_map/backward/pallas_call | solution.py:271
  63.5 14.7 %all_to_all.23.in_ref = bf16[32,72,128]{2,1,0:T(8,128)(2,1)S(1)} all-to-all(bf16[32,72,128]{2,1,0:T(8,128)(2,1)S(1)} %get-tuple-element.30), channel_id=1, replica_groups=mesh['seq'=32,'chan'=8] {'seq'}, dimensions={0} | all-to-all | bytes 1179648 | tf_op jit(solution)/shard_map/all_to_all | solution.py:347
  78.2 1.3 %last.1 = (bf16[256,512]{1,0:T(8,128)(2,1)}, bf16[256,512]{1,0:T(8,128)(2,1)}, bf16[256,512]{1,0:T(8,128)(2,1)}, f32[1,512]{1,0:T(1,128)}, bf16[256,512]{1,0:T(8,128)(2,1)}, /*index=5*/bf16[256,512]{1,0:T(8,128)(2,1)}) custom-call(bf16[32,72,128]{2,1,0:T(8,128)(2,1)S(1)} %all_to_all.23.in_ref, bf16[256,512]{1,0:T(8,128)(2,1)S(1)} %get-tuple-element.31.grad_ref, ...), custom_call_target="tpu_custom_call" | custom-call | tf_op jit(solution)/shard_map/last/pallas_call | solution.py:271
  (3 shorter events, 0.0 us)
Async XLA Ops:
  0.6 20.9 %copy-start = (bf16[256,1280]{1,0:T(8,128)(2,1)S(1)}, bf16[256,1280]{1,0:T(8,128)(2,1)}, u32[]{:S(2)}) copy-start(bf16[256,1280]{1,0:T(8,128)(2,1)} %constant.4.clone.steps_ref) | copy-start | bytes 1966084
  0.6 20.9 %copy-start.5 = (f32[2,34,256]{2,1,0:T(8,128)S(1)}, f32[2,34,256]{2,1,0:T(8,128)}, u32[]{:S(2)}) copy-start(f32[2,34,256]{2,1,0:T(8,128)} %constant.5.clone.turn_ref) | copy-start | bytes 208900
  0.7 20.8 %copy-start.4 = (bf16[256,512]{1,0:T(8,128)(2,1)S(1)}, bf16[256,512]{1,0:T(8,128)(2,1)}, u32[]{:S(2)}) copy-start(bf16[256,512]{1,0:T(8,128)(2,1)} %cot_ref.3) | copy-start | bytes 786436
  0.7 20.8 %copy-start.3 = (bf16[256,512]{1,0:T(8,128)(2,1)S(1)}, bf16[256,512]{1,0:T(8,128)(2,1)}, u32[]{:S(2)}) copy-start(bf16[256,512]{1,0:T(8,128)(2,1)} %gate_ref.3) | copy-start | bytes 786436
  2.1 33.7 %copy-start.6 = (f32[512]{0:T(512)S(1)}, f32[512]{0:T(512)}, u32[]{:S(2)}) copy-start(f32[512]{0:T(512)} %param.14) | copy-start | bytes 6148
  2.1 33.7 %copy-start.7 = (f32[512]{0:T(512)S(1)}, f32[512]{0:T(512)}, u32[]{:S(2)}) copy-start(f32[512]{0:T(512)} %param.13) | copy-start | bytes 6148
  2.3 44.9 %copy-start.1 = (bf16[256,512]{1,0:T(8,128)(2,1)S(1)}, bf16[256,512]{1,0:T(8,128)(2,1)}, u32[]{:S(2)}) copy-start(bf16[256,512]{1,0:T(8,128)(2,1)} %key_ref.3) | copy-start | bytes 786436
  2.3 44.9 %copy-start.2 = (bf16[256,512]{1,0:T(8,128)(2,1)S(1)}, bf16[256,512]{1,0:T(8,128)(2,1)}, u32[]{:S(2)}) copy-start(bf16[256,512]{1,0:T(8,128)(2,1)} %value_ref.3) | copy-start | bytes 786436
  36.1 1.2 %collective-permute-start = (f32[2,256]{1,0:T(2,128)S(1)}, f32[2,256]{1,0:T(2,128)S(1)}, u32[]{:S(2)}, u32[]{:S(2)}) collective-permute-start(f32[2,256]{1,0:T(2,128)S(1)} %sums.1), channel_id=1, source_target_pairs={{0,1},{1,0},{2,3},{3,2},{4,5},{5,4},{6,7},{7,6},{8,9},{9,8},{10,11... | collective-permute-start | bytes 6152 | tf_op jit(solution)/shard_map/ppermute | solution.py:282
  37.3 4.8 %collective-permute-start.1 = (f32[2,256]{1,0:T(2,128)S(1)}, f32[2,256]{1,0:T(2,128)S(1)}, u32[]{:S(2)}, u32[]{:S(2)}) collective-permute-start(f32[2,256]{1,0:T(2,128)S(1)} %add.9), channel_id=1, source_target_pairs={{0,2},{1,3},{2,0},{3,1},{4,6},{5,7},{6,4},{7,5},{8,10},{9,11},{10,... | collective-permute-start | bytes 6152 | tf_op jit(solution)/shard_map/ppermute | solution.py:283
  42.2 6.6 %collective-permute-start.2 = (f32[2,256]{1,0:T(2,128)S(1)}, f32[2,256]{1,0:T(2,128)S(1)}, u32[]{:S(2)}, u32[]{:S(2)}) collective-permute-start(f32[2,256]{1,0:T(2,128)S(1)} %add.10.after_ref), channel_id=1, source_target_pairs={{0,6},{1,7},{2,4},{3,5},{4,2},{5,3},{6,0},{7,1},{8,14},{9,15},{10,... | collective-permute-start | bytes 6152 | tf_op jit(solution)/shard_map/ppermute | solution.py:288

commit v8 on v7

--- a/solution.py
+++ b/solution.py
@@ -36,27 +36,27 @@
     enter = np.kron(np.concatenate([cosine, -sine[: PARTS - 1]], 0), eye)
     weight = np.where((low == 0) | (low == PARTS), 1.0, 2.0)[:, None] / 4
     leave = np.kron(np.concatenate([cosine * weight, (sine * weight)[: PARTS - 1]], 0).T, eye)
-    inner = 2 * np.pi * (near[:, None] * near[None, :] % NEAR) / NEAR
-    cosine, sine = np.cos(inner) / 16, -np.sin(inner) / 16
-    inner = np.block([[cosine, sine], [-sine, cosine]])
+    into, back = [], []
+    for odd in range(2):
+        inner = 2 * np.pi * (near[:, None] * (2 * near[None, :] + odd) % BLOCK) / BLOCK
+        cosine, sine = np.cos(inner) / 16, -np.sin(inner) / 16
+        into.append(np.block([[cosine, sine], [-sine, cosine]]))
+        back.append(np.block([[cosine.T, sine.T], [sine.T, -cosine.T]]))
     half = SPAN * HALF // 2
-    steps = np.concatenate([inner, leave, enter[:half], enter[half:]], 1)
+    steps = np.concatenate([*into, *back, leave, enter[:half], enter[half:]], 1)
     turn = 2 * np.pi * (low[:, None] * inside[None, :] % FULL) / FULL
-    pair = 2 * np.pi * inside[None, :] / BLOCK
-    turn = np.concatenate([turn, pair], 0)
     turn = np.stack([np.cos(turn), -np.sin(turn)])
     return steps.astype(np.float32).astype(bf16), turn.astype(np.float32)
 
 
 def open_tables(steps_ref, turn_ref):
-    cuts = (BLOCK, BLOCK + SPAN * HALF, 2 * BLOCK + SPAN * HALF)
-    enter = jnp.concatenate([steps_ref[:, cuts[1] : cuts[2]], steps_ref[:, cuts[2] :]], 0)
+    blocks = [steps_ref[:, at * BLOCK : (at + 1) * BLOCK] for at in range(8)]
     turn = [
-        jnp.broadcast_to(turn_ref[part, :BINS][:, None, :], (BINS, HALF, BLOCK)).reshape(BINS * HALF, BLOCK)
+        jnp.broadcast_to(turn_ref[part][:, None, :], (BINS, HALF, BLOCK)).reshape(BINS * HALF, BLOCK)
         for part in range(2)
     ]
-    pair = [turn_ref[part, BINS:, :NEAR] for part in range(2)]
-    return enter, steps_ref[:, cuts[0] : cuts[1]], steps_ref[:, : cuts[0]], turn, pair
+    enter, leave = jnp.concatenate(blocks[6:], 0), jnp.concatenate(blocks[4:6], 1)
+    return enter, leave, blocks[:2], blocks[2:4], turn
 
 
 def dot(first, second):
@@ -64,13 +64,10 @@
 
 
 def rotate(real, imag, turn):
-    return real * turn[0] - imag * turn[1], real * turn[1] + imag * turn[0]
-
-
-def rotate_first(real, imag, turn):
     cosine, sine = turn
     own = imag.shape[0]
-    turned_re, turned_im = rotate(real[:own], imag, (cosine[:own], sine[:own]))
+    turned_re = real[:own] * cosine[:own] - imag * sine[:own]
+    turned_im = real[:own] * sine[:own] + imag * cosine[:own]
     turned_re = jnp.concatenate([turned_re, real[own:] * cosine[own:]], 0)
     turned_im = jnp.concatenate([turned_im, real[own:] * sine[own:]], 0)
     return turned_re, turned_im
@@ -87,35 +84,33 @@
     return [dot(enter, half.astype(bf16)) for half in halves]
 
 
-def finish_spectrum(halves, inner, turn, pair):
+def finish_spectrum(halves, into, turn):
     pieces = ([], [], [], [])
     for mixed in halves:
-        real, imag = rotate_first(mixed[: BINS * HALF], mixed[BINS * HALF :], turn)
+        real, imag = rotate(mixed[: BINS * HALF], mixed[BINS * HALF :], turn)
         pieces[0].append(real[:, :NEAR] + real[:, NEAR:])
         pieces[1].append(imag[:, :NEAR] + imag[:, NEAR:])
-        real, imag = rotate(real[:, :NEAR] - real[:, NEAR:], imag[:, :NEAR] - imag[:, NEAR:], pair)
-        pieces[2].append(real)
-        pieces[3].append(imag)
+        pieces[2].append(real[:, :NEAR] - real[:, NEAR:])
+        pieces[3].append(imag[:, :NEAR] - imag[:, NEAR:])
     pieces = [join(piece) for piece in pieces]
-    return [dot(jnp.concatenate(pieces[at : at + 2], 1), inner) for at in (0, 2)]
-
-
-def invert_inner(products, inner):
+    return [dot(jnp.concatenate(pieces[2 * odd : 2 * odd + 2], 1), into[odd]) for odd in range(2)]
+
+
+def invert_inner(products, back):
     return [
-        dot(jnp.concatenate([real.astype(bf16), imag.astype(bf16)], 1), inner).reshape(BINS, PIECE, BLOCK)
-        for real, imag in products
+        dot(jnp.concatenate([real.astype(bf16), imag.astype(bf16)], 1), matrix).reshape(BINS, PIECE, BLOCK)
+        for (real, imag), matrix in zip(products, back, strict=True)
     ]
 
 
-def finish_inverse(parts, leave, turn, pair):
+def finish_inverse(parts, leave, turn):
     outs = []
     for half in range(2):
         rows = slice(half * HALF, (half + 1) * HALF)
-        first, second = [part[:, rows].reshape(BINS * HALF, BLOCK) for part in parts]
-        first_re, first_im = first[:, :NEAR], first[:, NEAR:]
-        second_re, second_im = rotate(second[:, :NEAR], second[:, NEAR:], pair)
-        real = jnp.concatenate([first_re + second_re, first_re - second_re], 1)
-        imag = jnp.concatenate([first_im + second_im, first_im - second_im], 1)
+        even, odd = [part[:, rows].reshape(BINS * HALF, BLOCK) for part in parts]
+        total, rest = even + odd, even - odd
+        real = jnp.concatenate([total[:, :NEAR], rest[:, :NEAR]], 1)
+        imag = jnp.concatenate([total[:, NEAR:], rest[:, NEAR:]], 1)
         own = (BINS - 2) * HALF
         turned_re = real * turn[0] - imag * turn[1]
         turned_im = real[:own] * turn[1][:own] + imag[:own] * turn[0][:own]
@@ -144,16 +139,16 @@
 def forward_kernel(in_ref, steps_ref, turn_ref, gate_ref, cot_ref, out_ref, gate_out, cot_out):
     gate_out[...] = gate_ref[...].T
     cot_out[...] = cot_ref[...].T
-    enter, leave, inner, turn, pair = open_tables(steps_ref, turn_ref)
+    enter, leave, into, back, turn = open_tables(steps_ref, turn_ref)
     first = enter_blocks(in_ref[:, :PIECE, :], enter)
     second = enter_blocks(in_ref[:, PIECE:, :], enter)
-    first, second = [finish_spectrum(halves, inner, turn, pair) for halves in (first, second)]
+    first, second = [finish_spectrum(halves, into, turn) for halves in (first, second)]
     products = []
     for one, other in zip(first, second, strict=True):
         one_re, one_im = parts_of(one)
         other_re, other_im = parts_of(other)
-        products.append((one_re * other_re - one_im * other_im, -(one_re * other_im + one_im * other_re)))
-    out_ref[...] = finish_inverse(invert_inner(products, inner), leave, turn, pair).astype(bf16)
+        products.append((one_re * other_re - one_im * other_im, one_re * other_im + one_im * other_re))
+    out_ref[...] = finish_inverse(invert_inner(products, back), leave, turn).astype(bf16)
 
 
 def between_kernel(
@@ -163,10 +158,10 @@
     _, gate, gated = gate_parts(conv_ref, pack_ref, gate_ref, skip_ref)
     push_ref[...] = cot_ref[...].astype(f32) * column(gain_ref) * gate
     hold_ref[...] = gated * gate
-    enter, _, inner, turn, pair = open_tables(steps_ref, turn_ref)
+    enter, _, into, _, turn = open_tables(steps_ref, turn_ref)
     for place in range(2):
         signal = in_ref[:, place * PIECE : (place + 1) * PIECE, :]
-        even, odd = finish_spectrum(enter_blocks(signal, enter), inner, turn, pair)
+        even, odd = finish_spectrum(enter_blocks(signal, enter), into, turn)
         spec_ref[2 * place] = even
         spec_ref[2 * place + 1] = odd
     mixed = (key_ref[...].astype(f32) * value_ref[...].astype(f32)).astype(bf16)
@@ -220,7 +215,7 @@
     grad_gated = inv_rms * (cot_ref[...].astype(f32) * gain) - gated * pull
     gate_out[...] = (grad_gated * full).astype(bf16)
     grad_out[...] = (grad_gated * gate).astype(bf16)
-    enter, leave, inner, turn, pair = open_tables(steps_ref, turn_ref)
+    enter, leave, into, back, turn = open_tables(steps_ref, turn_ref)
     grad = in_ref[...]
     bias = jnp.sum(grad.astype(f32) * pack_ref[:, :PIECE, :].astype(f32), axis=0)
     bias = jnp.sum(bias, axis=1, keepdims=True)
@@ -230,17 +225,17 @@
     for at, part in enumerate((high[:HALF], (bias - high)[:HALF], high[HALF:], (bias - high)[HALF:])):
         tail = jnp.where(lane == at, part, tail)
     out_ref[:, 4 * PIECE :, :] = jnp.broadcast_to(tail.astype(bf16)[None], (PARTS, TAIL, 128))
-    spectra = finish_spectrum(enter_blocks(grad, enter), inner, turn, pair)
+    spectra = finish_spectrum(enter_blocks(grad, enter), into, turn)
     inverses = []
     for other in (1, 0):
         products = []
         for parity, mine in enumerate(spectra):
             real, imag = parts_of(spec_ref[2 * other + parity])
             mine_re, mine_im = parts_of(mine)
-            products.append((real * mine_re + imag * mine_im, imag * mine_re - real * mine_im))
-        inverses.append(invert_inner(products, inner))
+            products.append((real * mine_re + imag * mine_im, real * mine_im - imag * mine_re))
+        inverses.append(invert_inner(products, back))
     for place, parts in enumerate(inverses):
-        result = finish_inverse(parts, leave, turn, pair).astype(bf16)
+        result = finish_inverse(parts, leave, turn).astype(bf16)
         out_ref[:, 2 * place * PIECE : (2 * place + 1) * PIECE, :] = result[:, :, :128]
         out_ref[:, (2 * place + 1) * PIECE : (2 * place + 2) * PIECE, :] = result[:, :, 128:]
 

time: 80.5 us -> 80 us (level)
  transfers between devices with their start and end apart: 3 -> 3, of which waited for: 3 -> 3; matrix products, arithmetic and copies ran while one was open for 0% -> 0% of each run, Pallas kernels for 2% -> 1%
where the time goes in v8:
time: 80 us; the launch traced here: 79 us
  blocking collectives  59.3 us (74%)
  starting transfers between devices  8.41 us (11%)
  Pallas kernels  5.98 us (7%)
  waiting for transfers between devices  3.07 us (4%)
  other arithmetic  1.46 us (2%)
    all_to_all x1, blocking collectives, on_device(): arrived = lax.all_to_all(packed, 'seq', 0, 0, tiled=True)  19 us
    all_to_all x1, blocking collectives, on_device(): result = lax.all_to_all(result, 'seq', 0, 0, tiled=True)  14.7 us
    all_to_all x1, blocking collectives, on_device(): grad_arrived = lax.all_to_all(grad, 'seq', 0, 0, tiled=True)  12.9 us
    all_to_all x1, blocking collectives, on_device(): conv = lax.all_to_all(conv, 'seq', 0, 0, tiled=True)  12.8 us
    pallas_call x7, Pallas kernels, call(): pl.pallas_call(kernel, name=name, out_shape=[jax.ShapeDtypeStruct(shape,...  5.98 us
    ppermute x1, starting transfers between devices, add_over_mirror(): return sums + lax.ppermute(sums, 'chan', mirror)  5.05 us
    ppermute x1, starting transfers between devices, add_over_pairs(): lax.ppermute(sums, 'chan', [(at, at ^ 2) for at in range(GROUP)])  3.27 us
  transfers between devices with their start and end apart: 3, of which 3 were waited for; matrix products, arithmetic and copies ran while one was open for 0% of the time, Pallas kernels for 1%

profile of v8, /device:TPU:0, one launch (start us, length us, event | category | flops | bytes accessed | tf_op | source)
XLA Modules:
  0.0 79.0 jit_solution(15959204877799998313)
XLA Ops:
  0.6 0.0 copy-start
  0.6 0.0 copy-start.5
  0.7 0.0 copy-start.4
  0.7 0.0 copy-start.3
  0.7 1.4 %compare_select_fusion = (bf16[256,512]{1,0:T(8,128)(2,1)S(1)}, bf16[256,512]{1,0:T(8,128)(2,1)S(1)}) fusion(bf16[256,512]{1,0:T(8,128)(2,1)} %param.12, bf16[256,512]{1,0:T(8,128)(2,1)} %key_ref.3, bf16[256,512]{1,0:T(8,128)(2,1)} %value_ref.3), kind=kLoop, calls=%fused_computation.1 | loop fusion | flops 786432 | bytes 1310720 | tf_op jit(solution)/shard_map/jit(_where)/select_n | solution.py:295
  2.1 0.0 copy-start.6
  2.1 0.0 copy-start.7
  2.2 0.2 pack.1.pack_ref
  2.3 19.0 %all_to_all.20.in_ref.pack_ref = bf16[32,32,256]{2,1,0:T(8,128)(2,1)S(1)} all-to-all(bf16[32,32,256]{2,1,0:T(8,128)(2,1)S(1)} %pack.1.pack_ref), channel_id=1, replica_groups=mesh['seq'=32,'chan'=8] {'seq'}, dimensions={0} | all-to-all | bytes 1048576 | tf_op jit(solution)/shard_map/all_to_all | solution.py:297
  21.4 0.0 copy-done
  21.4 0.0 copy-done.5
  21.4 0.0 copy-done.4
  21.4 0.0 copy-done.3
  21.4 0.0 copy-start.1
  21.4 0.0 copy-start.2
  21.4 1.4 %forward.1 = (bf16[32,16,256]{2,1,0:T(8,128)(2,1)S(1)}, bf16[512,256]{1,0:T(8,128)(2,1)S(1)}, bf16[512,256]{1,0:T(8,128)(2,1)S(1)}) custom-call(bf16[32,32,256]{2,1,0:T(8,128)(2,1)S(1)} %all_to_all.20.in_ref.pack_ref, bf16[256,2048]{1,0:T(8,128)(2,1)S(1)} %copy-done, f32[2,33,256]{2,1,0:T(8,128)S(1)} %copy-done.5, bf16[256,512]{1,0:T(8,128)(2,1)S(1)} %copy-done.3, ...), custom_call_target="tpu_custom_call" | custom-call | tf_op jit(solution)/shard_map/forward/pallas_call | solution.py:266
  22.8 12.8 %all_to_all.21.conv_ref = bf16[32,16,256]{2,1,0:T(8,128)(2,1)S(1)} all-to-all(bf16[32,16,256]{2,1,0:T(8,128)(2,1)S(1)} %get-tuple-element.23), channel_id=1, replica_groups=mesh['seq'=32,'chan'=8] {'seq'}, dimensions={0} | all-to-all | bytes 524288 | tf_op jit(solution)/shard_map/all_to_all | solution.py:308
  35.5 0.0 copy-done.6
  35.5 0.0 copy-done.7
  35.6 0.3 sums.1
  35.8 0.1 collective-permute-start
  36.0 1.1 %collective-permute-done = f32[2,256]{1,0:T(2,128)S(1)} collective-permute-done((f32[2,256]{1,0:T(2,128)S(1)}, f32[2,256]{1,0:T(2,128)S(1)}, u32[]{:S(2)}, u32[]{:S(2)}) %collective-permute-start) | collective-permute-done | bytes 2080 | tf_op jit(solution)/shard_map/ppermute | solution.py:277
  37.1 3.3 %collective-permute-start.1 = (f32[2,256]{1,0:T(2,128)S(1)}, f32[2,256]{1,0:T(2,128)S(1)}, u32[]{:S(2)}, u32[]{:S(2)}) collective-permute-start(f32[2,256]{1,0:T(2,128)S(1)} %add.9), channel_id=1, source_target_pairs={{0,2},{1,3},{2,0},{3,1},{4,6},{5,7},{6,4},{7,5},{8,10},{9,11},{10,... | collective-permute-start | bytes 6152 | tf_op jit(solution)/shard_map/ppermute | solution.py:278
  40.4 1.6 %collective-permute-done.1 = f32[2,256]{1,0:T(2,128)S(1)} collective-permute-done((f32[2,256]{1,0:T(2,128)S(1)}, f32[2,256]{1,0:T(2,128)S(1)}, u32[]{:S(2)}, u32[]{:S(2)}) %collective-permute-start.1) | collective-permute-done | bytes 2080 | tf_op jit(solution)/shard_map/ppermute | solution.py:278
  41.9 5.1 %collective-permute-start.2 = (f32[2,256]{1,0:T(2,128)S(1)}, f32[2,256]{1,0:T(2,128)S(1)}, u32[]{:S(2)}, u32[]{:S(2)}) collective-permute-start(f32[2,256]{1,0:T(2,128)S(1)} %add.10.after_ref), channel_id=1, source_target_pairs={{0,6},{1,7},{2,4},{3,5},{4,2},{5,3},{6,0},{7,1},{8,14},{9,15},{10,... | collective-permute-start | bytes 6152 | tf_op jit(solution)/shard_map/ppermute | solution.py:283
  47.0 0.0 copy-done.1
  47.0 0.0 copy-done.2
  47.0 1.2 %between.1 = (f32[4,528,256]{2,1,0:T(8,128)S(1)}, f32[256,512]{1,0:T(8,128)S(1)}, f32[512,256]{1,0:T(8,128)S(1)}, f32[512,256]{1,0:T(8,128)S(1)}) custom-call(bf16[32,32,256]{2,1,0:T(8,128)(2,1)S(1)} %all_to_all.20.in_ref.pack_ref, bf16[256,2048]{1,0:T(8,128)(2,1)S(1)} %copy-done, f32[2,33,256]{2,1,0:T(8,128)S(1)} %copy-done.5, ...), custom_call_target="tpu_custom_call" | custom-call | tf_op jit(solution)/shard_map/between/pallas_call | solution.py:266
  48.2 0.4 collective-permute-done.2
  48.6 0.1 grad.1
  48.6 12.9 %all_to_all.22.in_ref = bf16[32,16,256]{2,1,0:T(8,128)(2,1)S(1)} all-to-all(bf16[32,16,256]{2,1,0:T(8,128)(2,1)S(1)} %grad.1), channel_id=1, replica_groups=mesh['seq'=32,'chan'=8] {'seq'}, dimensions={0} | all-to-all | bytes 524288 | tf_op jit(solution)/shard_map/all_to_all | solution.py:326
  61.5 1.6 %backward.1 = (bf16[32,72,128]{2,1,0:T(8,128)(2,1)S(1)}, bf16[256,512]{1,0:T(8,128)(2,1)S(1)}, bf16[256,512]{1,0:T(8,128)(2,1)S(1)}, bf16[256,512]{1,0:T(8,128)(2,1)S(1)}) custom-call(bf16[32,16,256]{2,1,0:T(8,128)(2,1)S(1)} %all_to_all.22.in_ref, bf16[32,32,256]{2,1,0:T(8,128)(2,1)S(1)} %all_to_all.20.in_ref.pack_ref, ...), custom_call_target="tpu_custom_call" | custom-call | tf_op jit(solution)/shard_map/backward/pallas_call | solution.py:266
  63.1 14.7 %all_to_all.23.in_ref = bf16[32,72,128]{2,1,0:T(8,128)(2,1)S(1)} all-to-all(bf16[32,72,128]{2,1,0:T(8,128)(2,1)S(1)} %get-tuple-element.30), channel_id=1, replica_groups=mesh['seq'=32,'chan'=8] {'seq'}, dimensions={0} | all-to-all | bytes 1179648 | tf_op jit(solution)/shard_map/all_to_all | solution.py:342
  77.7 1.3 %last.1 = (bf16[256,512]{1,0:T(8,128)(2,1)}, bf16[256,512]{1,0:T(8,128)(2,1)}, bf16[256,512]{1,0:T(8,128)(2,1)}, f32[1,512]{1,0:T(1,128)}, bf16[256,512]{1,0:T(8,128)(2,1)}, /*index=5*/bf16[256,512]{1,0:T(8,128)(2,1)}) custom-call(bf16[32,72,128]{2,1,0:T(8,128)(2,1)S(1)} %all_to_all.23.in_ref, bf16[256,512]{1,0:T(8,128)(2,1)S(1)} %get-tuple-element.31.grad_ref, ...), custom_call_target="tpu_custom_call" | custom-call | tf_op jit(solution)/shard_map/last/pallas_call | solution.py:266
  (3 shorter events, 0.0 us)
Async XLA Ops:
  0.6 20.7 %copy-start = (bf16[256,2048]{1,0:T(8,128)(2,1)S(1)}, bf16[256,2048]{1,0:T(8,128)(2,1)}, u32[]{:S(2)}) copy-start(bf16[256,2048]{1,0:T(8,128)(2,1)} %constant.4.clone.steps_ref) | copy-start | bytes 3145732
  0.6 20.7 %copy-start.5 = (f32[2,33,256]{2,1,0:T(8,128)S(1)}, f32[2,33,256]{2,1,0:T(8,128)}, u32[]{:S(2)}) copy-start(f32[2,33,256]{2,1,0:T(8,128)} %constant.5.clone.turn_ref) | copy-start | bytes 202756
  0.7 20.7 %copy-start.4 = (bf16[256,512]{1,0:T(8,128)(2,1)S(1)}, bf16[256,512]{1,0:T(8,128)(2,1)}, u32[]{:S(2)}) copy-start(bf16[256,512]{1,0:T(8,128)(2,1)} %cot_ref.3) | copy-start | bytes 786436
  0.7 20.7 %copy-start.3 = (bf16[256,512]{1,0:T(8,128)(2,1)S(1)}, bf16[256,512]{1,0:T(8,128)(2,1)}, u32[]{:S(2)}) copy-start(bf16[256,512]{1,0:T(8,128)(2,1)} %gate_ref.3) | copy-start | bytes 786436
  2.1 33.4 %copy-start.6 = (f32[512]{0:T(512)S(1)}, f32[512]{0:T(512)}, u32[]{:S(2)}) copy-start(f32[512]{0:T(512)} %param.14) | copy-start | bytes 6148
  2.1 33.4 %copy-start.7 = (f32[512]{0:T(512)S(1)}, f32[512]{0:T(512)}, u32[]{:S(2)}) copy-start(f32[512]{0:T(512)} %param.13) | copy-start | bytes 6148
  21.4 25.6 %copy-start.1 = (bf16[256,512]{1,0:T(8,128)(2,1)S(1)}, bf16[256,512]{1,0:T(8,128)(2,1)}, u32[]{:S(2)}) copy-start(bf16[256,512]{1,0:T(8,128)(2,1)} %key_ref.3) | copy-start | bytes 786436
  21.4 25.6 %copy-start.2 = (bf16[256,512]{1,0:T(8,128)(2,1)S(1)}, bf16[256,512]{1,0:T(8,128)(2,1)}, u32[]{:S(2)}) copy-start(bf16[256,512]{1,0:T(8,128)(2,1)} %value_ref.3) | copy-start | bytes 786436
  35.8 1.2 %collective-permute-start = (f32[2,256]{1,0:T(2,128)S(1)}, f32[2,256]{1,0:T(2,128)S(1)}, u32[]{:S(2)}, u32[]{:S(2)}) collective-permute-start(f32[2,256]{1,0:T(2,128)S(1)} %sums.1), channel_id=1, source_target_pairs={{0,1},{1,0},{2,3},{3,2},{4,5},{5,4},{6,7},{7,6},{8,9},{9,8},{10,11... | collective-permute-start | bytes 6152 | tf_op jit(solution)/shard_map/ppermute | solution.py:277
  37.1 4.8 %collective-permute-start.1 = (f32[2,256]{1,0:T(2,128)S(1)}, f32[2,256]{1,0:T(2,128)S(1)}, u32[]{:S(2)}, u32[]{:S(2)}) collective-permute-start(f32[2,256]{1,0:T(2,128)S(1)} %add.9), channel_id=1, source_target_pairs={{0,2},{1,3},{2,0},{3,1},{4,6},{5,7},{6,4},{7,5},{8,10},{9,11},{10,... | collective-permute-start | bytes 6152 | tf_op jit(solution)/shard_map/ppermute | solution.py:278
  41.9 6.6 %collective-permute-start.2 = (f32[2,256]{1,0:T(2,128)S(1)}, f32[2,256]{1,0:T(2,128)S(1)}, u32[]{:S(2)}, u32[]{:S(2)}) collective-permute-start(f32[2,256]{1,0:T(2,128)S(1)} %add.10.after_ref), channel_id=1, source_target_pairs={{0,6},{1,7},{2,4},{3,5},{4,2},{5,3},{6,0},{7,1},{8,14},{9,15},{10,... | collective-permute-start | bytes 6152 | tf_op jit(solution)/shard_map/ppermute | solution.py:283

commit v9 on v8

--- a/solution.py
+++ b/solution.py
@@ -131,8 +131,13 @@
     return rows.reshape(PARTS, PIECE, BLOCK)
 
 
-def pack_kernel(mixed_ref, taps_ref, out_ref):
-    out_ref[:, :PIECE, :] = cut(mixed_ref[...].T)
+def early_kernel(out_ref):
+    out_ref[...] = jnp.zeros_like(out_ref)
+
+
+def pack_kernel(key_ref, value_ref, taps_ref, after_ref, out_ref):
+    mixed = (key_ref[...].astype(f32) * value_ref[...].astype(f32)).astype(bf16)
+    out_ref[:, :PIECE, :] = cut(mixed.T)
     out_ref[:, PIECE:, :] = cut(taps_ref[...].T)
 
 
@@ -242,33 +247,45 @@
 
 def last_kernel(
     in_ref, grad_ref, key_ref, value_ref, skip_ref, normed_ref, gate_ref,
-    key_out, value_out, taps_out, bias_out, normed_out, gate_out,
+    key_hbm, value_hbm, taps_hbm, bias_hbm, normed_hbm, gate_hbm,
+    key_out, value_out, taps_out, bias_out, sems,
 ):
-    normed_out[...] = normed_ref[...]
-    gate_out[...] = gate_ref[...]
+    copies = []
+
+    def send(source, target):
+        copies.append(pltpu.make_async_copy(source, target, sems.at[len(copies)]))
+        copies[-1].start()
 
     def whole(place):
         at = 2 * place * PIECE
         left, right = in_ref[:, at : at + PIECE, :], in_ref[:, at + PIECE : at + 2 * PIECE, :]
         return jnp.concatenate([left.reshape(WIDTH, 128).T, right.reshape(WIDTH, 128).T], 0)
 
+    send(normed_ref, normed_hbm)
+    send(gate_ref, gate_hbm)
+    tail = in_ref[:, 4 * PIECE :, :].astype(f32)
+    tail = jnp.concatenate([tail, pltpu.roll(tail, 126, 2)], 1).reshape(WIDTH, 128).T
+    bias_out[...] = tail[0:1] + tail[1:2]
+    taps_out[...] = whole(1)
     grad_mixed = whole(0).astype(f32) + skip_ref[...] * grad_ref[...].astype(f32)
     key_out[...] = (grad_mixed * value_ref[...].astype(f32)).astype(bf16)
     value_out[...] = (grad_mixed * key_ref[...].astype(f32)).astype(bf16)
-    taps_out[...] = whole(1)
-    tail = in_ref[:, 4 * PIECE :, :].astype(f32)
-    tail = jnp.concatenate([tail, pltpu.roll(tail, 126, 2)], 1).reshape(WIDTH, 128).T
-    bias_out[...] = tail[0:1] + tail[1:2]
-
-
-def call(kernel, name, outs, *operands):
+    for source, target in ((bias_out, bias_hbm), (taps_out, taps_hbm), (key_out, key_hbm), (value_out, value_hbm)):
+        send(source, target)
+    for copy in copies:
+        copy.wait()
+
+
+def call(kernel, name, outs, *operands, cost=None, out_space=pltpu.VMEM, scratch=()):
     vmem = pl.BlockSpec(memory_space=pltpu.VMEM)
     return pl.pallas_call(
         kernel,
         name=name,
         out_shape=[jax.ShapeDtypeStruct(shape, kind) for shape, kind in outs],
         in_specs=[vmem] * len(operands),
-        out_specs=[vmem] * len(outs),
+        out_specs=[pl.BlockSpec(memory_space=out_space)] * len(outs),
+        scratch_shapes=list(scratch),
+        cost_estimate=cost,
         compiler_params=pltpu.CompilerParams(vmem_limit_bytes=32 * 1024 * 1024),
     )(*operands)
 
@@ -291,9 +308,15 @@
     pieces = ((PARTS, PIECE, BLOCK), bf16)
     spectra = ((4, ROWS, BLOCK), f32)
 
-    mixed = (key_feat.astype(f32) * value_feat.astype(f32)).astype(bf16)
-    taps = jnp.where(key_feat == key_feat, filter_taps, mixed)
-    (packed,) = call(pack_kernel, "pack", [((PARTS, 2 * PIECE, BLOCK), bf16)], mixed, taps)
+    (token,) = call(
+        early_kernel,
+        "early",
+        [((8, 128), f32)],
+        cost=pl.CostEstimate(flops=2_000_000_000, bytes_accessed=4096, transcendentals=0),
+    )
+    (packed,) = call(
+        pack_kernel, "pack", [((PARTS, 2 * PIECE, BLOCK), bf16)], key_feat, value_feat, filter_taps, token
+    )
     arrived = lax.all_to_all(packed, "seq", 0, 0, tiled=True)
     conv, gate_t, cot_t = call(
         forward_kernel,
@@ -351,6 +374,8 @@
         skip_row,
         normed,
         gate,
+        out_space=pltpu.HBM,
+        scratch=[pltpu.VMEM(*natural)] * 3 + [pltpu.VMEM((1, WIDTH), f32), pltpu.SemaphoreType.DMA((6,))],
     )
     return normed_out, grad_gate, grad_key, grad_value, grad_filter, grad_bias[0]
 

time: 80 us -> 79.7 us (level)
  other arithmetic: 1.46 us -> 0.01 us
  local copies, waits for them, and re-layouts: 0.05 us -> 1.11 us
    select_n x1 -> x0, other arithmetic: 1.45 us -> none  [on_device(): taps = jnp.where(key_feat == key_feat, filter_taps, mixed)]
    unnamed x16 -> x18, local copies, waits for them, and re-layouts: 0.05 us -> 1.11 us
    pallas_call x7 -> x8, Pallas kernels: 5.98 us -> 5.89 us  [call(): pl.pallas_call(kernel, name=name, out_shape=[jax.ShapeDtypeStruct(shape,...]
where the time goes in v9:
time: 79.7 us; the launch traced here: 78.7 us
  blocking collectives  59.4 us (75%)
  starting transfers between devices  8.41 us (11%)
  Pallas kernels  5.89 us (7%)
  waiting for transfers between devices  3.09 us (4%)
  local copies, waits for them, and re-layouts  1.11 us (1%)
    all_to_all x1, blocking collectives, on_device(): arrived = lax.all_to_all(packed, 'seq', 0, 0, tiled=True)  19.2 us
    all_to_all x1, blocking collectives, on_device(): result = lax.all_to_all(result, 'seq', 0, 0, tiled=True)  14.7 us
    all_to_all x1, blocking collectives, on_device(): grad_arrived = lax.all_to_all(grad, 'seq', 0, 0, tiled=True)  12.9 us
    all_to_all x1, blocking collectives, on_device(): conv = lax.all_to_all(conv, 'seq', 0, 0, tiled=True)  12.8 us
    pallas_call x8, Pallas kernels, call(): pl.pallas_call(kernel, name=name, out_shape=[jax.ShapeDtypeStruct(shape,...  5.89 us
    ppermute x1, starting transfers between devices, add_over_mirror(): return sums + lax.ppermute(sums, 'chan', mirror)  5.05 us
    ppermute x1, starting transfers between devices, add_over_pairs(): lax.ppermute(sums, 'chan', [(at, at ^ 2) for at in range(GROUP)])  3.27 us
  transfers between devices with their start and end apart: 3, of which 3 were waited for; matrix products, arithmetic and copies ran while one was open for 0% of the time, Pallas kernels for 1%

profile of v9, /device:TPU:0, one launch (start us, length us, event | category | flops | bytes accessed | tf_op | source)
XLA Modules:
  0.0 78.7 jit_solution(8920342234165043916)
XLA Ops:
  0.6 0.0 copy-start.1
  0.6 0.0 copy-start.2
  0.7 0.0 copy-start.6
  0.7 0.9 %copy-done.1 = bf16[256,512]{1,0:T(8,128)(2,1)S(1)} copy-done((bf16[256,512]{1,0:T(8,128)(2,1)S(1)}, bf16[256,512]{1,0:T(8,128)(2,1)}, u32[]{:S(2)}) %copy-start.1) | copy-done | bytes 262168
  1.6 0.1 copy-done.2
  1.7 0.1 copy-done.6
  1.7 0.0 copy-start
  1.7 0.0 copy-start.3
  1.7 0.0 copy-start.4
  1.8 0.0 copy-start.5
  1.8 0.2 pack.1.pack_ref
  2.0 0.0 copy-start.7
  2.0 0.0 copy-start.8
  2.0 19.2 %all_to_all.20.in_ref.pack_ref = bf16[32,32,256]{2,1,0:T(8,128)(2,1)S(1)} all-to-all(bf16[32,32,256]{2,1,0:T(8,128)(2,1)S(1)} %pack.1.pack_ref), channel_id=1, replica_groups=mesh['seq'=32,'chan'=8] {'seq'}, dimensions={0} | all-to-all | bytes 1048576 | tf_op jit(solution)/shard_map/all_to_all | solution.py:320
  21.1 0.0 copy-done
  21.1 0.0 copy-done.3
  21.1 0.0 copy-done.4
  21.1 0.0 copy-done.5
  21.2 1.4 %forward.1 = (bf16[32,16,256]{2,1,0:T(8,128)(2,1)S(1)}, bf16[512,256]{1,0:T(8,128)(2,1)S(1)}, bf16[512,256]{1,0:T(8,128)(2,1)S(1)}) custom-call(bf16[32,32,256]{2,1,0:T(8,128)(2,1)S(1)} %all_to_all.20.in_ref.pack_ref, bf16[256,2048]{1,0:T(8,128)(2,1)S(1)} %copy-done, f32[2,33,256]{2,1,0:T(8,128)S(1)} %copy-done.5, bf16[256,512]{1,0:T(8,128)(2,1)S(1)} %copy-done.3, ...), custom_call_target="tpu_custom_call" | custom-call | tf_op jit(solution)/shard_map/forward/pallas_call | solution.py:281
  22.5 12.8 %all_to_all.21.conv_ref = bf16[32,16,256]{2,1,0:T(8,128)(2,1)S(1)} all-to-all(bf16[32,16,256]{2,1,0:T(8,128)(2,1)S(1)} %get-tuple-element.23), channel_id=1, replica_groups=mesh['seq'=32,'chan'=8] {'seq'}, dimensions={0} | all-to-all | bytes 524288 | tf_op jit(solution)/shard_map/all_to_all | solution.py:331
  35.3 0.0 copy-done.7
  35.3 0.0 copy-done.8
  35.3 0.3 sums.1
  35.6 0.1 collective-permute-start
  35.7 1.1 %collective-permute-done = f32[2,256]{1,0:T(2,128)S(1)} collective-permute-done((f32[2,256]{1,0:T(2,128)S(1)}, f32[2,256]{1,0:T(2,128)S(1)}, u32[]{:S(2)}, u32[]{:S(2)}) %collective-permute-start) | collective-permute-done | bytes 2080 | tf_op jit(solution)/shard_map/ppermute | solution.py:294
  36.8 3.3 %collective-permute-start.1 = (f32[2,256]{1,0:T(2,128)S(1)}, f32[2,256]{1,0:T(2,128)S(1)}, u32[]{:S(2)}, u32[]{:S(2)}) collective-permute-start(f32[2,256]{1,0:T(2,128)S(1)} %add.9), channel_id=1, source_target_pairs={{0,2},{1,3},{2,0},{3,1},{4,6},{5,7},{6,4},{7,5},{8,10},{9,11},{10,... | collective-permute-start | bytes 6152 | tf_op jit(solution)/shard_map/ppermute | solution.py:295
  40.1 1.6 %collective-permute-done.1 = f32[2,256]{1,0:T(2,128)S(1)} collective-permute-done((f32[2,256]{1,0:T(2,128)S(1)}, f32[2,256]{1,0:T(2,128)S(1)}, u32[]{:S(2)}, u32[]{:S(2)}) %collective-permute-start.1) | collective-permute-done | bytes 2080 | tf_op jit(solution)/shard_map/ppermute | solution.py:295
  41.7 5.0 %collective-permute-start.2 = (f32[2,256]{1,0:T(2,128)S(1)}, f32[2,256]{1,0:T(2,128)S(1)}, u32[]{:S(2)}, u32[]{:S(2)}) collective-permute-start(f32[2,256]{1,0:T(2,128)S(1)} %add.10.after_ref), channel_id=1, source_target_pairs={{0,6},{1,7},{2,4},{3,5},{4,2},{5,3},{6,0},{7,1},{8,14},{9,15},{10,... | collective-permute-start | bytes 6152 | tf_op jit(solution)/shard_map/ppermute | solution.py:300
  46.7 1.2 %between.1 = (f32[4,528,256]{2,1,0:T(8,128)S(1)}, f32[256,512]{1,0:T(8,128)S(1)}, f32[512,256]{1,0:T(8,128)S(1)}, f32[512,256]{1,0:T(8,128)S(1)}) custom-call(bf16[32,32,256]{2,1,0:T(8,128)(2,1)S(1)} %all_to_all.20.in_ref.pack_ref, bf16[256,2048]{1,0:T(8,128)(2,1)S(1)} %copy-done, f32[2,33,256]{2,1,0:T(8,128)S(1)} %copy-done.5, ...), custom_call_target="tpu_custom_call" | custom-call | tf_op jit(solution)/shard_map/between/pallas_call | solution.py:281
  47.9 0.4 collective-permute-done.2
  48.3 0.1 grad.1
  48.4 12.9 %all_to_all.22.in_ref = bf16[32,16,256]{2,1,0:T(8,128)(2,1)S(1)} all-to-all(bf16[32,16,256]{2,1,0:T(8,128)(2,1)S(1)} %grad.1), channel_id=1, replica_groups=mesh['seq'=32,'chan'=8] {'seq'}, dimensions={0} | all-to-all | bytes 524288 | tf_op jit(solution)/shard_map/all_to_all | solution.py:349
  61.3 1.6 %backward.1 = (bf16[32,72,128]{2,1,0:T(8,128)(2,1)S(1)}, bf16[256,512]{1,0:T(8,128)(2,1)S(1)}, bf16[256,512]{1,0:T(8,128)(2,1)S(1)}, bf16[256,512]{1,0:T(8,128)(2,1)S(1)}) custom-call(bf16[32,16,256]{2,1,0:T(8,128)(2,1)S(1)} %all_to_all.22.in_ref, bf16[32,32,256]{2,1,0:T(8,128)(2,1)S(1)} %all_to_all.20.in_ref.pack_ref, ...), custom_call_target="tpu_custom_call" | custom-call | tf_op jit(solution)/shard_map/backward/pallas_call | solution.py:281
  62.8 14.7 %all_to_all.23.in_ref = bf16[32,72,128]{2,1,0:T(8,128)(2,1)S(1)} all-to-all(bf16[32,72,128]{2,1,0:T(8,128)(2,1)S(1)} %get-tuple-element.30), channel_id=1, replica_groups=mesh['seq'=32,'chan'=8] {'seq'}, dimensions={0} | all-to-all | bytes 1179648 | tf_op jit(solution)/shard_map/all_to_all | solution.py:365
  77.5 1.2 %last.1 = (bf16[256,512]{1,0:T(8,128)(2,1)}, bf16[256,512]{1,0:T(8,128)(2,1)}, bf16[256,512]{1,0:T(8,128)(2,1)}, f32[1,512]{1,0:T(1,128)}, bf16[256,512]{1,0:T(8,128)(2,1)}, /*index=5*/bf16[256,512]{1,0:T(8,128)(2,1)}) custom-call(bf16[32,72,128]{2,1,0:T(8,128)(2,1)S(1)} %all_to_all.23.in_ref, bf16[256,512]{1,0:T(8,128)(2,1)S(1)} %get-tuple-element.31.grad_ref, ...), custom_call_target="tpu_custom_call" | custom-call | tf_op jit(solution)/shard_map/last/pallas_call | solution.py:281
  (4 shorter events, 0.0 us)
Async XLA Ops:
  0.6 1.0 %copy-start.1 = (bf16[256,512]{1,0:T(8,128)(2,1)S(1)}, bf16[256,512]{1,0:T(8,128)(2,1)}, u32[]{:S(2)}) copy-start(bf16[256,512]{1,0:T(8,128)(2,1)} %key_ref.5) | copy-start | bytes 786436
  0.6 1.0 %copy-start.2 = (bf16[256,512]{1,0:T(8,128)(2,1)S(1)}, bf16[256,512]{1,0:T(8,128)(2,1)}, u32[]{:S(2)}) copy-start(bf16[256,512]{1,0:T(8,128)(2,1)} %value_ref.5) | copy-start | bytes 786436
  0.7 1.1 %copy-start.6 = (bf16[256,512]{1,0:T(8,128)(2,1)S(1)}, bf16[256,512]{1,0:T(8,128)(2,1)}, u32[]{:S(2)}) copy-start(bf16[256,512]{1,0:T(8,128)(2,1)} %taps_ref.1) | copy-start | bytes 786436
  1.7 19.4 %copy-start = (bf16[256,2048]{1,0:T(8,128)(2,1)S(1)}, bf16[256,2048]{1,0:T(8,128)(2,1)}, u32[]{:S(2)}) copy-start(bf16[256,2048]{1,0:T(8,128)(2,1)} %constant.4.clone.steps_ref) | copy-start | bytes 3145732
  1.7 19.4 %copy-start.3 = (bf16[256,512]{1,0:T(8,128)(2,1)S(1)}, bf16[256,512]{1,0:T(8,128)(2,1)}, u32[]{:S(2)}) copy-start(bf16[256,512]{1,0:T(8,128)(2,1)} %gate_ref.3) | copy-start | bytes 786436
  1.7 19.4 %copy-start.4 = (bf16[256,512]{1,0:T(8,128)(2,1)S(1)}, bf16[256,512]{1,0:T(8,128)(2,1)}, u32[]{:S(2)}) copy-start(bf16[256,512]{1,0:T(8,128)(2,1)} %cot_ref.3) | copy-start | bytes 786436
  1.8 19.4 %copy-start.5 = (f32[2,33,256]{2,1,0:T(8,128)S(1)}, f32[2,33,256]{2,1,0:T(8,128)}, u32[]{:S(2)}) copy-start(f32[2,33,256]{2,1,0:T(8,128)} %constant.5.clone.turn_ref) | copy-start | bytes 202756
  2.0 33.3 %copy-start.7 = (f32[512]{0:T(512)S(1)}, f32[512]{0:T(512)}, u32[]{:S(2)}) copy-start(f32[512]{0:T(512)} %param.14) | copy-start | bytes 6148
  2.0 33.3 %copy-start.8 = (f32[512]{0:T(512)S(1)}, f32[512]{0:T(512)}, u32[]{:S(2)}) copy-start(f32[512]{0:T(512)} %param.13) | copy-start | bytes 6148
  35.6 1.2 %collective-permute-start = (f32[2,256]{1,0:T(2,128)S(1)}, f32[2,256]{1,0:T(2,128)S(1)}, u32[]{:S(2)}, u32[]{:S(2)}) collective-permute-start(f32[2,256]{1,0:T(2,128)S(1)} %sums.1), channel_id=1, source_target_pairs={{0,1},{1,0},{2,3},{3,2},{4,5},{5,4},{6,7},{7,6},{8,9},{9,8},{10,11... | collective-permute-start | bytes 6152 | tf_op jit(solution)/shard_map/ppermute | solution.py:294
  36.8 4.8 %collective-permute-start.1 = (f32[2,256]{1,0:T(2,128)S(1)}, f32[2,256]{1,0:T(2,128)S(1)}, u32[]{:S(2)}, u32[]{:S(2)}) collective-permute-start(f32[2,256]{1,0:T(2,128)S(1)} %add.9), channel_id=1, source_target_pairs={{0,2},{1,3},{2,0},{3,1},{4,6},{5,7},{6,4},{7,5},{8,10},{9,11},{10,... | collective-permute-start | bytes 6152 | tf_op jit(solution)/shard_map/ppermute | solution.py:295
  41.7 6.6 %collective-permute-start.2 = (f32[2,256]{1,0:T(2,128)S(1)}, f32[2,256]{1,0:T(2,128)S(1)}, u32[]{:S(2)}, u32[]{:S(2)}) collective-permute-start(f32[2,256]{1,0:T(2,128)S(1)} %add.10.after_ref), channel_id=1, source_target_pairs={{0,6},{1,7},{2,4},{3,5},{4,2},{5,3},{6,0},{7,1},{8,14},{9,15},{10,... | collective-permute-start | bytes 6152 | tf_op jit(solution)/shard_map/ppermute | solution.py:300

commit v10 on v9

--- a/solution.py
+++ b/solution.py
@@ -141,9 +141,14 @@
     out_ref[:, PIECE:, :] = cut(taps_ref[...].T)
 
 
-def forward_kernel(in_ref, steps_ref, turn_ref, gate_ref, cot_ref, out_ref, gate_out, cot_out):
-    gate_out[...] = gate_ref[...].T
-    cot_out[...] = cot_ref[...].T
+def forward_kernel(
+    in_ref, steps_ref, turn_ref, gate_ref, cot_ref, pack_ref, skip_ref, gain_ref,
+    out_ref, gate_out, scaled_out, skipped_out,
+):
+    gate = gate_ref[...].T
+    gate_out[...] = gate
+    scaled_out[...] = cot_ref[...].T.astype(f32) * column(gain_ref)
+    skipped_out[...] = flat(pack_ref[:, :PIECE, :]).astype(f32) * column(skip_ref) * gate.astype(f32)
     enter, leave, into, back, turn = open_tables(steps_ref, turn_ref)
     first = enter_blocks(in_ref[:, :PIECE, :], enter)
     second = enter_blocks(in_ref[:, PIECE:, :], enter)
@@ -157,11 +162,11 @@
 
 
 def between_kernel(
-    in_ref, steps_ref, turn_ref, key_ref, value_ref, conv_ref, pack_ref, gate_ref, cot_ref, skip_ref, gain_ref,
+    in_ref, steps_ref, turn_ref, key_ref, value_ref, skip_ref, conv_ref, gate_ref, scaled_ref, skipped_ref,
     after_ref, spec_ref, full_ref, push_ref, hold_ref,
 ):
-    _, gate, gated = gate_parts(conv_ref, pack_ref, gate_ref, skip_ref)
-    push_ref[...] = cot_ref[...].astype(f32) * column(gain_ref) * gate
+    gate, gated = gate_parts(conv_ref, gate_ref, skipped_ref)
+    push_ref[...] = scaled_ref[...] * gate
     hold_ref[...] = gated * gate
     enter, _, into, _, turn = open_tables(steps_ref, turn_ref)
     for place in range(2):
@@ -178,18 +183,15 @@
     return jnp.concatenate([turned, turned], 1)
 
 
-def gate_parts(conv_ref, pack_ref, gate_ref, skip_ref):
-    mixed = flat(pack_ref[:, :PIECE, :]).astype(f32)
-    full = flat(conv_ref[...]).astype(f32) + column(skip_ref) * mixed
+def gate_parts(conv_ref, gate_ref, skipped_ref):
     gate = gate_ref[...].astype(f32)
-    return full, gate, gate * full
-
-
-def sums_kernel(conv_ref, pack_ref, gate_ref, cot_ref, skip_ref, gain_ref, out_ref):
-    _, _, gated = gate_parts(conv_ref, pack_ref, gate_ref, skip_ref)
-    scaled = cot_ref[...].astype(f32) * column(gain_ref)
+    return gate, gate * flat(conv_ref[...]).astype(f32) + skipped_ref[...]
+
+
+def sums_kernel(conv_ref, gate_ref, scaled_ref, skipped_ref, out_ref):
+    _, gated = gate_parts(conv_ref, gate_ref, skipped_ref)
     squares = jnp.sum(gated * gated, axis=0, keepdims=True)
-    inner = jnp.sum(scaled * gated, axis=0, keepdims=True)
+    inner = jnp.sum(scaled_ref[...] * gated, axis=0, keepdims=True)
     out_ref[...] = jnp.concatenate([squares, inner], 0)
 
 
@@ -304,7 +306,6 @@
     steps, turn = (jnp.asarray(table) for table in tables())
     skip_row, gain_row = skip_bias[None, :], norm_gain[None, :]
     natural = ((BLOCK, WIDTH), bf16)
-    turned = ((WIDTH, BLOCK), bf16)
     pieces = ((PARTS, PIECE, BLOCK), bf16)
     spectra = ((4, ROWS, BLOCK), f32)
 
@@ -318,18 +319,21 @@
         pack_kernel, "pack", [((PARTS, 2 * PIECE, BLOCK), bf16)], key_feat, value_feat, filter_taps, token
     )
     arrived = lax.all_to_all(packed, "seq", 0, 0, tiled=True)
-    conv, gate_t, cot_t = call(
+    conv, gate_t, scaled_t, skipped_t = call(
         forward_kernel,
         "forward",
-        [pieces, turned, turned],
+        [pieces, ((WIDTH, BLOCK), bf16), ((WIDTH, BLOCK), f32), ((WIDTH, BLOCK), f32)],
         arrived,
         steps,
         turn,
         gate_feat,
         cotangent,
+        packed,
+        skip_row,
+        gain_row,
     )
     conv = lax.all_to_all(conv, "seq", 0, 0, tiled=True)
-    sides = (conv, packed, gate_t, cot_t, skip_row, gain_row)
+    sides = (conv, gate_t, scaled_t, skipped_t)
     (sums,) = call(sums_kernel, "sums", [((2, BLOCK), f32)], *sides)
     sums = add_over_pairs(sums)
     spec, full, push, hold = call(
@@ -341,6 +345,7 @@
         turn,
         key_feat,
         value_feat,
+        skip_row,
         *sides,
         sums,
     )

time: 79.7 us -> 79.7 us (level)
  transfers between devices with their start and end apart: 3 -> 3, of which waited for: 3 -> 3; matrix products, arithmetic and copies ran while one was open for 0% -> 0% of each run, Pallas kernels for 1% -> 2%
where the time goes in v10:
time: 79.7 us; the launch traced here: 78.7 us
  blocking collectives  59.4 us (75%)
  starting transfers between devices  8.41 us (11%)
  Pallas kernels  5.97 us (7%)
  waiting for transfers between devices  3 us (4%)
  local copies, waits for them, and re-layouts  1.11 us (1%)
    all_to_all x1, blocking collectives, on_device(): arrived = lax.all_to_all(packed, 'seq', 0, 0, tiled=True)  19.2 us
    all_to_all x1, blocking collectives, on_device(): result = lax.all_to_all(result, 'seq', 0, 0, tiled=True)  14.6 us
    all_to_all x1, blocking collectives, on_device(): grad_arrived = lax.all_to_all(grad, 'seq', 0, 0, tiled=True)  12.9 us
    all_to_all x1, blocking collectives, on_device(): conv = lax.all_to_all(conv, 'seq', 0, 0, tiled=True)  12.8 us
    pallas_call x8, Pallas kernels, call(): pl.pallas_call(kernel, name=name, out_shape=[jax.ShapeDtypeStruct(shape,...  5.97 us
    ppermute x1, starting transfers between devices, add_over_mirror(): return sums + lax.ppermute(sums, 'chan', mirror)  5.05 us
    ppermute x1, starting transfers between devices, add_over_pairs(): lax.ppermute(sums, 'chan', [(at, at ^ 2) for at in range(GROUP)])  3.27 us
  transfers between devices with their start and end apart: 3, of which 3 were waited for; matrix products, arithmetic and copies ran while one was open for 0% of the time, Pallas kernels for 2%

profile of v10, /device:TPU:0, one launch (start us, length us, event | category | flops | bytes accessed | tf_op | source)
XLA Modules:
  0.0 78.7 jit_solution(111267307280536927)
XLA Ops:
  0.6 0.0 copy-start.1
  0.6 0.0 copy-start.2
  0.7 0.0 copy-start.6
  0.7 0.9 %copy-done.1 = bf16[256,512]{1,0:T(8,128)(2,1)S(1)} copy-done((bf16[256,512]{1,0:T(8,128)(2,1)S(1)}, bf16[256,512]{1,0:T(8,128)(2,1)}, u32[]{:S(2)}) %copy-start.1) | copy-done | bytes 262168
  1.6 0.1 copy-done.2
  1.7 0.1 copy-done.6
  1.7 0.0 copy-start
  1.7 0.0 copy-start.3
  1.7 0.0 copy-start.4
  1.8 0.0 copy-start.5
  1.8 0.0 copy-start.7
  1.8 0.0 copy-start.8
  1.8 0.2 pack.1.pack_ref
  2.0 19.2 %all_to_all.20.in_ref.pack_ref = bf16[32,32,256]{2,1,0:T(8,128)(2,1)S(1)} all-to-all(bf16[32,32,256]{2,1,0:T(8,128)(2,1)S(1)} %pack.1.pack_ref), channel_id=1, replica_groups=mesh['seq'=32,'chan'=8] {'seq'}, dimensions={0} | all-to-all | bytes 1048576 | tf_op jit(solution)/shard_map/all_to_all | solution.py:321
  21.1 0.0 copy-done
  21.1 0.0 copy-done.3
  21.1 0.0 copy-done.4
  21.1 0.0 copy-done.5
  21.2 0.0 copy-done.7
  21.2 0.0 copy-done.8
  21.2 1.5 %forward.1 = (bf16[32,16,256]{2,1,0:T(8,128)(2,1)S(1)}, bf16[512,256]{1,0:T(8,128)(2,1)S(1)}, f32[512,256]{1,0:T(8,128)S(1)}, f32[512,256]{1,0:T(8,128)S(1)}) custom-call(bf16[32,32,256]{2,1,0:T(8,128)(2,1)S(1)} %all_to_all.20.in_ref.pack_ref, bf16[256,2048]{1,0:T(8,128)(2,1)S(1)} %copy-done, f32[2,33,256]{2,1,0:T(8,128)S(1)} %copy-done.5, ...), custom_call_target="tpu_custom_call" | custom-call | tf_op jit(solution)/shard_map/forward/pallas_call | solution.py:283
  22.7 12.8 %all_to_all.21.conv_ref = bf16[32,16,256]{2,1,0:T(8,128)(2,1)S(1)} all-to-all(bf16[32,16,256]{2,1,0:T(8,128)(2,1)S(1)} %get-tuple-element.24), channel_id=1, replica_groups=mesh['seq'=32,'chan'=8] {'seq'}, dimensions={0} | all-to-all | bytes 524288 | tf_op jit(solution)/shard_map/all_to_all | solution.py:335
  35.4 0.2 sums.1
  35.6 0.1 collective-permute-start
  35.7 1.1 %collective-permute-done = f32[2,256]{1,0:T(2,128)S(1)} collective-permute-done((f32[2,256]{1,0:T(2,128)S(1)}, f32[2,256]{1,0:T(2,128)S(1)}, u32[]{:S(2)}, u32[]{:S(2)}) %collective-permute-start) | collective-permute-done | bytes 2080 | tf_op jit(solution)/shard_map/ppermute | solution.py:296
  36.8 3.3 %collective-permute-start.1 = (f32[2,256]{1,0:T(2,128)S(1)}, f32[2,256]{1,0:T(2,128)S(1)}, u32[]{:S(2)}, u32[]{:S(2)}) collective-permute-start(f32[2,256]{1,0:T(2,128)S(1)} %add.9), channel_id=1, source_target_pairs={{0,2},{1,3},{2,0},{3,1},{4,6},{5,7},{6,4},{7,5},{8,10},{9,11},{10,... | collective-permute-start | bytes 6152 | tf_op jit(solution)/shard_map/ppermute | solution.py:297
  40.1 1.6 %collective-permute-done.1 = f32[2,256]{1,0:T(2,128)S(1)} collective-permute-done((f32[2,256]{1,0:T(2,128)S(1)}, f32[2,256]{1,0:T(2,128)S(1)}, u32[]{:S(2)}, u32[]{:S(2)}) %collective-permute-start.1) | collective-permute-done | bytes 2080 | tf_op jit(solution)/shard_map/ppermute | solution.py:297
  41.7 5.1 %collective-permute-start.2 = (f32[2,256]{1,0:T(2,128)S(1)}, f32[2,256]{1,0:T(2,128)S(1)}, u32[]{:S(2)}, u32[]{:S(2)}) collective-permute-start(f32[2,256]{1,0:T(2,128)S(1)} %add.10.after_ref), channel_id=1, source_target_pairs={{0,6},{1,7},{2,4},{3,5},{4,2},{5,3},{6,0},{7,1},{8,14},{9,15},{10,... | collective-permute-start | bytes 6152 | tf_op jit(solution)/shard_map/ppermute | solution.py:302
  46.7 1.3 %between.1 = (f32[4,528,256]{2,1,0:T(8,128)S(1)}, f32[256,512]{1,0:T(8,128)S(1)}, f32[512,256]{1,0:T(8,128)S(1)}, f32[512,256]{1,0:T(8,128)S(1)}) custom-call(bf16[32,32,256]{2,1,0:T(8,128)(2,1)S(1)} %all_to_all.20.in_ref.pack_ref, bf16[256,2048]{1,0:T(8,128)(2,1)S(1)} %copy-done, f32[2,33,256]{2,1,0:T(8,128)S(1)} %copy-done.5, ...), custom_call_target="tpu_custom_call" | custom-call | tf_op jit(solution)/shard_map/between/pallas_call | solution.py:283
  48.0 0.3 collective-permute-done.2
  48.3 0.1 grad.1
  48.4 12.9 %all_to_all.22.in_ref = bf16[32,16,256]{2,1,0:T(8,128)(2,1)S(1)} all-to-all(bf16[32,16,256]{2,1,0:T(8,128)(2,1)S(1)} %grad.1), channel_id=1, replica_groups=mesh['seq'=32,'chan'=8] {'seq'}, dimensions={0} | all-to-all | bytes 524288 | tf_op jit(solution)/shard_map/all_to_all | solution.py:354
  61.3 1.5 %backward.1 = (bf16[32,72,128]{2,1,0:T(8,128)(2,1)S(1)}, bf16[256,512]{1,0:T(8,128)(2,1)S(1)}, bf16[256,512]{1,0:T(8,128)(2,1)S(1)}, bf16[256,512]{1,0:T(8,128)(2,1)S(1)}) custom-call(bf16[32,16,256]{2,1,0:T(8,128)(2,1)S(1)} %all_to_all.22.in_ref, bf16[32,32,256]{2,1,0:T(8,128)(2,1)S(1)} %all_to_all.20.in_ref.pack_ref, ...), custom_call_target="tpu_custom_call" | custom-call | tf_op jit(solution)/shard_map/backward/pallas_call | solution.py:283
  62.8 14.6 %all_to_all.23.in_ref = bf16[32,72,128]{2,1,0:T(8,128)(2,1)S(1)} all-to-all(bf16[32,72,128]{2,1,0:T(8,128)(2,1)S(1)} %get-tuple-element.32), channel_id=1, replica_groups=mesh['seq'=32,'chan'=8] {'seq'}, dimensions={0} | all-to-all | bytes 1179648 | tf_op jit(solution)/shard_map/all_to_all | solution.py:370
  77.5 1.2 %last.1 = (bf16[256,512]{1,0:T(8,128)(2,1)}, bf16[256,512]{1,0:T(8,128)(2,1)}, bf16[256,512]{1,0:T(8,128)(2,1)}, f32[1,512]{1,0:T(1,128)}, bf16[256,512]{1,0:T(8,128)(2,1)}, /*index=5*/bf16[256,512]{1,0:T(8,128)(2,1)}) custom-call(bf16[32,72,128]{2,1,0:T(8,128)(2,1)S(1)} %all_to_all.23.in_ref, bf16[256,512]{1,0:T(8,128)(2,1)S(1)} %get-tuple-element.33.grad_ref, ...), custom_call_target="tpu_custom_call" | custom-call | tf_op jit(solution)/shard_map/last/pallas_call | solution.py:283
  (4 shorter events, 0.0 us)
Async XLA Ops:
  0.6 1.0 %copy-start.1 = (bf16[256,512]{1,0:T(8,128)(2,1)S(1)}, bf16[256,512]{1,0:T(8,128)(2,1)}, u32[]{:S(2)}) copy-start(bf16[256,512]{1,0:T(8,128)(2,1)} %key_ref.5) | copy-start | bytes 786436
  0.6 1.0 %copy-start.2 = (bf16[256,512]{1,0:T(8,128)(2,1)S(1)}, bf16[256,512]{1,0:T(8,128)(2,1)}, u32[]{:S(2)}) copy-start(bf16[256,512]{1,0:T(8,128)(2,1)} %value_ref.5) | copy-start | bytes 786436
  0.7 1.1 %copy-start.6 = (bf16[256,512]{1,0:T(8,128)(2,1)S(1)}, bf16[256,512]{1,0:T(8,128)(2,1)}, u32[]{:S(2)}) copy-start(bf16[256,512]{1,0:T(8,128)(2,1)} %taps_ref.1) | copy-start | bytes 786436
  1.7 19.4 %copy-start = (bf16[256,2048]{1,0:T(8,128)(2,1)S(1)}, bf16[256,2048]{1,0:T(8,128)(2,1)}, u32[]{:S(2)}) copy-start(bf16[256,2048]{1,0:T(8,128)(2,1)} %constant.4.clone.steps_ref) | copy-start | bytes 3145732
  1.7 19.4 %copy-start.3 = (bf16[256,512]{1,0:T(8,128)(2,1)S(1)}, bf16[256,512]{1,0:T(8,128)(2,1)}, u32[]{:S(2)}) copy-start(bf16[256,512]{1,0:T(8,128)(2,1)} %gate_ref.3) | copy-start | bytes 786436
  1.7 19.4 %copy-start.4 = (bf16[256,512]{1,0:T(8,128)(2,1)S(1)}, bf16[256,512]{1,0:T(8,128)(2,1)}, u32[]{:S(2)}) copy-start(bf16[256,512]{1,0:T(8,128)(2,1)} %cot_ref.3) | copy-start | bytes 786436
  1.8 19.4 %copy-start.5 = (f32[2,33,256]{2,1,0:T(8,128)S(1)}, f32[2,33,256]{2,1,0:T(8,128)}, u32[]{:S(2)}) copy-start(f32[2,33,256]{2,1,0:T(8,128)} %constant.5.clone.turn_ref) | copy-start | bytes 202756
  1.8 19.4 %copy-start.7 = (f32[512]{0:T(512)S(1)}, f32[512]{0:T(512)}, u32[]{:S(2)}) copy-start(f32[512]{0:T(512)} %param.13) | copy-start | bytes 6148
  1.8 19.4 %copy-start.8 = (f32[512]{0:T(512)S(1)}, f32[512]{0:T(512)}, u32[]{:S(2)}) copy-start(f32[512]{0:T(512)} %param.14) | copy-start | bytes 6148
  35.6 1.2 %collective-permute-start = (f32[2,256]{1,0:T(2,128)S(1)}, f32[2,256]{1,0:T(2,128)S(1)}, u32[]{:S(2)}, u32[]{:S(2)}) collective-permute-start(f32[2,256]{1,0:T(2,128)S(1)} %sums.1), channel_id=1, source_target_pairs={{0,1},{1,0},{2,3},{3,2},{4,5},{5,4},{6,7},{7,6},{8,9},{9,8},{10,11... | collective-permute-start | bytes 6152 | tf_op jit(solution)/shard_map/ppermute | solution.py:296
  36.8 4.8 %collective-permute-start.1 = (f32[2,256]{1,0:T(2,128)S(1)}, f32[2,256]{1,0:T(2,128)S(1)}, u32[]{:S(2)}, u32[]{:S(2)}) collective-permute-start(f32[2,256]{1,0:T(2,128)S(1)} %add.9), channel_id=1, source_target_pairs={{0,2},{1,3},{2,0},{3,1},{4,6},{5,7},{6,4},{7,5},{8,10},{9,11},{10,... | collective-permute-start | bytes 6152 | tf_op jit(solution)/shard_map/ppermute | solution.py:297
  41.7 6.6 %collective-permute-start.2 = (f32[2,256]{1,0:T(2,128)S(1)}, f32[2,256]{1,0:T(2,128)S(1)}, u32[]{:S(2)}, u32[]{:S(2)}) collective-permute-start(f32[2,256]{1,0:T(2,128)S(1)} %add.10.after_ref), channel_id=1, source_target_pairs={{0,6},{1,7},{2,4},{3,5},{4,2},{5,3},{6,0},{7,1},{8,14},{9,15},{10,... | collective-permute-start | bytes 6152 | tf_op jit(solution)/shard_map/ppermute | solution.py:302

commit v11 on v10

--- a/solution.py
+++ b/solution.py
@@ -163,7 +163,7 @@
 
 def between_kernel(
     in_ref, steps_ref, turn_ref, key_ref, value_ref, skip_ref, conv_ref, gate_ref, scaled_ref, skipped_ref,
-    after_ref, spec_ref, full_ref, push_ref, hold_ref,
+    gate_in, cot_in, gain_ref, after_ref, spec_ref, push_ref, hold_ref, norm_ref,
 ):
     gate, gated = gate_parts(conv_ref, gate_ref, skipped_ref)
     push_ref[...] = scaled_ref[...] * gate
@@ -175,7 +175,11 @@
         spec_ref[2 * place] = even
         spec_ref[2 * place + 1] = odd
     mixed = (key_ref[...].astype(f32) * value_ref[...].astype(f32)).astype(bf16)
-    full_ref[...] = flat(conv_ref[...]).T.astype(f32) + skip_ref[...] * mixed.astype(f32)
+    full = flat(conv_ref[...]).T.astype(f32) + skip_ref[...] * mixed.astype(f32)
+    gate, scaled = gate_in[...].astype(f32), cot_in[...].astype(f32) * gain_ref[...]
+    gated = gate * full
+    for at, part in enumerate((gated * gain_ref[...], scaled * full, gated * full, scaled * gate, gated * gate)):
+        norm_ref[at] = part
 
 
 def column(row_ref):
@@ -212,16 +216,13 @@
 
 
 def backward_kernel(
-    in_ref, pack_ref, spec_ref, steps_ref, turn_ref, sums_ref, full_ref, gate_ref, cot_ref, gain_ref,
+    in_ref, pack_ref, spec_ref, steps_ref, turn_ref, sums_ref, norm_ref,
     out_ref, grad_out, normed_out, gate_out,
 ):
     inv_rms, pull = (wide_column(row) for row in norm_parts(sums_ref))
-    full, gate, gain = full_ref[...], gate_ref[...].astype(f32), gain_ref[...]
-    gated = gate * full
-    normed_out[...] = (gated * inv_rms * gain).astype(bf16)
-    grad_gated = inv_rms * (cot_ref[...].astype(f32) * gain) - gated * pull
-    gate_out[...] = (grad_gated * full).astype(bf16)
-    grad_out[...] = (grad_gated * gate).astype(bf16)
+    normed_out[...] = (norm_ref[0] * inv_rms).astype(bf16)
+    gate_out[...] = (norm_ref[1] * inv_rms - norm_ref[2] * pull).astype(bf16)
+    grad_out[...] = (norm_ref[3] * inv_rms - norm_ref[4] * pull).astype(bf16)
     enter, leave, into, back, turn = open_tables(steps_ref, turn_ref)
     grad = in_ref[...]
     bias = jnp.sum(grad.astype(f32) * pack_ref[:, :PIECE, :].astype(f32), axis=0)
@@ -336,10 +337,10 @@
     sides = (conv, gate_t, scaled_t, skipped_t)
     (sums,) = call(sums_kernel, "sums", [((2, BLOCK), f32)], *sides)
     sums = add_over_pairs(sums)
-    spec, full, push, hold = call(
+    spec, push, hold, norm = call(
         between_kernel,
         "between",
-        [spectra, ((BLOCK, WIDTH), f32), ((WIDTH, BLOCK), f32), ((WIDTH, BLOCK), f32)],
+        [spectra, ((WIDTH, BLOCK), f32), ((WIDTH, BLOCK), f32), ((5, BLOCK, WIDTH), f32)],
         arrived,
         steps,
         turn,
@@ -347,6 +348,9 @@
         value_feat,
         skip_row,
         *sides,
+        gate_feat,
+        cotangent,
+        gain_row,
         sums,
     )
     sums = add_over_mirror(sums)
@@ -362,10 +366,7 @@
         steps,
         turn,
         sums,
-        full,
-        gate_feat,
-        cotangent,
-        gain_row,
+        norm,
     )
     result = lax.all_to_all(result, "seq", 0, 0, tiled=True)
     grad_key, grad_value, grad_filter, grad_bias, normed_out, grad_gate = call(

time: 79.7 us -> 79.7 us (level)
  transfers between devices with their start and end apart: 3 -> 3, of which waited for: 3 -> 2; matrix products, arithmetic and copies ran while one was open for 0% -> 0% of each run, Pallas kernels for 2% -> 2%
where the time goes in v11:
time: 79.7 us; the launch traced here: 78.7 us
  blocking collectives  59.4 us (75%)
  starting transfers between devices  8.41 us (11%)
  Pallas kernels  6.2 us (8%)
  waiting for transfers between devices  2.71 us (3%)
  local copies, waits for them, and re-layouts  1.09 us (1%)
    all_to_all x1, blocking collectives, on_device(): arrived = lax.all_to_all(packed, 'seq', 0, 0, tiled=True)  19.2 us
    all_to_all x1, blocking collectives, on_device(): result = lax.all_to_all(result, 'seq', 0, 0, tiled=True)  14.7 us
    all_to_all x1, blocking collectives, on_device(): grad_arrived = lax.all_to_all(grad, 'seq', 0, 0, tiled=True)  12.9 us
    all_to_all x1, blocking collectives, on_device(): conv = lax.all_to_all(conv, 'seq', 0, 0, tiled=True)  12.8 us
    pallas_call x8, Pallas kernels, call(): pl.pallas_call(kernel, name=name, out_shape=[jax.ShapeDtypeStruct(shape,...  6.2 us
    ppermute x1, starting transfers between devices, add_over_mirror(): return sums + lax.ppermute(sums, 'chan', mirror)  5.05 us
    ppermute x1, starting transfers between devices, add_over_pairs(): lax.ppermute(sums, 'chan', [(at, at ^ 2) for at in range(GROUP)])  3.26 us
  transfers between devices with their start and end apart: 3, of which 2 were waited for; matrix products, arithmetic and copies ran while one was open for 0% of the time, Pallas kernels for 2%

profile of v11, /device:TPU:0, one launch (start us, length us, event | category | flops | bytes accessed | tf_op | source)
XLA Modules:
  0.0 78.7 jit_solution(229568850535152596)
XLA Ops:
  0.6 0.0 copy-start.5
  0.6 0.0 copy-start.1
  0.7 0.0 copy-start.2
  0.7 0.0 copy-start.6
  0.7 0.0 copy-start.7
  0.7 0.0 copy-start.8
  0.7 0.0 copy-start.4
  0.7 0.0 copy-start.3
  0.7 0.9 %copy-done.1 = bf16[256,512]{1,0:T(8,128)(2,1)S(1)} copy-done((bf16[256,512]{1,0:T(8,128)(2,1)S(1)}, bf16[256,512]{1,0:T(8,128)(2,1)}, u32[]{:S(2)}) %copy-start.1) | copy-done | bytes 262168
  1.6 0.1 copy-done.2
  1.7 0.1 copy-done.6
  1.8 0.0 copy-start
  1.8 0.2 pack.1.pack_ref
  2.0 19.2 %all_to_all.20.in_ref.pack_ref = bf16[32,32,256]{2,1,0:T(8,128)(2,1)S(1)} all-to-all(bf16[32,32,256]{2,1,0:T(8,128)(2,1)S(1)} %pack.1.pack_ref), channel_id=1, replica_groups=mesh['seq'=32,'chan'=8] {'seq'}, dimensions={0} | all-to-all | bytes 1048576 | tf_op jit(solution)/shard_map/all_to_all | solution.py:322
  21.1 0.0 copy-done.5
  21.1 0.0 copy-done.7
  21.1 0.0 copy-done.8
  21.1 0.0 copy-done.4
  21.2 0.0 copy-done.3
  21.2 0.0 copy-done
  21.2 1.5 %forward.1 = (bf16[32,16,256]{2,1,0:T(8,128)(2,1)S(1)}, bf16[512,256]{1,0:T(8,128)(2,1)S(1)}, f32[512,256]{1,0:T(8,128)S(1)}, f32[512,256]{1,0:T(8,128)S(1)}) custom-call(bf16[32,32,256]{2,1,0:T(8,128)(2,1)S(1)} %all_to_all.20.in_ref.pack_ref, bf16[256,2048]{1,0:T(8,128)(2,1)S(1)} %copy-done, f32[2,33,256]{2,1,0:T(8,128)S(1)} %copy-done.5, ...), custom_call_target="tpu_custom_call" | custom-call | tf_op jit(solution)/shard_map/forward/pallas_call | solution.py:284
  22.7 12.8 %all_to_all.21.conv_ref = bf16[32,16,256]{2,1,0:T(8,128)(2,1)S(1)} all-to-all(bf16[32,16,256]{2,1,0:T(8,128)(2,1)S(1)} %get-tuple-element.24), channel_id=1, replica_groups=mesh['seq'=32,'chan'=8] {'seq'}, dimensions={0} | all-to-all | bytes 524288 | tf_op jit(solution)/shard_map/all_to_all | solution.py:336
  35.4 0.2 sums.1
  35.6 0.1 collective-permute-start
  35.7 1.1 %collective-permute-done = f32[2,256]{1,0:T(2,128)S(1)} collective-permute-done((f32[2,256]{1,0:T(2,128)S(1)}, f32[2,256]{1,0:T(2,128)S(1)}, u32[]{:S(2)}, u32[]{:S(2)}) %collective-permute-start) | collective-permute-done | bytes 2080 | tf_op jit(solution)/shard_map/ppermute | solution.py:297
  36.9 3.3 %collective-permute-start.1 = (f32[2,256]{1,0:T(2,128)S(1)}, f32[2,256]{1,0:T(2,128)S(1)}, u32[]{:S(2)}, u32[]{:S(2)}) collective-permute-start(f32[2,256]{1,0:T(2,128)S(1)} %add.9), channel_id=1, source_target_pairs={{0,2},{1,3},{2,0},{3,1},{4,6},{5,7},{6,4},{7,5},{8,10},{9,11},{10,... | collective-permute-start | bytes 6152 | tf_op jit(solution)/shard_map/ppermute | solution.py:298
  40.1 1.6 %collective-permute-done.1 = f32[2,256]{1,0:T(2,128)S(1)} collective-permute-done((f32[2,256]{1,0:T(2,128)S(1)}, f32[2,256]{1,0:T(2,128)S(1)}, u32[]{:S(2)}, u32[]{:S(2)}) %collective-permute-start.1) | collective-permute-done | bytes 2080 | tf_op jit(solution)/shard_map/ppermute | solution.py:298
  41.7 5.1 %collective-permute-start.2 = (f32[2,256]{1,0:T(2,128)S(1)}, f32[2,256]{1,0:T(2,128)S(1)}, u32[]{:S(2)}, u32[]{:S(2)}) collective-permute-start(f32[2,256]{1,0:T(2,128)S(1)} %add.10.after_ref), channel_id=1, source_target_pairs={{0,6},{1,7},{2,4},{3,5},{4,2},{5,3},{6,0},{7,1},{8,14},{9,15},{10,... | collective-permute-start | bytes 6152 | tf_op jit(solution)/shard_map/ppermute | solution.py:303
  46.8 1.5 %between.1 = (f32[4,528,256]{2,1,0:T(8,128)S(1)}, f32[512,256]{1,0:T(8,128)S(1)}, f32[512,256]{1,0:T(8,128)S(1)}, f32[5,256,512]{2,1,0:T(8,128)S(1)}) custom-call(bf16[32,32,256]{2,1,0:T(8,128)(2,1)S(1)} %all_to_all.20.in_ref.pack_ref, bf16[256,2048]{1,0:T(8,128)(2,1)S(1)} %copy-done, f32[2,33,256]{2,1,0:T(8,128)S(1)} %copy-done.5, ...), custom_call_target="tpu_custom_call" | custom-call | tf_op jit(solution)/shard_map/between/pallas_call | solution.py:284
  48.3 0.0 collective-permute-done.2
  48.3 0.1 grad.1
  48.4 12.9 %all_to_all.22.in_ref = bf16[32,16,256]{2,1,0:T(8,128)(2,1)S(1)} all-to-all(bf16[32,16,256]{2,1,0:T(8,128)(2,1)S(1)} %grad.1), channel_id=1, replica_groups=mesh['seq'=32,'chan'=8] {'seq'}, dimensions={0} | all-to-all | bytes 524288 | tf_op jit(solution)/shard_map/all_to_all | solution.py:358
  61.3 1.5 %backward.1 = (bf16[32,72,128]{2,1,0:T(8,128)(2,1)S(1)}, bf16[256,512]{1,0:T(8,128)(2,1)S(1)}, bf16[256,512]{1,0:T(8,128)(2,1)S(1)}, bf16[256,512]{1,0:T(8,128)(2,1)S(1)}) custom-call(bf16[32,16,256]{2,1,0:T(8,128)(2,1)S(1)} %all_to_all.22.in_ref, bf16[32,32,256]{2,1,0:T(8,128)(2,1)S(1)} %all_to_all.20.in_ref.pack_ref, ...), custom_call_target="tpu_custom_call" | custom-call | tf_op jit(solution)/shard_map/backward/pallas_call | solution.py:284
  62.8 14.7 %all_to_all.23.in_ref = bf16[32,72,128]{2,1,0:T(8,128)(2,1)S(1)} all-to-all(bf16[32,72,128]{2,1,0:T(8,128)(2,1)S(1)} %get-tuple-element.32), channel_id=1, replica_groups=mesh['seq'=32,'chan'=8] {'seq'}, dimensions={0} | all-to-all | bytes 1179648 | tf_op jit(solution)/shard_map/all_to_all | solution.py:371
  77.5 1.2 %last.1 = (bf16[256,512]{1,0:T(8,128)(2,1)}, bf16[256,512]{1,0:T(8,128)(2,1)}, bf16[256,512]{1,0:T(8,128)(2,1)}, f32[1,512]{1,0:T(1,128)}, bf16[256,512]{1,0:T(8,128)(2,1)}, /*index=5*/bf16[256,512]{1,0:T(8,128)(2,1)}) custom-call(bf16[32,72,128]{2,1,0:T(8,128)(2,1)S(1)} %all_to_all.23.in_ref, bf16[256,512]{1,0:T(8,128)(2,1)S(1)} %get-tuple-element.33.grad_ref, ...), custom_call_target="tpu_custom_call" | custom-call | tf_op jit(solution)/shard_map/last/pallas_call | solution.py:284
  (4 shorter events, 0.0 us)
Async XLA Ops:
  0.6 20.5 %copy-start.5 = (f32[2,33,256]{2,1,0:T(8,128)S(1)}, f32[2,33,256]{2,1,0:T(8,128)}, u32[]{:S(2)}) copy-start(f32[2,33,256]{2,1,0:T(8,128)} %constant.5.clone.turn_ref) | copy-start | bytes 202756
  0.6 1.0 %copy-start.1 = (bf16[256,512]{1,0:T(8,128)(2,1)S(1)}, bf16[256,512]{1,0:T(8,128)(2,1)}, u32[]{:S(2)}) copy-start(bf16[256,512]{1,0:T(8,128)(2,1)} %key_ref.5) | copy-start | bytes 786436
  0.7 1.1 %copy-start.2 = (bf16[256,512]{1,0:T(8,128)(2,1)S(1)}, bf16[256,512]{1,0:T(8,128)(2,1)}, u32[]{:S(2)}) copy-start(bf16[256,512]{1,0:T(8,128)(2,1)} %value_ref.5) | copy-start | bytes 786436
  0.7 1.1 %copy-start.6 = (bf16[256,512]{1,0:T(8,128)(2,1)S(1)}, bf16[256,512]{1,0:T(8,128)(2,1)}, u32[]{:S(2)}) copy-start(bf16[256,512]{1,0:T(8,128)(2,1)} %taps_ref.1) | copy-start | bytes 786436
  0.7 20.5 %copy-start.7 = (f32[512]{0:T(512)S(1)}, f32[512]{0:T(512)}, u32[]{:S(2)}) copy-start(f32[512]{0:T(512)} %param.13) | copy-start | bytes 6148
  0.7 20.5 %copy-start.8 = (f32[512]{0:T(512)S(1)}, f32[512]{0:T(512)}, u32[]{:S(2)}) copy-start(f32[512]{0:T(512)} %param.14) | copy-start | bytes 6148
  0.7 20.5 %copy-start.4 = (bf16[256,512]{1,0:T(8,128)(2,1)S(1)}, bf16[256,512]{1,0:T(8,128)(2,1)}, u32[]{:S(2)}) copy-start(bf16[256,512]{1,0:T(8,128)(2,1)} %cot_in.1) | copy-start | bytes 786436
  0.7 20.5 %copy-start.3 = (bf16[256,512]{1,0:T(8,128)(2,1)S(1)}, bf16[256,512]{1,0:T(8,128)(2,1)}, u32[]{:S(2)}) copy-start(bf16[256,512]{1,0:T(8,128)(2,1)} %gate_in.1) | copy-start | bytes 786436
  1.8 19.4 %copy-start = (bf16[256,2048]{1,0:T(8,128)(2,1)S(1)}, bf16[256,2048]{1,0:T(8,128)(2,1)}, u32[]{:S(2)}) copy-start(bf16[256,2048]{1,0:T(8,128)(2,1)} %constant.4.clone.steps_ref) | copy-start | bytes 3145732
  35.6 1.2 %collective-permute-start = (f32[2,256]{1,0:T(2,128)S(1)}, f32[2,256]{1,0:T(2,128)S(1)}, u32[]{:S(2)}, u32[]{:S(2)}) collective-permute-start(f32[2,256]{1,0:T(2,128)S(1)} %sums.1), channel_id=1, source_target_pairs={{0,1},{1,0},{2,3},{3,2},{4,5},{5,4},{6,7},{7,6},{8,9},{9,8},{10,11... | collective-permute-start | bytes 6152 | tf_op jit(solution)/shard_map/ppermute | solution.py:297
  36.9 4.8 %collective-permute-start.1 = (f32[2,256]{1,0:T(2,128)S(1)}, f32[2,256]{1,0:T(2,128)S(1)}, u32[]{:S(2)}, u32[]{:S(2)}) collective-permute-start(f32[2,256]{1,0:T(2,128)S(1)} %add.9), channel_id=1, source_target_pairs={{0,2},{1,3},{2,0},{3,1},{4,6},{5,7},{6,4},{7,5},{8,10},{9,11},{10,... | collective-permute-start | bytes 6152 | tf_op jit(solution)/shard_map/ppermute | solution.py:298
  41.7 6.6 %collective-permute-start.2 = (f32[2,256]{1,0:T(2,128)S(1)}, f32[2,256]{1,0:T(2,128)S(1)}, u32[]{:S(2)}, u32[]{:S(2)}) collective-permute-start(f32[2,256]{1,0:T(2,128)S(1)} %add.10.after_ref), channel_id=1, source_target_pairs={{0,6},{1,7},{2,4},{3,5},{4,2},{5,3},{6,0},{7,1},{8,14},{9,15},{10,... | collective-permute-start | bytes 6152 | tf_op jit(solution)/shard_map/ppermute | solution.py:303

commit v12 on v10

--- a/solution.py
+++ b/solution.py
@@ -292,14 +292,14 @@
     )(*operands)
 
 
-def add_over_pairs(sums):
+def add_over_mirror(sums):
     sums = sums + lax.ppermute(sums, "chan", [(at, at ^ 1) for at in range(GROUP)])
-    return sums + lax.ppermute(sums, "chan", [(at, at ^ 2) for at in range(GROUP)])
-
-
-def add_over_mirror(sums):
     mirror = [(at, (CHIPS - 1 - at // 2) * 2 + at % 2) for at in range(GROUP)]
     return sums + lax.ppermute(sums, "chan", mirror)
+
+
+def add_over_pairs(sums):
+    return sums + lax.ppermute(sums, "chan", [(at, at ^ 2) for at in range(GROUP)])
 
 
 def on_device(gate_feat, key_feat, value_feat, filter_taps, skip_bias, norm_gain, cotangent):
@@ -335,7 +335,7 @@
     conv = lax.all_to_all(conv, "seq", 0, 0, tiled=True)
     sides = (conv, gate_t, scaled_t, skipped_t)
     (sums,) = call(sums_kernel, "sums", [((2, BLOCK), f32)], *sides)
-    sums = add_over_pairs(sums)
+    sums = add_over_mirror(sums)
     spec, full, push, hold = call(
         between_kernel,
         "between",
@@ -349,7 +349,7 @@
         *sides,
         sums,
     )
-    sums = add_over_mirror(sums)
+    sums = add_over_pairs(sums)
     (grad,) = call(grad_kernel, "grad", [pieces], sums, push, hold)
     grad_arrived = lax.all_to_all(grad, "seq", 0, 0, tiled=True)
     result, grad_conv, normed, gate = call(

time: 79.7 us -> 79.7 us (level)
  starting transfers between devices: 8.41 us -> 7.49 us
  waiting for transfers between devices: 3 us -> 3.91 us
    ppermute x1, waiting for transfers between devices: 0.29 us -> 1.56 us  [add_over_mirror(): return sums + lax.ppermute(sums, 'chan', mirror)]
    ppermute x1, starting transfers between devices: 3.27 us -> 2 us  [add_over_pairs(): lax.ppermute(sums, 'chan', [(at, at ^ 2) for at in range(GROUP)])]
where the time goes in v12:
time: 79.7 us; the launch traced here: 78.7 us
  blocking collectives  59.4 us (75%)
  starting transfers between devices  7.49 us (9%)
  Pallas kernels  5.97 us (7%)
  waiting for transfers between devices  3.91 us (5%)
  local copies, waits for them, and re-layouts  1.11 us (1%)
    all_to_all x1, blocking collectives, on_device(): arrived = lax.all_to_all(packed, 'seq', 0, 0, tiled=True)  19.2 us
    all_to_all x1, blocking collectives, on_device(): result = lax.all_to_all(result, 'seq', 0, 0, tiled=True)  14.6 us
    all_to_all x1, blocking collectives, on_device(): grad_arrived = lax.all_to_all(grad, 'seq', 0, 0, tiled=True)  12.9 us
    all_to_all x1, blocking collectives, on_device(): conv = lax.all_to_all(conv, 'seq', 0, 0, tiled=True)  12.8 us
    pallas_call x8, Pallas kernels, call(): pl.pallas_call(kernel, name=name, out_shape=[jax.ShapeDtypeStruct(shape,...  5.97 us
    ppermute x1, starting transfers between devices, add_over_mirror(): return sums + lax.ppermute(sums, 'chan', mirror)  5.4 us
    ppermute x1, starting transfers between devices, add_over_pairs(): lax.ppermute(sums, 'chan', [(at, at ^ 2) for at in range(GROUP)])  2 us
  transfers between devices with their start and end apart: 3, of which 3 were waited for; matrix products, arithmetic and copies ran while one was open for 0% of the time, Pallas kernels for 2%

profile of v12, /device:TPU:0, one launch (start us, length us, event | category | flops | bytes accessed | tf_op | source)
XLA Modules:
  0.0 78.7 jit_solution(12564927915048761308)
XLA Ops:
  0.6 0.0 copy-start.1
  0.6 0.0 copy-start.2
  0.7 0.0 copy-start.6
  0.7 0.9 %copy-done.1 = bf16[256,512]{1,0:T(8,128)(2,1)S(1)} copy-done((bf16[256,512]{1,0:T(8,128)(2,1)S(1)}, bf16[256,512]{1,0:T(8,128)(2,1)}, u32[]{:S(2)}) %copy-start.1) | copy-done | bytes 262168
  1.6 0.1 copy-done.2
  1.7 0.1 copy-done.6
  1.7 0.0 copy-start
  1.7 0.0 copy-start.3
  1.7 0.0 copy-start.4
  1.8 0.0 copy-start.5
  1.8 0.0 copy-start.7
  1.8 0.0 copy-start.8
  1.8 0.2 pack.1.pack_ref
  2.0 19.2 %all_to_all.20.in_ref.pack_ref = bf16[32,32,256]{2,1,0:T(8,128)(2,1)S(1)} all-to-all(bf16[32,32,256]{2,1,0:T(8,128)(2,1)S(1)} %pack.1.pack_ref), channel_id=1, replica_groups=mesh['seq'=32,'chan'=8] {'seq'}, dimensions={0} | all-to-all | bytes 1048576 | tf_op jit(solution)/shard_map/all_to_all | solution.py:321
  21.1 0.0 copy-done
  21.1 0.0 copy-done.3
  21.1 0.0 copy-done.4
  21.1 0.0 copy-done.5
  21.2 0.0 copy-done.7
  21.2 0.0 copy-done.8
  21.2 1.5 %forward.1 = (bf16[32,16,256]{2,1,0:T(8,128)(2,1)S(1)}, bf16[512,256]{1,0:T(8,128)(2,1)S(1)}, f32[512,256]{1,0:T(8,128)S(1)}, f32[512,256]{1,0:T(8,128)S(1)}) custom-call(bf16[32,32,256]{2,1,0:T(8,128)(2,1)S(1)} %all_to_all.20.in_ref.pack_ref, bf16[256,2048]{1,0:T(8,128)(2,1)S(1)} %copy-done, f32[2,33,256]{2,1,0:T(8,128)S(1)} %copy-done.5, ...), custom_call_target="tpu_custom_call" | custom-call | tf_op jit(solution)/shard_map/forward/pallas_call | solution.py:283
  22.7 12.8 %all_to_all.21.conv_ref = bf16[32,16,256]{2,1,0:T(8,128)(2,1)S(1)} all-to-all(bf16[32,16,256]{2,1,0:T(8,128)(2,1)S(1)} %get-tuple-element.24), channel_id=1, replica_groups=mesh['seq'=32,'chan'=8] {'seq'}, dimensions={0} | all-to-all | bytes 524288 | tf_op jit(solution)/shard_map/all_to_all | solution.py:335
  35.4 0.2 sums.1
  35.6 0.1 collective-permute-start
  35.7 1.1 %collective-permute-done = f32[2,256]{1,0:T(2,128)S(1)} collective-permute-done((f32[2,256]{1,0:T(2,128)S(1)}, f32[2,256]{1,0:T(2,128)S(1)}, u32[]{:S(2)}, u32[]{:S(2)}) %collective-permute-start) | collective-permute-done | bytes 2080 | tf_op jit(solution)/shard_map/ppermute | solution.py:296
  36.8 5.4 %collective-permute-start.1 = (f32[2,256]{1,0:T(2,128)S(1)}, f32[2,256]{1,0:T(2,128)S(1)}, u32[]{:S(2)}, u32[]{:S(2)}) collective-permute-start(f32[2,256]{1,0:T(2,128)S(1)} %add.9), channel_id=1, source_target_pairs={{0,6},{1,7},{2,4},{3,5},{4,2},{5,3},{6,0},{7,1},{8,14},{9,15},{10,... | collective-permute-start | bytes 6152 | tf_op jit(solution)/shard_map/ppermute | solution.py:298
  42.3 1.6 %collective-permute-done.1 = f32[2,256]{1,0:T(2,128)S(1)} collective-permute-done((f32[2,256]{1,0:T(2,128)S(1)}, f32[2,256]{1,0:T(2,128)S(1)}, u32[]{:S(2)}, u32[]{:S(2)}) %collective-permute-start.1) | collective-permute-done | bytes 2080 | tf_op jit(solution)/shard_map/ppermute | solution.py:298
  43.8 2.0 %collective-permute-start.2 = (f32[2,256]{1,0:T(2,128)S(1)}, f32[2,256]{1,0:T(2,128)S(1)}, u32[]{:S(2)}, u32[]{:S(2)}) collective-permute-start(f32[2,256]{1,0:T(2,128)S(1)} %add.10.after_ref), channel_id=1, source_target_pairs={{0,2},{1,3},{2,0},{3,1},{4,6},{5,7},{6,4},{7,5},{8,10},{9,11},{10,... | collective-permute-start | bytes 6152 | tf_op jit(solution)/shard_map/ppermute | solution.py:302
  45.8 1.3 %between.1 = (f32[4,528,256]{2,1,0:T(8,128)S(1)}, f32[256,512]{1,0:T(8,128)S(1)}, f32[512,256]{1,0:T(8,128)S(1)}, f32[512,256]{1,0:T(8,128)S(1)}) custom-call(bf16[32,32,256]{2,1,0:T(8,128)(2,1)S(1)} %all_to_all.20.in_ref.pack_ref, bf16[256,2048]{1,0:T(8,128)(2,1)S(1)} %copy-done, f32[2,33,256]{2,1,0:T(8,128)S(1)} %copy-done.5, ...), custom_call_target="tpu_custom_call" | custom-call | tf_op jit(solution)/shard_map/between/pallas_call | solution.py:283
  47.1 1.2 %collective-permute-done.2 = f32[2,256]{1,0:T(2,128)S(1)} collective-permute-done((f32[2,256]{1,0:T(2,128)S(1)}, f32[2,256]{1,0:T(2,128)S(1)}, u32[]{:S(2)}, u32[]{:S(2)}) %collective-permute-start.2) | collective-permute-done | bytes 2080 | tf_op jit(solution)/shard_map/ppermute | solution.py:302
  48.3 0.1 grad.1
  48.4 12.9 %all_to_all.22.in_ref = bf16[32,16,256]{2,1,0:T(8,128)(2,1)S(1)} all-to-all(bf16[32,16,256]{2,1,0:T(8,128)(2,1)S(1)} %grad.1), channel_id=1, replica_groups=mesh['seq'=32,'chan'=8] {'seq'}, dimensions={0} | all-to-all | bytes 524288 | tf_op jit(solution)/shard_map/all_to_all | solution.py:354
  61.3 1.5 %backward.1 = (bf16[32,72,128]{2,1,0:T(8,128)(2,1)S(1)}, bf16[256,512]{1,0:T(8,128)(2,1)S(1)}, bf16[256,512]{1,0:T(8,128)(2,1)S(1)}, bf16[256,512]{1,0:T(8,128)(2,1)S(1)}) custom-call(bf16[32,16,256]{2,1,0:T(8,128)(2,1)S(1)} %all_to_all.22.in_ref, bf16[32,32,256]{2,1,0:T(8,128)(2,1)S(1)} %all_to_all.20.in_ref.pack_ref, ...), custom_call_target="tpu_custom_call" | custom-call | tf_op jit(solution)/shard_map/backward/pallas_call | solution.py:283
  62.8 14.6 %all_to_all.23.in_ref = bf16[32,72,128]{2,1,0:T(8,128)(2,1)S(1)} all-to-all(bf16[32,72,128]{2,1,0:T(8,128)(2,1)S(1)} %get-tuple-element.32), channel_id=1, replica_groups=mesh['seq'=32,'chan'=8] {'seq'}, dimensions={0} | all-to-all | bytes 1179648 | tf_op jit(solution)/shard_map/all_to_all | solution.py:370
  77.5 1.2 %last.1 = (bf16[256,512]{1,0:T(8,128)(2,1)}, bf16[256,512]{1,0:T(8,128)(2,1)}, bf16[256,512]{1,0:T(8,128)(2,1)}, f32[1,512]{1,0:T(1,128)}, bf16[256,512]{1,0:T(8,128)(2,1)}, /*index=5*/bf16[256,512]{1,0:T(8,128)(2,1)}) custom-call(bf16[32,72,128]{2,1,0:T(8,128)(2,1)S(1)} %all_to_all.23.in_ref, bf16[256,512]{1,0:T(8,128)(2,1)S(1)} %get-tuple-element.33.grad_ref, ...), custom_call_target="tpu_custom_call" | custom-call | tf_op jit(solution)/shard_map/last/pallas_call | solution.py:283
  (4 shorter events, 0.0 us)
Async XLA Ops:
  0.6 1.0 %copy-start.1 = (bf16[256,512]{1,0:T(8,128)(2,1)S(1)}, bf16[256,512]{1,0:T(8,128)(2,1)}, u32[]{:S(2)}) copy-start(bf16[256,512]{1,0:T(8,128)(2,1)} %key_ref.5) | copy-start | bytes 786436
  0.6 1.0 %copy-start.2 = (bf16[256,512]{1,0:T(8,128)(2,1)S(1)}, bf16[256,512]{1,0:T(8,128)(2,1)}, u32[]{:S(2)}) copy-start(bf16[256,512]{1,0:T(8,128)(2,1)} %value_ref.5) | copy-start | bytes 786436
  0.7 1.1 %copy-start.6 = (bf16[256,512]{1,0:T(8,128)(2,1)S(1)}, bf16[256,512]{1,0:T(8,128)(2,1)}, u32[]{:S(2)}) copy-start(bf16[256,512]{1,0:T(8,128)(2,1)} %taps_ref.1) | copy-start | bytes 786436
  1.7 19.4 %copy-start = (bf16[256,2048]{1,0:T(8,128)(2,1)S(1)}, bf16[256,2048]{1,0:T(8,128)(2,1)}, u32[]{:S(2)}) copy-start(bf16[256,2048]{1,0:T(8,128)(2,1)} %constant.4.clone.steps_ref) | copy-start | bytes 3145732
  1.7 19.4 %copy-start.3 = (bf16[256,512]{1,0:T(8,128)(2,1)S(1)}, bf16[256,512]{1,0:T(8,128)(2,1)}, u32[]{:S(2)}) copy-start(bf16[256,512]{1,0:T(8,128)(2,1)} %gate_ref.3) | copy-start | bytes 786436
  1.7 19.4 %copy-start.4 = (bf16[256,512]{1,0:T(8,128)(2,1)S(1)}, bf16[256,512]{1,0:T(8,128)(2,1)}, u32[]{:S(2)}) copy-start(bf16[256,512]{1,0:T(8,128)(2,1)} %cot_ref.3) | copy-start | bytes 786436
  1.8 19.4 %copy-start.5 = (f32[2,33,256]{2,1,0:T(8,128)S(1)}, f32[2,33,256]{2,1,0:T(8,128)}, u32[]{:S(2)}) copy-start(f32[2,33,256]{2,1,0:T(8,128)} %constant.5.clone.turn_ref) | copy-start | bytes 202756
  1.8 19.4 %copy-start.7 = (f32[512]{0:T(512)S(1)}, f32[512]{0:T(512)}, u32[]{:S(2)}) copy-start(f32[512]{0:T(512)} %param.13) | copy-start | bytes 6148
  1.8 19.4 %copy-start.8 = (f32[512]{0:T(512)S(1)}, f32[512]{0:T(512)}, u32[]{:S(2)}) copy-start(f32[512]{0:T(512)} %param.14) | copy-start | bytes 6148
  35.6 1.2 %collective-permute-start = (f32[2,256]{1,0:T(2,128)S(1)}, f32[2,256]{1,0:T(2,128)S(1)}, u32[]{:S(2)}, u32[]{:S(2)}) collective-permute-start(f32[2,256]{1,0:T(2,128)S(1)} %sums.1), channel_id=1, source_target_pairs={{0,1},{1,0},{2,3},{3,2},{4,5},{5,4},{6,7},{7,6},{8,9},{9,8},{10,11... | collective-permute-start | bytes 6152 | tf_op jit(solution)/shard_map/ppermute | solution.py:296
  36.8 7.0 %collective-permute-start.1 = (f32[2,256]{1,0:T(2,128)S(1)}, f32[2,256]{1,0:T(2,128)S(1)}, u32[]{:S(2)}, u32[]{:S(2)}) collective-permute-start(f32[2,256]{1,0:T(2,128)S(1)} %add.9), channel_id=1, source_target_pairs={{0,6},{1,7},{2,4},{3,5},{4,2},{5,3},{6,0},{7,1},{8,14},{9,15},{10,... | collective-permute-start | bytes 6152 | tf_op jit(solution)/shard_map/ppermute | solution.py:298
  43.8 4.5 %collective-permute-start.2 = (f32[2,256]{1,0:T(2,128)S(1)}, f32[2,256]{1,0:T(2,128)S(1)}, u32[]{:S(2)}, u32[]{:S(2)}) collective-permute-start(f32[2,256]{1,0:T(2,128)S(1)} %add.10.after_ref), channel_id=1, source_target_pairs={{0,2},{1,3},{2,0},{3,1},{4,6},{5,7},{6,4},{7,5},{8,10},{9,11},{10,... | collective-permute-start | bytes 6152 | tf_op jit(solution)/shard_map/ppermute | solution.py:302
